TPU v7x, 128 devices: a whole 4x4x4 slice. The times are simulated.
128 devices in a mesh: row: 16 (over y, x), col: 8 (over z, core).
Axes of the slice: x: 4, y: 4, z: 4, core: 2. Of those that a mesh axis runs over, the one named last changes fastest.
Arguments:
- features: bfloat16 [512, 384, 1024], P('row', 'col'), may hold values from -6 to 6
- conv_weight: bfloat16 [9216, 256], P(('row', 'col')), may hold values from -0.0625 to 0.0625
- conv_bias: float32 [256], replicated, may hold values from -3 to 3
- proj_weight: bfloat16 [256, 256], P(('row', 'col')), may hold values from -0.375 to 0.375
- cotangent: bfloat16 [512, 384, 256], P('row', 'col'), may hold values from -6 to 6
Outputs:
- projected: bfloat16 [512, 384, 256], P('row', 'col')
- features_grad: bfloat16 [512, 384, 1024], P('row', 'col')
- conv_weight_grad: float32 [9216, 256], P(('row', 'col'))
- proj_weight_grad: float32 [256, 256], P(('row', 'col'))
- bias_grad: float32 [256], P(('row', 'col'))
All inputs are finite; a program needn't handle non-finite values.
Results may differ from a plain program's by a relative error of at most 0.015.
Values may be sent and summed in bfloat16 or wider, within the bound.
No kernel may reach another device: no remote copies, remote signals or barrier semaphores. Data moves between devices by JAX's collectives and lax.ppermute only.
A program may use at most 192 MiB of HBM per device.

v0:
```python
import jax
import jax.numpy as jnp
from jax import lax
from jax.sharding import PartitionSpec as P

DILATION_RATE = 16


def padded(x, sides, width):
    for axis, dim in sides:
        size, length = (lax.axis_size(axis), x.shape[dim])
        up = [(i, (i + 1) % size) for i in range(size - 1)]
        down = [(j, i) for i, j in up]
        last = lax.slice_in_dim(x, length - width, length, axis=dim)
        first = lax.slice_in_dim(x, 0, width, axis=dim)
        before = lax.ppermute(last, axis, up)
        after = lax.ppermute(first, axis, down)
        x = jnp.concatenate([before, x, after], axis=dim)
    return x


def window(padded_input, left_operand, right_operand, row_count, column_count):
    return padded_input[
        left_operand * DILATION_RATE : left_operand * DILATION_RATE + row_count,
        right_operand * DILATION_RATE : right_operand * DILATION_RATE + column_count,
    ]


def body(features, conv_weight, conv_bias, proj_weight, cotangent):
    row_count, column_count, in_channels = features.shape
    out_channels = conv_bias.shape[0]
    pixels = row_count * column_count
    padded_input = padded(features, (("row", 0), ("col", 1)), DILATION_RATE)
    conv_full, proj_full = (
        lax.all_gather(conv_weight, ("row", "col"), axis=0, tiled=True),
        lax.all_gather(proj_weight, ("row", "col"), axis=0, tiled=True),
    )
    pre = jnp.zeros((pixels, out_channels), jnp.float32)
    for left_operand in range(3):
        for right_operand in range(3):
            tap = 3 * left_operand + right_operand
            piece = window(
                padded_input, left_operand, right_operand, row_count, column_count
            ).reshape(pixels, in_channels)
            pre = pre + jnp.dot(
                piece,
                conv_full[tap * in_channels : (tap + 1) * in_channels],
                preferred_element_type=jnp.float32,
            )
    pre = pre + conv_bias[None, :]
    sig = jax.nn.sigmoid(pre)
    hidden = (pre * sig).astype(jnp.bfloat16)
    projected = jnp.dot(hidden, proj_full, preferred_element_type=jnp.float32).astype(jnp.bfloat16)
    grad_flat = cotangent.reshape(pixels, out_channels)
    hidden_grad = lax.dot_general(
        grad_flat, proj_full, (((1,), (1,)), ((), ())), preferred_element_type=jnp.float32
    )
    preactivation_gradient = (hidden_grad * sig * (1.0 + pre * (1.0 - sig))).astype(jnp.bfloat16)
    proj_term = lax.dot_general(
        hidden, grad_flat, (((0,), (0,)), ((), ())), preferred_element_type=jnp.float32
    )
    bias_term = jnp.sum(preactivation_gradient.astype(jnp.float32), axis=0)
    proj_weight_grad, bias_grad = (
        lax.psum_scatter(proj_term, ("row", "col"), scatter_dimension=0, tiled=True),
        lax.psum_scatter(bias_term, ("row", "col"), scatter_dimension=0, tiled=True),
    )
    padded_gradient = padded(
        preactivation_gradient.reshape(row_count, column_count, out_channels),
        (("row", 0), ("col", 1)),
        DILATION_RATE,
    )
    features_grad = jnp.zeros((pixels, in_channels), jnp.float32)
    blocks = []
    for left_operand in range(3):
        for right_operand in range(3):
            tap = 3 * left_operand + right_operand
            piece = window(
                padded_input, left_operand, right_operand, row_count, column_count
            ).reshape(pixels, in_channels)
            blocks.append(
                lax.dot_general(
                    piece,
                    preactivation_gradient,
                    (((0,), (0,)), ((), ())),
                    preferred_element_type=jnp.float32,
                )
            )
            back = window(
                padded_gradient, 2 - left_operand, 2 - right_operand, row_count, column_count
            ).reshape(pixels, out_channels)
            features_grad = features_grad + lax.dot_general(
                back,
                conv_full[tap * in_channels : (tap + 1) * in_channels],
                (((1,), (1,)), ((), ())),
                preferred_element_type=jnp.float32,
            )
    weight_term = jnp.concatenate(blocks, axis=0)
    conv_weight_grad = lax.psum_scatter(
        weight_term, ("row", "col"), scatter_dimension=0, tiled=True
    )
    return (
        projected.reshape(row_count, column_count, out_channels),
        features_grad.astype(jnp.bfloat16).reshape(row_count, column_count, in_channels),
        conv_weight_grad,
        proj_weight_grad,
        bias_grad,
    )


def solution(mesh):
    placed = (
        P("row", "col", None),
        P(("row", "col"), None),
        P(),
        P(("row", "col"), None),
        P("row", "col", None),
    )
    return jax.shard_map(
        body,
        mesh=mesh,
        in_specs=placed,
        out_specs=(
            P("row", "col", None),
            P("row", "col", None),
            P(("row", "col"), None),
            P(("row", "col"), None),
            P(("row", "col")),
        ),
        check_vma=False,
    )
```

profile of v0, /device:TPU:1, one launch (start us, length us, event | category | flops | bytes accessed | tf_op | source)
XLA Modules:
  0.0 539.0 jit_solution(4898019133952266723)
XLA Ops:
  8.0 2.3 fusion.51
  10.2 4.3 collective-permute-start
  14.6 1.3 collective-permute-start.1
  15.9 32.6 %collective-permute-done = bf16[16,48,1024]{2,1,0:T(8,128)(2,1)S(1)} collective-permute-done((bf16[16,48,1024]{2,1,0:T(8,128)(2,1)S(1)}, bf16[16,48,1024]{2,1,0:T(8,128)(2,1)S(1)}, u32[]{:S(2)}, u32[]{:S(2)}) %collective-permute-start) | collective-permute-done | bytes 1572896 | tf_op jit(solution)/shard_map/ppermute | solution.py:16
  48.6 4.1 collective-permute-done.1
  52.7 3.2 pad_maximum_fusion.3
  56.1 2.8 fusion.50
  58.9 1.0 copy-done.2
  60.0 5.6 %collective-permute-start.2 = (bf16[64,16,1024]{2,1,0:T(8,128)(2,1)}, bf16[64,16,1024]{2,1,0:T(8,128)(2,1)S(1)}, u32[]{:S(2)}, u32[]{:S(2)}) collective-permute-start(bf16[64,16,1024]{2,1,0:T(8,128)(2,1)} %get-tuple-element.14), channel_id=1, source_target_pairs={{0,1},{1,2},{2,3},{3,4},{4,5},{5,6},{6,7},{8,9},{9,10},{10,11},{11... | collective-permute-start | bytes 6291464 | tf_op jit(solution)/shard_map/ppermute | solution.py:16
  65.6 1.9 collective-permute-start.3
  67.5 58.4 %all-gather = bf16[128,2,256]{2,1,0:T(2,128)(2,1)S(1)} all-gather(bf16[1,2,256]{2,1,0:T(2,128)(2,1)S(1)} %bitcast.107), channel_id=1, replica_groups=mesh['row'=16,'col'=8] {'row','col'}, dimensions={0}, use_global_device_ids=true | all-gather | bytes 132096 | tf_op jit(solution)/shard_map/all_gather | solution.py:36
  126.0 11.5 %fusion = (bf16[32,48,1024]{2,1,0:T(8,128)(2,1)}, bf16[32,48,1024]{2,1,0:T(8,128)(2,1)}, bf16[32,48,1024]{2,1,0:T(8,128)(2,1)}, bf16[32,48,1024]{2,1,0:T(8,128)(...) fusion(bf16[64,48,1024]{2,1,0:T(8,128)(2,1)} %copy-done.2, ...), kind=kLoop, calls=%fused_computation.9 | loop fusion | flops 37748736 | bytes 29360128 | tf_op jit(solution)/shard_map/concatenate | solution.py:18
  137.6 3.1 fusion.37
  141.0 3.0 fusion.41
  147.9 1.0 fusion.16
  149.7 1.0 fusion.26
  151.6 1.0 fusion.22
  153.5 1.0 fusion.11
  155.4 1.5 multiply_convert_fusion
  157.8 2.0 convolution_dynamic-update-slice_fusion.7
  159.8 2.0 convolution_dynamic-update-slice_fusion.6
  161.7 2.0 convolution_dynamic-update-slice_fusion.5
  163.7 2.2 convolution_dynamic-update-slice_fusion.4
  166.0 2.4 fusion.13
  168.4 2.0 convolution_dynamic-update-slice_fusion.3
  170.4 2.0 convolution_dynamic-update-slice_fusion.2
  172.4 2.1 convolution_dynamic-update-slice_fusion.1
  174.5 1.1 fusion.55
  175.7 3.9 convolution_dynamic-update-slice_fusion
  179.7 1.3 collective-permute-start.4
  181.0 1.3 collective-permute-start.5
  182.3 4.7 fusion.31
  187.0 67.1 %all-reduce.1 = f32[256]{0:T(256)S(1)} all-reduce(f32[256]{0:T(256)S(1)} %get-tuple-element.37), channel_id=4, replica_groups=mesh['row'=16,'col'=8] {'row','col'}, use_global_device_ids=true, to_apply=%region_3.0.clone | all-reduce | flops 256 | bytes 2048
  254.7 1.2 convolution_convert_fusion
  256.0 58.5 %all-reduce.4.cloned.1.call-done = f32[256,256]{1,0:T(8,128)} async-done(((f32[256,256]{1,0:T(8,128)}), f32[256,256]{1,0:T(8,128)}) %all-reduce.4.cloned.1.call-update) | async-done | bytes 262160
  314.5 1.3 constant_dynamic-slice_fusion
  315.8 2.9 collective-permute-start.6
  318.8 2.6 collective-permute-start.7
  321.6 4.8 fusion.43
  326.4 3.7 fusion.20
  330.1 1.2 maximum_maximum_fusion
  331.6 3.6 fusion.28
  335.3 3.6 fusion.35
  338.9 3.7 fusion.39
  342.6 3.6 fusion.47
  346.2 3.7 fusion.24
  349.9 19.3 %add_convert_fusion = bf16[1536,1024]{1,0:T(8,128)(2,1)} fusion(f32[1536,1024]{1,0:T(8,128)} %fusion.20, f32[1536,1024]{1,0:T(8,128)} %fusion.24, f32[1536,1024]{1,0:T(8,128)} %fusion.28, f32[1536,1024]{1,0:T(8,128)} %fusion.31, f32[1536,1024]{1,0:T(8,128)} %fusion.35, f32[1536,1024]{1,0:T(8,128)} %fusion.39, f32[1536,1024]{1,0:T(8,128)} %fusion.47, ...), kind=kOutput, calls=%fused_computation.8 | convolution fusion | flops 819462144 | bytes 54788096 | tf_op jit(solution)/shard_map/dot_general | solution.py:91
  369.2 163.3 %reduce-scatter.2.cloned.1.call-done = f32[72,256]{1,0:T(8,128)} async-done(((f32[9216,256]{1,0:T(8,128)}), f32[72,256]{1,0:T(8,128)}) %reduce-scatter.2.cloned.1.call-update) | async-done | bytes 73744 | tf_op jit(solution)/shard_map/reduce_scatter | solution.py:98
  (60 shorter events, 10.8 us)
Async XLA Ops:
  7.2 149.8 %copy-start = (bf16[32,48,256]{2,1,0:T(8,128)(2,1)S(1)}, bf16[32,48,256]{2,1,0:T(8,128)(2,1)}, u32[]{:S(2)}) copy-start(bf16[32,48,256]{2,1,0:T(8,128)(2,1)} %param.9) | copy-start | bytes 2359300
  7.2 130.4 %all-gather.3.cloned.1.call-start = ((), (), s32[]{:S(2)}) async-start(), calls=%async_computation.1 | async-start | bytes 4755456 | tf_op jit(solution)/shard_map/all_gather | solution.py:35
  7.9 306.6 %all-reduce.4.cloned.1.call-start = ((), (), s32[]{:S(2)}) async-start(), calls=%async_computation.3 | async-start | bytes 524288
  10.2 42.5 %copy-start.4 = (bf16[32,48,1024]{2,1,0:T(8,128)(2,1)S(1)}, bf16[32,48,1024]{2,1,0:T(8,128)(2,1)}, u32[]{:S(2)}) copy-start(bf16[32,48,1024]{2,1,0:T(8,128)(2,1)} %param.5) | copy-start | bytes 9437188
  10.2 38.2 %collective-permute-start = (bf16[16,48,1024]{2,1,0:T(8,128)(2,1)S(1)}, bf16[16,48,1024]{2,1,0:T(8,128)(2,1)S(1)}, u32[]{:S(2)}, u32[]{:S(2)}) collective-permute-start(bf16[16,48,1024]{2,1,0:T(8,128)(2,1)S(1)} %get-tuple-element.20), channel_id=1, source_target_pairs={{0,8},{8,16},{16,24},{24,32},{32,40},{40,48},{48,56},{56,64},{64,7... | collective-permute-start | bytes 4718600 | tf_op jit(solution)/shard_map/ppermute | solution.py:16
  14.6 38.1 %collective-permute-start.1 = (bf16[16,48,1024]{2,1,0:T(8,128)(2,1)S(1)}, bf16[16,48,1024]{2,1,0:T(8,128)(2,1)S(1)}, u32[]{:S(2)}, u32[]{:S(2)}) collective-permute-start(bf16[16,48,1024]{2,1,0:T(8,128)(2,1)S(1)} %get-tuple-element.19), channel_id=1, source_target_pairs={{8,0},{16,8},{24,16},{32,24},{40,32},{48,40},{56,48},{64,56},{72,6... | collective-permute-start | bytes 4718600 | tf_op jit(solution)/shard_map/ppermute | solution.py:17
  56.1 3.9 copy-start.2
  56.1 11.4 %copy-start.14 = (bf16[2,256]{1,0:T(2,128)(2,1)S(1)}, bf16[2,256]{1,0:T(2,128)(2,1)}, u32[]{:S(2)}) copy-start(bf16[2,256]{1,0:T(2,128)(2,1)} %param.8) | copy-start | bytes 3076
  60.0 66.0 %collective-permute-start.2 = (bf16[64,16,1024]{2,1,0:T(8,128)(2,1)}, bf16[64,16,1024]{2,1,0:T(8,128)(2,1)S(1)}, u32[]{:S(2)}, u32[]{:S(2)}) collective-permute-start(bf16[64,16,1024]{2,1,0:T(8,128)(2,1)} %get-tuple-element.14), channel_id=1, source_target_pairs={{0,1},{1,2},{2,3},{3,4},{4,5},{5,6},{6,7},{8,9},{9,10},{10,11},{11... | collective-permute-start | bytes 6291464 | tf_op jit(solution)/shard_map/ppermute | solution.py:16
  65.6 60.4 %collective-permute-start.3 = (bf16[64,16,1024]{2,1,0:T(8,128)(2,1)}, bf16[64,16,1024]{2,1,0:T(8,128)(2,1)}, u32[]{:S(2)}, u32[]{:S(2)}) collective-permute-start(bf16[64,16,1024]{2,1,0:T(8,128)(2,1)} %get-tuple-element.15), channel_id=1, source_target_pairs={{1,0},{2,1},{3,2},{4,3},{5,4},{6,5},{7,6},{9,8},{10,9},{11,10},{12... | collective-permute-start | bytes 6291464 | tf_op jit(solution)/shard_map/ppermute | solution.py:17
  137.6 3.4 copy-start.6
  141.0 3.1 copy-start.13
  144.1 1.9 copy-start.5
  146.0 1.9 copy-start.7
  147.9 1.9 copy-start.8
  149.7 1.9 copy-start.12
  151.6 1.9 copy-start.3
  153.5 1.9 copy-start.9
  153.5 1.9 copy-start.15
  159.8 2.0 copy-start.11
  161.7 2.0 copy-start.10
  175.6 356.9 %reduce-scatter.2.cloned.1.call-start = ((), (), s32[]{:S(2)}) async-start(), calls=%async_computation.2 | async-start | bytes 9510912 | tf_op jit(solution)/shard_map/reduce_scatter | solution.py:98
  179.7 136.1 %collective-permute-start.4 = (bf16[16,48,256]{2,1,0:T(8,128)(2,1)S(1)}, bf16[16,48,256]{2,1,0:T(8,128)(2,1)S(1)}, u32[]{:S(2)}, u32[]{:S(2)}) collective-permute-start(bf16[16,48,256]{2,1,0:T(8,128)(2,1)S(1)} %bitcast.106), channel_id=1, source_target_pairs={{0,8},{8,16},{16,24},{24,32},{32,40},{40,48},{48,56},{56,64},{64,7... | collective-permute-start | bytes 1179656 | tf_op jit(solution)/shard_map/ppermute | solution.py:16
  181.0 134.8 %collective-permute-start.5 = (bf16[16,48,256]{2,1,0:T(8,128)(2,1)S(1)}, bf16[16,48,256]{2,1,0:T(8,128)(2,1)S(1)}, u32[]{:S(2)}, u32[]{:S(2)}) collective-permute-start(bf16[16,48,256]{2,1,0:T(8,128)(2,1)S(1)} %bitcast.105), channel_id=1, source_target_pairs={{8,0},{16,8},{24,16},{32,24},{40,32},{48,40},{56,48},{64,56},{72,6... | collective-permute-start | bytes 1179656 | tf_op jit(solution)/shard_map/ppermute | solution.py:17
  315.8 14.3 %collective-permute-start.6 = (bf16[64,16,256]{2,1,0:T(8,128)(2,1)S(1)}, bf16[64,16,256]{2,1,0:T(8,128)(2,1)S(1)}, u32[]{:S(2)}, u32[]{:S(2)}) collective-permute-start(bf16[64,16,256]{2,1,0:T(8,128)(2,1)S(1)} %get-tuple-element.30), channel_id=1, source_target_pairs={{1,0},{2,1},{3,2},{4,3},{5,4},{6,5},{7,6},{9,8},{10,9},{11,10},{12... | collective-permute-start | bytes 1572872 | tf_op jit(solution)/shard_map/ppermute | solution.py:17
  318.8 11.3 %collective-permute-start.7 = (bf16[64,16,256]{2,1,0:T(8,128)(2,1)S(1)}, bf16[64,16,256]{2,1,0:T(8,128)(2,1)S(1)}, u32[]{:S(2)}, u32[]{:S(2)}) collective-permute-start(bf16[64,16,256]{2,1,0:T(8,128)(2,1)S(1)} %get-tuple-element.29), channel_id=1, source_target_pairs={{0,1},{1,2},{2,3},{3,4},{4,5},{5,6},{6,7},{8,9},{9,10},{10,11},{11... | collective-permute-start | bytes 1572872 | tf_op jit(solution)/shard_map/ppermute | solution.py:16
  321.4 5.0 slice-start
  321.6 4.9 slice-start.1
  349.9 182.6 %copy-start.1 = (bf16[32,48,256]{2,1,0:T(8,128)(2,1)S(1)}, bf16[32,48,256]{2,1,0:T(8,128)(2,1)}, u32[]{:S(2)}) copy-start(bf16[32,48,256]{2,1,0:T(8,128)(2,1)} %param.9) | copy-start | bytes 2359300
Sparse Core Ops, SparseCore 0:
  11.0 72.6 all-gather.2
  175.7 138.6 all-reduce.3
  320.1 212.3 reduce-scatter.1
where the time goes:
time: 541 us; the launch traced here: 539 us
  waiting for transfers between devices  259 us (48%)
  blocking collectives  126 us (23%)
  matrix products  88.3 us (16%)
  starting transfers between devices  21.4 us (4%)
  other arithmetic  16.2 us (3%)
  local copies, waits for them, and re-layouts  14.3 us (3%)
  between operations  14.1 us (3%)
    reduce_scatter x1, waiting for transfers between devices, body(): lax.psum_scatter(weight_term, ('row', 'col'), scatter_dimension=0, tiled=...  163 us
    unnamed x1, blocking collectives  67.1 us
    unnamed x4, waiting for transfers between devices  59.2 us
    all_gather x1, blocking collectives, body(): lax.all_gather(proj_weight, ('row', 'col'), axis=0, tiled=True)  58.4 us
    dot_general x9, matrix products, body(): lax.dot_general(back, conv_full[tap * in_channels:(tap + 1) * in_channels...  50.8 us
    ppermute x4, waiting for transfers between devices, padded(): before = lax.ppermute(last, axis, up)  32.6 us
    dot_general x9, matrix products, body(): lax.dot_general(piece, preactivation_gradient, (((0,), (0,)), ((), ())),...  20.6 us
    concatenate x5, other arithmetic, padded(): x = jnp.concatenate([before, x, after], axis=dim)  16.2 us
  transfers between devices with their start and end apart: 11, of which 4 were waited for; matrix products, arithmetic and copies ran while one was open for 15% of the time, Pallas kernels for 0%

commit v1 on v0

v1 whole, which is shorter than its diff:
```python
import functools

import jax
import jax.numpy as jnp
import numpy as np
from jax import lax
from jax.experimental import pallas as pl
from jax.experimental.pallas import tpu as pltpu
from jax.sharding import Mesh, PartitionSpec as P

D = 16
CHIPS = ("y", "x", "z")
ALL = ("y", "x", "z", "core")
BF = jnp.bfloat16
F32 = jnp.float32
VMEM_LIMIT = 56 * 1024 * 1024

NN = (((1,), (0,)), ((), ()))
NT = (((1,), (1,)), ((), ()))


def dot(a, b, dims=NN):
    return lax.dot_general(a, b, dims, preferred_element_type=F32)


def vmem():
    return pl.BlockSpec(memory_space=pltpu.VMEM)


def hbm():
    return pl.BlockSpec(memory_space=pl.ANY)


def params():
    return pltpu.CompilerParams(vmem_limit_bytes=VMEM_LIMIT)


def cost(flops, size):
    return pl.CostEstimate(flops=flops, bytes_accessed=size, transcendentals=0)


def load_weights(core_ref, mine_ref, other_ref, w_ref, sems):
    core = core_ref[0]
    copies = []
    for k, (ref, half) in enumerate(((mine_ref, core), (other_ref, 1 - core))):
        lanes = pl.ds(pl.multiple_of(half * 128, 128), 128)
        copy = pltpu.make_async_copy(
            ref.at[:, pl.ds(0, 144), :], w_ref.at[:, :, lanes], sems.at[k]
        )
        copy.start()
        copies.append(copy)
    for copy in copies:
        copy.wait()
    return w_ref.reshape(9216, 256)


def tap(w, a, b):
    return w[(3 * a + b) * 1024 : (3 * a + b + 1) * 1024, :]


def px(ref, r0, r1, c0, c1):
    return ref[r0:r1, c0:c1, :].reshape((r1 - r0) * (c1 - c0), ref.shape[2])


def halo_kernel(core_ref, f_ref, mine_ref, other_ref, n_ref, s_ref, l_ref, r_ref, w_ref, acc, sems):
    w = load_weights(core_ref, mine_ref, other_ref, w_ref, sems)
    for out, a, r0, block in ((n_ref, 2, 0, 0), (s_ref, 0, 16, 3)):
        acc[...] = jnp.zeros_like(acc)
        for b in range(3):
            c = (2 - b) * D
            acc[:, c : c + 48, :] += dot(px(f_ref, r0, r0 + 16, 0, 48), tap(w, a, b)).reshape(16, 48, 256)
        l_ref[16 * block : 16 * block + 16] = acc[:, 0:16, :].astype(BF)
        out[...] = acc[:, 16:64, :].astype(BF)
        r_ref[16 * block : 16 * block + 16] = acc[:, 64:80, :].astype(BF)
    for out, b, c0 in ((l_ref, 2, 0), (r_ref, 0, 32)):
        mid = dot(px(f_ref, 0, 32, c0, c0 + 16), tap(w, 1, b))
        top = mid[:256] + dot(px(f_ref, 16, 32, c0, c0 + 16), tap(w, 2, b))
        low = mid[256:] + dot(px(f_ref, 0, 16, c0, c0 + 16), tap(w, 0, b))
        out[16:32] = top.reshape(16, 16, 256).astype(BF)
        out[32:48] = low.reshape(16, 16, 256).astype(BF)


def own_kernel(core_ref, f_ref, mine_ref, other_ref, cot_ref, proj_ref, bias_ref, pre_ref, hg_ref, w_ref, sems):
    w = load_weights(core_ref, mine_ref, other_ref, w_ref, sems)
    pre_ref[...] = (dot(px(f_ref, 0, 32, 0, 48), tap(w, 1, 1)) + bias_ref[...]).reshape(32, 48, 256)
    for a, rows in ((0, ((0, 16), (16, 32))), (1, ((0, 32), (0, 32))), (2, ((16, 32), (0, 16)))):
        for b, cols in ((0, ((0, 32), (16, 48))), (1, ((0, 48), (0, 48))), (2, ((16, 48), (0, 32)))):
            if a == 1 and b == 1:
                continue
            (fr, pr), (fc, pc) = rows, cols
            pre_ref[pr[0] : pr[1], pc[0] : pc[1], :] += dot(px(f_ref, *fr, *fc), tap(w, a, b)).reshape(
                pr[1] - pr[0], pc[1] - pc[0], 256
            )
    hg_ref[...] = dot(px(cot_ref, 0, 32, 0, 48), proj_ref[...], NT).reshape(32, 48, 256)


def point_kernel(core_ref, pre_ref, hg_ref, n_ref, s_ref, inner_ref, outer_ref, cn_ref, cs_ref, hid_ref, g_ref):
    core = core_ref[0]
    pre_ref[0:16] += n_ref[...].astype(F32)
    pre_ref[16:32] += s_ref[...].astype(F32)
    inner = pl.ds(pl.multiple_of(32 - 32 * core, 16), 16)
    outer = pl.ds(pl.multiple_of(32 * core, 16), 16)
    pre_ref[:, inner, :] += inner_ref[...].astype(F32)
    pre_ref[:, outer, :] += outer_ref[...].astype(F32)
    pre_ref[0:16, outer, :] += cn_ref[...].astype(F32)
    pre_ref[16:32, outer, :] += cs_ref[...].astype(F32)

    @pl.loop(0, 32)
    def _(r):
        pre = pre_ref[r]
        s = jax.nn.sigmoid(pre)
        hid_ref[r] = (pre * s).astype(BF)
        g_ref[r] = (hg_ref[r] * s * (1.0 + pre * (1.0 - s))).astype(BF)


def proj_kernel(hid_ref, cot_ref, proj_ref, g_ref, out_ref, pw_ref, bias_ref):
    hidden = px(hid_ref, 0, 32, 0, 48)
    out_ref[...] = dot(hidden, proj_ref[...]).astype(BF).reshape(32, 48, 256)
    pw_ref[...] = dot(hidden.T, px(cot_ref, 0, 32, 0, 48))
    bias_ref[...] = jnp.sum(px(g_ref, 0, 32, 0, 48).astype(F32), axis=0, keepdims=True)


def wgrad_kernel(core_ref, ft_ref, g_ref, mine_ref, other_ref):
    t = pl.program_id(0)
    row, col = (2 - t // 3) * D, (2 - t % 3) * D
    blocks = [
        g_ref[pl.ds(row + 16 * i, 16), pl.ds(pl.multiple_of(col + 16 * j, 16), 16), :].reshape(256, 256)
        for i in range(2)
        for j in range(3)
    ]
    res = dot(ft_ref[...], jnp.concatenate(blocks, axis=0))
    low, high = res[:, :128], res[:, 128:]
    first = core_ref[0] == 0
    mine_ref[...] = jnp.where(first, low, high).astype(BF)
    other_ref[...] = jnp.where(first, high, low).astype(BF)


def fgrad_kernel(core_ref, g_ref, mine_ref, other_ref, out_ref, w_ref, acc, sems):
    w = load_weights(core_ref, mine_ref, other_ref, w_ref, sems)
    acc[...] = jnp.zeros_like(acc)

    @pl.loop(0, 9)
    def _(t):
        row, col = (2 - t // 3) * D, (2 - t % 3) * D
        win = g_ref[pl.ds(row, 32), pl.ds(pl.multiple_of(col, 16), 48), :].reshape(1536, 256)
        acc[...] += dot(win, w[pl.ds(pl.multiple_of(t * 1024, 1024), 1024), :], NT)

    out_ref[...] = acc[...].astype(BF).reshape(32, 48, 1024)


def body(features, conv_weight, conv_bias, proj_weight, cotangent):
    core = lax.axis_index("core")
    is0 = core == 0
    core_s = core.astype(jnp.int32).reshape(1)
    smem = pl.BlockSpec(memory_space=pltpu.SMEM)

    def send(x, dr, dc):
        perm = []
        for i in range(128):
            r, c = i // 8, i % 8
            step = dc[c % 2]
            r2, c2 = r + dr, c + step
            if 0 <= r2 < 16 and 0 <= c2 < 8:
                perm.append((i, r2 * 8 + c2))
        return lax.ppermute(x, ALL, perm)

    SAME, INNER, OUTER = (0, 0), (1, -1), (-1, 1)

    shard = jnp.concatenate([conv_weight, proj_weight], axis=0)
    halves = jnp.where(is0, shard[:, 128:], shard[:, :128])
    keep = jnp.where(is0, shard[:, :128], shard[:, 128:])
    got = send(halves, 0, INNER)
    low, high = jnp.where(is0, keep, got), jnp.where(is0, got, keep)
    chunk = jnp.concatenate([low[:72], high[:72], low[72:], high[72:], jnp.zeros((4, 128), BF)], axis=0)
    mine = lax.all_to_all(jnp.broadcast_to(chunk[None], (64, 152, 128)), CHIPS, 0, 0)
    other = send(mine, 0, INNER)
    pm, po = mine[:, 144:148].reshape(256, 128), other[:, 144:148].reshape(256, 128)
    proj = jnp.concatenate([jnp.where(is0, pm, po), jnp.where(is0, po, pm)], axis=1)

    ft = features.reshape(2, 16, 3, 16, 1024).transpose(4, 0, 2, 1, 3).reshape(1024, 1536)

    wscratch = pltpu.VMEM((64, 144, 256), BF)
    tile_f32 = jax.ShapeDtypeStruct((32, 48, 256), F32)
    tile_bf = jax.ShapeDtypeStruct((32, 48, 256), BF)
    strip = jax.ShapeDtypeStruct((16, 48, 256), BF)
    side = jax.ShapeDtypeStruct((64, 16, 256), BF)

    n, s, l, r = pl.pallas_call(
        halo_kernel,
        out_shape=(strip, strip, side, side),
        in_specs=[smem, vmem(), hbm(), hbm()],
        out_specs=(vmem(),) * 4,
        scratch_shapes=[wscratch, pltpu.VMEM((16, 80, 256), F32), pltpu.SemaphoreType.DMA((2,))],
        compiler_params=params(),
        cost_estimate=cost(int(3.5e9), 9 << 20),
        name="halo",
    )(core_s, features, mine, other)
    inner_out, outer_out = jnp.where(is0, r, l), jnp.where(is0, l, r)
    inner = send(inner_out, 0, INNER)
    zero = jnp.zeros((16, 32, 256), BF)

    def widen(x):
        return jnp.where(is0, jnp.concatenate([zero, x], 1), jnp.concatenate([x, zero], 1))

    from_s = send(n + widen(inner[0:16]), -1, SAME)
    from_n = send(s + widen(inner[48:64]), 1, SAME)
    outer = send(outer_out[16:48], 0, OUTER)
    corner_s = send(outer_out[0:16], -1, OUTER)
    corner_n = send(outer_out[48:64], 1, OUTER)

    pre, hg = pl.pallas_call(
        own_kernel,
        out_shape=(tile_f32, tile_f32),
        in_specs=[smem, vmem(), hbm(), hbm(), vmem(), vmem(), vmem()],
        out_specs=(vmem(),) * 2,
        scratch_shapes=[wscratch, pltpu.SemaphoreType.DMA((2,))],
        compiler_params=params(),
        cost_estimate=cost(int(4.0e9), 12 << 20),
        name="own",
    )(core_s, features, mine, other, cotangent, proj, conv_bias.reshape(1, 256))

    hidden, g = pl.pallas_call(
        point_kernel,
        out_shape=(tile_bf, tile_bf),
        in_specs=[smem] + [vmem()] * 8,
        out_specs=(vmem(),) * 2,
        compiler_params=params(),
        cost_estimate=cost(int(1e8), 6 << 20),
        name="point",
    )(core_s, pre, hg, from_n, from_s, inner[16:48], outer, corner_n, corner_s)

    gl, gr = g[:, 0:16], g[:, 32:48]
    g_inner, g_outer = jnp.where(is0, gr, gl), jnp.where(is0, gl, gr)
    top = send(g[16:32], 1, SAME)
    bottom = send(g[0:16], -1, SAME)
    h_outer = send(g_outer, 0, OUTER)
    h_top = send(g_outer[16:32], 1, OUTER)
    h_bottom = send(g_outer[0:16], -1, OUTER)
    h_inner = send(g_inner, 0, INNER)
    edge = jnp.concatenate([top, bottom], axis=0)
    edge = jnp.where(is0, edge[:, 32:48], edge[:, 0:16])
    edge = send(edge, 0, INNER)

    projected, proj_term, bias_term = pl.pallas_call(
        proj_kernel,
        out_shape=(tile_bf, jax.ShapeDtypeStruct((256, 256), F32), jax.ShapeDtypeStruct((1, 256), F32)),
        in_specs=[vmem()] * 4,
        out_specs=(vmem(),) * 3,
        compiler_params=params(),
        cost_estimate=cost(int(4e8), 4 << 20),
        name="proj",
    )(hidden, cotangent, proj, g)

    outer_col = jnp.concatenate([h_top, h_outer, h_bottom], axis=0)
    inner_col = jnp.concatenate([edge[0:16], h_inner, edge[16:32]], axis=0)
    middle = jnp.concatenate([top, g, bottom], axis=0)
    gpad = jnp.concatenate(
        [jnp.where(is0, outer_col, inner_col), middle, jnp.where(is0, inner_col, outer_col)], axis=1
    )

    half = jax.ShapeDtypeStruct((9216, 128), BF)
    w_mine, w_other = pl.pallas_call(
        wgrad_kernel,
        grid=(9,),
        out_shape=(half, half),
        in_specs=[smem, vmem(), vmem()],
        out_specs=(pl.BlockSpec((1024, 128), lambda t: (t, 0)),) * 2,
        compiler_params=params(),
        cost_estimate=cost(int(7.2e9), 12 << 20),
        name="wgrad",
    )(core_s, ft, gpad)

    pl_, ph = proj_term[:, :128], proj_term[:, 128:]
    bias_rows = jnp.pad(bias_term.reshape(64, 1, 4), ((0, 0), (0, 3), (0, 124)))

    def with_proj(w, p):
        return jnp.concatenate([w.reshape(64, 144, 128), p.astype(BF).reshape(64, 4, 128), bias_rows.astype(BF)], 1)

    received = send(with_proj(w_other, jnp.where(is0, ph, pl_)), 0, INNER)
    total = with_proj(w_mine, jnp.where(is0, pl_, ph)).astype(F32) + received.astype(F32)
    pieces = lax.all_to_all(total.astype(BF), CHIPS, 0, 0)

    features_grad = pl.pallas_call(
        fgrad_kernel,
        out_shape=jax.ShapeDtypeStruct((32, 48, 1024), BF),
        in_specs=[smem, vmem(), hbm(), hbm()],
        out_specs=vmem(),
        scratch_shapes=[wscratch, pltpu.VMEM((1536, 1024), F32), pltpu.SemaphoreType.DMA((2,))],
        compiler_params=params(),
        cost_estimate=cost(int(7.2e9), 12 << 20),
        name="fgrad",
    )(core_s, gpad, mine, other)

    sums = jnp.sum(pieces.astype(F32), axis=0)
    lo, hi = jnp.concatenate([sums[:72], sums[144:146]], 0), jnp.concatenate([sums[72:144], sums[146:148]], 0)
    keep = jnp.where(is0, lo, hi)
    got = send(jnp.where(is0, hi, lo), 0, INNER)
    full = jnp.concatenate([jnp.where(is0, keep, got), jnp.where(is0, got, keep)], axis=1)
    bias_grad = jnp.where(is0, sums[148, 0:2], sums[148, 2:4])
    return projected, features_grad, full[:72], full[72:74], bias_grad


def solution(mesh):
    fine = Mesh(mesh.devices.reshape(4, 4, 4, 2), ALL)
    tile = P(("y", "x"), ("z", "core"), None)
    rows = P(ALL, None)
    return jax.shard_map(
        body,
        mesh=fine,
        in_specs=(tile, rows, P(), rows, tile),
        out_specs=(tile, tile, rows, rows, P(ALL)),
        check_vma=False,
    )
```

time: 541 us -> 213 us (0.39)
  waiting for transfers between devices: 259 us -> 31.7 us
  matrix products: 88.3 us -> 0 us
  blocking collectives: 126 us -> 44.4 us
  Pallas kernels: 0 us -> 56 us
  starting transfers between devices: 21.4 us -> 50.1 us
  between operations: 14.1 us -> 1.1 us
    reduce_scatter x1 -> x0, waiting for transfers between devices: 163 us -> none  [body(): lax.psum_scatter(weight_term, ('row', 'col'), scatter_dimension=0, tiled=...]
    dot_general x30 -> x0, matrix products: 88.3 us -> none  [the longest x9 50.8 us: body(): lax.dot_general(back, conv_full[tap * in_channels:(tap + 1) * in_channels...]
    unnamed x1 -> x0, blocking collectives: 67.1 us -> none
    unnamed x4 -> x0, waiting for transfers between devices: 59.2 us -> none
    all_gather x1 -> x0, blocking collectives: 58.4 us -> none  [body(): lax.all_gather(proj_weight, ('row', 'col'), axis=0, tiled=True)]
    pallas_call x0 -> x6, Pallas kernels: none -> 56 us  [the longest x1 16.1 us: body(): pl.pallas_call(fgrad_kernel, out_shape=jax.ShapeDtypeStruct((32, 48, 1024...]
    all_to_all x0 -> x1, blocking collectives: none -> 44.4 us  [body(): lax.all_to_all(jnp.broadcast_to(chunk[None], (64, 152, 128)), CHIPS, 0, 0)]
    ppermute x8 -> x17, waiting for transfers between devices: 36.7 us -> 15.8 us  [send(): return lax.ppermute(x, ALL, perm)]
  transfers between devices with their start and end apart: 11 -> 18, of which waited for: 4 -> 7; matrix products, arithmetic and copies ran while one was open for 15% -> 6% of each run, Pallas kernels for 0% -> 14%
where the time goes in v1:
time: 213 us; the launch traced here: 212 us
  Pallas kernels  56 us (26%)
  starting transfers between devices  50.1 us (24%)
  blocking collectives  44.4 us (21%)
  waiting for transfers between devices  31.7 us (15%)
  other arithmetic  15.2 us (7%)
  local copies, waits for them, and re-layouts  13.7 us (6%)
    all_to_all x1, blocking collectives, body(): lax.all_to_all(jnp.broadcast_to(chunk[None], (64, 152, 128)), CHIPS, 0, 0)  44.4 us
    ppermute x17, starting transfers between devices, send(): return lax.ppermute(x, ALL, perm)  31.8 us
    all_to_all x1, starting transfers between devices, body(): pieces = lax.all_to_all(total.astype(BF), CHIPS, 0, 0)  18.3 us
    pallas_call x1, Pallas kernels, body(): pl.pallas_call(fgrad_kernel, out_shape=jax.ShapeDtypeStruct((32, 48, 1024...  16.1 us
    all_to_all x1, waiting for transfers between devices, body(): pieces = lax.all_to_all(total.astype(BF), CHIPS, 0, 0)  15.9 us
    ppermute x17, waiting for transfers between devices, send(): return lax.ppermute(x, ALL, perm)  15.8 us
    pallas_call x1, Pallas kernels, body(): pl.pallas_call(wgrad_kernel, grid=(9,), out_shape=(half, half), in_specs=...  12.6 us
    pallas_call x1, Pallas kernels, body(): pl.pallas_call(own_kernel, out_shape=(tile_f32, tile_f32), in_specs=[smem...  10.4 us
  transfers between devices with their start and end apart: 18, of which 7 were waited for; matrix products, arithmetic and copies ran while one was open for 6% of the time, Pallas kernels for 14%

profile of v1, /device:TPU:1, one launch (start us, length us, event | category | flops | bytes accessed | tf_op | source)
XLA Modules:
  0.0 212.2 jit_solution(15734868533400351704)
XLA Ops:
  0.6 0.8 constant_dynamic-update-slice_fusion.1
  1.4 0.7 constant_dynamic-update-slice_fusion
  2.1 1.5 collective-permute-start
  3.6 0.8 collective-permute-done
  4.9 44.4 %all_to_all.10.mine_ref = bf16[64,152,128]{2,1,0:T(8,128)(2,1)S(1)} all-to-all(bf16[64,152,128]{2,1,0:T(8,128)(2,1)S(1)} %broadcast_in_dim.5), channel_id=1, replica_groups=mesh['y'=4,'x'=4,'z'=4,'core'=2] {'y','x','z'}, dimensions={0} | all-to-all | bytes 4980736 | tf_op jit(solution)/shard_map/all_to_all | solution.py:175
  49.3 1.9 collective-permute-start.1
  51.2 4.3 %collective-permute-done.1.other_ref = bf16[64,152,128]{2,1,0:T(8,128)(2,1)S(1)} collective-permute-done((bf16[64,152,128]{2,1,0:T(8,128)(2,1)S(1)}, bf16[64,152,128]{2,1,0:T(8,128)(2,1)S(1)}, u32[]{:S(2)}, u32[]{:S(2)}) %collective-permute-start.1) | collective-permute-done | bytes 2490400 | tf_op jit(solution)/shard_map/ppermute | solution.py:165
  55.6 1.5 copy-done.11
  57.1 9.1 %halo.1 = (bf16[16,48,256]{2,1,0:T(8,128)(2,1)}, bf16[16,48,256]{2,1,0:T(8,128)(2,1)}, bf16[64,16,256]{2,1,0:T(8,128)(2,1)}, bf16[64,16,256]{2,1,0:T(8,128)(2,1)}) custom-call(s32[1]{0:T(128)} %bitcast.core_ref, bf16[32,48,1024]{2,1,0:T(8,128)(2,1)} %f_ref.3, bf16[64,152,128]{2,1,0:T(8,128)(2,1)} %copy-done.2, bf16[64,152,128]{2,1,0:T(8,128)(2,1)} %copy-done.11), custom_call_target="tpu_custom_call" | custom-call | flops 3500000000 | bytes 9437184 | tf_op jit(solution)/shard_map/halo/pallas_call | solution.py:188
  66.1 2.3 %broadcast_select_fusion.2 = (bf16[64,16,256]{2,1,0:T(8,128)(2,1)}, bf16[64,16,256]{2,1,0:T(8,128)(2,1)}) fusion(bf16[64,16,256]{2,1,0:T(8,128)(2,1)} %get-tuple-element.22, bf16[64,16,256]{2,1,0:T(8,128)(2,1)} %get-tuple-element.21, pred[]{:T(512)S(6)} %eq.3), kind=kLoop, calls=%fused_computation.10 | loop fusion | flops 524288 | bytes 2097153 | tf_op jit(solution)/shard_map/jit(_where)/select_n | solution.py:198
  69.1 2.9 %copy.16.ft_ref = bf16[1024,1536]{1,0:T(8,128)(2,1)} copy(bf16[1024,1536]{0,1:T(8,128)(2,1)S(1)} %bitcast.14) | data formatting | bytes 6291456 | tf_op jit(solution)/shard_map/reshape | solution.py:180
  72.0 1.0 slice.149
  73.1 2.3 %collective-permute-start.5 = (bf16[32,16,256]{2,1,0:T(8,128)(2,1)S(1)}, bf16[32,16,256]{2,1,0:T(8,128)(2,1)S(1)}, u32[]{:S(2)}, u32[]{:S(2)}) collective-permute-start(bf16[32,16,256]{2,1,0:T(8,128)(2,1)S(1)} %slice.149), channel_id=1, source_target_pairs={{1,2},{2,1},{3,4},{4,3},{5,6},{6,5},{9,10},{10,9},{11,12},{12,11},... | collective-permute-start | bytes 786440 | tf_op jit(solution)/shard_map/ppermute | solution.py:165
  75.4 1.0 fusion.8
  76.4 3.3 %collective-permute-start.6 = (bf16[16,16,256]{2,1,0:T(8,128)(2,1)S(1)}, bf16[16,16,256]{2,1,0:T(8,128)(2,1)S(1)}, u32[]{:S(2)}, u32[]{:S(2)}) collective-permute-start(bf16[16,16,256]{2,1,0:T(8,128)(2,1)S(1)} %get-tuple-element.42), channel_id=1, source_target_pairs={{1,10},{2,9},{3,12},{4,11},{5,14},{6,13},{9,18},{10,17},{11,20},{1... | collective-permute-start | bytes 393224 | tf_op jit(solution)/shard_map/ppermute | solution.py:165
  79.7 1.3 collective-permute-start.7
  81.0 1.0 broadcast_select_fusion.7
  82.0 1.0 fusion.9
  83.1 4.4 %collective-permute-start.3 = (bf16[16,48,256]{2,1,0:T(8,128)(2,1)S(1)}, bf16[16,48,256]{2,1,0:T(8,128)(2,1)S(1)}, u32[]{:S(2)}, u32[]{:S(2)}) collective-permute-start(bf16[16,48,256]{2,1,0:T(8,128)(2,1)S(1)} %select_add_fusion.1), channel_id=1, source_target_pairs={{0,8},{1,9},{2,10},{3,11},{4,12},{5,13},{6,14},{7,15},{8,16},{9,17... | collective-permute-start | bytes 1179656 | tf_op jit(solution)/shard_map/ppermute | solution.py:165
  87.6 1.3 collective-permute-start.4
  88.9 0.7 pad_maximum_fusion.2.proj_ref
  89.6 10.4 %own.1 = (f32[32,48,256]{2,1,0:T(8,128)}, f32[32,48,256]{2,1,0:T(8,128)}) custom-call(s32[1]{0:T(128)} %bitcast.core_ref, bf16[32,48,1024]{2,1,0:T(8,128)(2,1)} %f_ref.3, bf16[64,152,128]{2,1,0:T(8,128)(2,1)} %copy-done.2, bf16[64,152,128]{2,1,0:T(8,128)(2,1)} %copy-done.11, bf16[32,48,256]{2,1,0:T(8,128)(2,1)} %cot_ref.3, ...), custom_call_target="tpu_custom_call" | custom-call | flops 4000000000 | bytes 12582912 | tf_op jit(solution)/shard_map/own/pallas_call | solution.py:211
  100.0 1.7 slice.148.inner_ref
  102.7 4.6 %point.1 = (bf16[32,48,256]{2,1,0:T(8,128)(2,1)}, bf16[32,48,256]{2,1,0:T(8,128)(2,1)}) custom-call(s32[1]{0:T(128)} %bitcast.core_ref, f32[32,48,256]{2,1,0:T(8,128)} %get-tuple-element.18.pre_ref, f32[32,48,256]{2,1,0:T(8,128)} %get-tuple-element.19.hg_ref, bf16[16,48,256]{2,1,0:T(8,128)(2,1)} %copy-done.4, bf16[16,48,256]{2,1,0:T(8,128)(2,1)} %copy-done.5, ...), custom_call_target="tpu_custom_call" | custom-call | flops 100000000 | bytes 6291456 | tf_op jit(solution)/shard_map/point/pallas_call | solution.py:222
  107.3 1.1 broadcast_select_fusion.4
  108.4 1.2 fusion.7
  109.6 4.0 %collective-permute-start.11 = (bf16[16,48,256]{2,1,0:T(8,128)(2,1)S(1)}, bf16[16,48,256]{2,1,0:T(8,128)(2,1)S(1)}, u32[]{:S(2)}, u32[]{:S(2)}) collective-permute-start(bf16[16,48,256]{2,1,0:T(8,128)(2,1)S(1)} %get-tuple-element.40), channel_id=1, source_target_pairs={{0,8},{1,9},{2,10},{3,11},{4,12},{5,13},{6,14},{7,15},{8,16},{9,17... | collective-permute-start | bytes 1179656 | tf_op jit(solution)/shard_map/ppermute | solution.py:165
  113.6 3.8 %collective-permute-start.9 = (bf16[32,16,256]{2,1,0:T(8,128)(2,1)S(1)}, bf16[32,16,256]{2,1,0:T(8,128)(2,1)S(1)}, u32[]{:S(2)}, u32[]{:S(2)}) collective-permute-start(bf16[32,16,256]{2,1,0:T(8,128)(2,1)S(1)} %get-tuple-element.38), channel_id=1, source_target_pairs={{1,2},{2,1},{3,4},{4,3},{5,6},{6,5},{9,10},{10,9},{11,12},{12,11},... | collective-permute-start | bytes 786440 | tf_op jit(solution)/shard_map/ppermute | solution.py:165
  117.4 1.7 collective-permute-start.8
  119.1 1.3 collective-permute-start.10
  120.4 1.5 collective-permute-start.12
  121.9 3.2 %proj.1 = (bf16[32,48,256]{2,1,0:T(8,128)(2,1)}, f32[256,256]{1,0:T(8,128)}, f32[1,256]{1,0:T(1,128)}) custom-call(bf16[32,48,256]{2,1,0:T(8,128)(2,1)} %get-tuple-element.24.hid_ref, bf16[32,48,256]{2,1,0:T(8,128)(2,1)} %cot_ref.3, bf16[256,256]{1,0:T(8,128)(2,1)} %pad_maximum_fusion.2.proj_ref, bf16[32,48,256]{2,1,0:T(8,128)(2,1)} %get-tuple-element.25.g_ref), custom_call_target="tpu_custom_call" | custom-call | flops 400000000 | bytes 4194304 | tf_op jit(solution)/shard_map/proj/pallas_call | solution.py:244
  125.1 0.7 convert_reduce_fusion.1
  125.9 1.0 select_convert_fusion.1
  127.1 4.3 %collective-permute-done.12 = bf16[16,48,256]{2,1,0:T(8,128)(2,1)S(1)} collective-permute-done((bf16[16,48,256]{2,1,0:T(8,128)(2,1)S(1)}, bf16[16,48,256]{2,1,0:T(8,128)(2,1)S(1)}, u32[]{:S(2)}, u32[]{:S(2)}) %collective-permute-start.12) | collective-permute-done | bytes 393248 | tf_op jit(solution)/shard_map/ppermute | solution.py:165
  131.6 1.4 collective-permute-done.13
  133.2 1.7 pad_maximum_fusion.g_ref
  134.9 12.6 %wgrad.1 = (bf16[9216,128]{1,0:T(8,128)(2,1)}, bf16[9216,128]{1,0:T(8,128)(2,1)}) custom-call(s32[1]{0:T(128)} %bitcast.core_ref, bf16[1024,1536]{1,0:T(8,128)(2,1)} %copy.16.ft_ref, bf16[64,80,256]{2,1,0:T(8,128)(2,1)} %pad_maximum_fusion.g_ref), custom_call_target="tpu_custom_call" | custom-call | flops 7200000000 | bytes 12582912 | tf_op jit(solution)/shard_map/wgrad/pallas_call | solution.py:262
  147.5 2.0 fusion.2
  149.8 4.6 %collective-permute-done.15 = bf16[64,152,128]{2,1,0:T(8,128)(2,1)S(1)} collective-permute-done((bf16[64,152,128]{2,1,0:T(8,128)(2,1)S(1)}, bf16[64,152,128]{2,1,0:T(8,128)(2,1)S(1)}, u32[]{:S(2)}, u32[]{:S(2)}) %collective-permute-start.15) | collective-permute-done | bytes 2490400 | tf_op jit(solution)/shard_map/ppermute | solution.py:165
  154.3 2.3 %add_convert_fusion = bf16[64,152,128]{2,1,0:T(8,128)(2,1)} fusion(bf16[64,152,128]{2,1,0:T(8,128)(2,1)S(1)} %collective-permute-done.15, bf16[64,1,4]{2,1,0:T(2,128)(2,1)S(1)} %reshape.57, bf16[64,4,128]{2,1,0:T(4,128)(2,1)S(1)} %bitcast.18, bf16[64,144,128]{2,1,0:T(8,128)(2,1)S(1)} %bitcast.16), kind=kLoop, calls=%fused_computation.2 | loop fusion | flops 13697024 | bytes 7406080 | tf_op jit(solution)/shard_map/convert_element_type | solution.py:281
  156.6 18.3 %all-to-all-start.1 = ((bf16[64,152,128]{2,1,0:T(8,128)(2,1)}), bf16[64,152,128]{2,1,0:T(8,128)(2,1)S(1)}, u32[]{:S(2)}, u32[]{:S(2)}) async-start(bf16[64,152,128]{2,1,0:T(8,128)(2,1)} %add_convert_fusion), calls=%async_computation.1 | async-start | bytes 4980736 | tf_op jit(solution)/shard_map/all_to_all | solution.py:281
  174.9 16.1 %fgrad.1 = bf16[32,48,1024]{2,1,0:T(8,128)(2,1)} custom-call(s32[1]{0:T(128)} %bitcast.core_ref, bf16[64,80,256]{2,1,0:T(8,128)(2,1)} %pad_maximum_fusion.g_ref, bf16[64,152,128]{2,1,0:T(8,128)(2,1)} %copy-done.2, bf16[64,152,128]{2,1,0:T(8,128)(2,1)} %copy-done.11), custom_call_target="tpu_custom_call" | custom-call | flops 7200000000 | bytes 12582912 | tf_op jit(solution)/shard_map/fgrad/pallas_call | solution.py:283
  191.0 15.9 %all-to-all-done.1 = bf16[64,152,128]{2,1,0:T(8,128)(2,1)S(1)} async-done(((bf16[64,152,128]{2,1,0:T(8,128)(2,1)}), bf16[64,152,128]{2,1,0:T(8,128)(2,1)S(1)}, u32[]{:S(2)}, u32[]{:S(2)}) %all-to-all-start.1) | async-done | bytes 2490400 | tf_op jit(solution)/shard_map/all_to_all | solution.py:281
  207.3 2.7 %collective-permute-start.16 = (f32[74,128]{1,0:T(8,128)S(1)}, f32[74,128]{1,0:T(8,128)S(1)}, u32[]{:S(2)}, u32[]{:S(2)}) collective-permute-start(f32[74,128]{1,0:T(8,128)S(1)} %fusion.4), channel_id=1, source_target_pairs={{0,1},{1,0},{2,3},{3,2},{4,5},{5,4},{6,7},{7,6},{8,9},{9,8},{10,11... | collective-permute-start | bytes 113672 | tf_op jit(solution)/shard_map/ppermute | solution.py:165
  210.1 0.6 fusion.6
  210.9 0.6 fusion.3
  211.6 0.6 pad_maximum_fusion.5
  (66 shorter events, 3.8 us)
Async XLA Ops:
  2.1 2.3 %collective-permute-start = (bf16[74,128]{1,0:T(8,128)(2,1)S(1)}, bf16[74,128]{1,0:T(8,128)(2,1)S(1)}, u32[]{:S(2)}, u32[]{:S(2)}) collective-permute-start(bf16[74,128]{1,0:T(8,128)(2,1)S(1)} %broadcast_select_fusion.12), channel_id=1, source_target_pairs={{0,1},{1,0},{2,3},{3,2},{4,5},{5,4},{6,7},{7,6},{8,9},{9,8},{10,11... | collective-permute-start | bytes 56840 | tf_op jit(solution)/shard_map/ppermute | solution.py:165
  49.3 6.3 %copy-start.2 = (bf16[64,152,128]{2,1,0:T(8,128)(2,1)}, bf16[64,152,128]{2,1,0:T(8,128)(2,1)S(1)}, u32[]{:S(2)}) copy-start(bf16[64,152,128]{2,1,0:T(8,128)(2,1)S(1)} %all_to_all.10.mine_ref) | copy-start | bytes 7471108
  49.3 6.3 %collective-permute-start.1 = (bf16[64,152,128]{2,1,0:T(8,128)(2,1)S(1)}, bf16[64,152,128]{2,1,0:T(8,128)(2,1)S(1)}, u32[]{:S(2)}, u32[]{:S(2)}) collective-permute-start(bf16[64,152,128]{2,1,0:T(8,128)(2,1)S(1)} %all_to_all.10.mine_ref), channel_id=1, source_target_pairs={{0,1},{1,0},{2,3},{3,2},{4,5},{5,4},{6,7},{7,6},{8,9},{9,8},{10,11... | collective-permute-start | bytes 7471112 | tf_op jit(solution)/shard_map/ppermute | solution.py:165
  55.6 1.5 copy-start.11
  57.1 11.7 %copy-start.1 = (bf16[32,48,1024]{2,1,0:T(8,128)(2,1)S(1)}, bf16[32,48,1024]{2,1,0:T(8,128)(2,1)}, u32[]{:S(2)}) copy-start(bf16[32,48,1024]{2,1,0:T(8,128)(2,1)} %f_ref.3) | copy-start | bytes 9437188
  68.4 13.6 %collective-permute-start.2 = (bf16[64,16,256]{2,1,0:T(8,128)(2,1)}, bf16[64,16,256]{2,1,0:T(8,128)(2,1)}, u32[]{:S(2)}, u32[]{:S(2)}) collective-permute-start(bf16[64,16,256]{2,1,0:T(8,128)(2,1)} %get-tuple-element.36), channel_id=1, source_target_pairs={{0,1},{1,0},{2,3},{3,2},{4,5},{5,4},{6,7},{7,6},{8,9},{9,8},{10,11... | collective-permute-start | bytes 1572872 | tf_op jit(solution)/shard_map/ppermute | solution.py:165
  69.1 13.9 %copy-start.7 = (bf16[16,48,256]{2,1,0:T(8,128)(2,1)S(1)}, bf16[16,48,256]{2,1,0:T(8,128)(2,1)}, u32[]{:S(2)}) copy-start(bf16[16,48,256]{2,1,0:T(8,128)(2,1)} %get-tuple-element.20) | copy-start | bytes 1179652
  72.0 15.5 %copy-start.6 = (bf16[16,48,256]{2,1,0:T(8,128)(2,1)S(1)}, bf16[16,48,256]{2,1,0:T(8,128)(2,1)}, u32[]{:S(2)}) copy-start(bf16[16,48,256]{2,1,0:T(8,128)(2,1)} %get-tuple-element.23) | copy-start | bytes 1179652
  73.1 28.6 %collective-permute-start.5 = (bf16[32,16,256]{2,1,0:T(8,128)(2,1)S(1)}, bf16[32,16,256]{2,1,0:T(8,128)(2,1)S(1)}, u32[]{:S(2)}, u32[]{:S(2)}) collective-permute-start(bf16[32,16,256]{2,1,0:T(8,128)(2,1)S(1)} %slice.149), channel_id=1, source_target_pairs={{1,2},{2,1},{3,4},{4,3},{5,6},{6,5},{9,10},{10,9},{11,12},{12,11},... | collective-permute-start | bytes 786440 | tf_op jit(solution)/shard_map/ppermute | solution.py:165
  76.4 25.3 %collective-permute-start.6 = (bf16[16,16,256]{2,1,0:T(8,128)(2,1)S(1)}, bf16[16,16,256]{2,1,0:T(8,128)(2,1)S(1)}, u32[]{:S(2)}, u32[]{:S(2)}) collective-permute-start(bf16[16,16,256]{2,1,0:T(8,128)(2,1)S(1)} %get-tuple-element.42), channel_id=1, source_target_pairs={{1,10},{2,9},{3,12},{4,11},{5,14},{6,13},{9,18},{10,17},{11,20},{1... | collective-permute-start | bytes 393224 | tf_op jit(solution)/shard_map/ppermute | solution.py:165
  79.7 22.0 %collective-permute-start.7 = (bf16[16,16,256]{2,1,0:T(8,128)(2,1)S(1)}, bf16[16,16,256]{2,1,0:T(8,128)(2,1)S(1)}, u32[]{:S(2)}, u32[]{:S(2)}) collective-permute-start(bf16[16,16,256]{2,1,0:T(8,128)(2,1)S(1)} %get-tuple-element.41), channel_id=1, source_target_pairs={{9,2},{10,1},{11,4},{12,3},{13,6},{14,5},{17,10},{18,9},{19,12},{2... | collective-permute-start | bytes 393224 | tf_op jit(solution)/shard_map/ppermute | solution.py:165
  83.1 18.6 %collective-permute-start.3 = (bf16[16,48,256]{2,1,0:T(8,128)(2,1)S(1)}, bf16[16,48,256]{2,1,0:T(8,128)(2,1)S(1)}, u32[]{:S(2)}, u32[]{:S(2)}) collective-permute-start(bf16[16,48,256]{2,1,0:T(8,128)(2,1)S(1)} %select_add_fusion.1), channel_id=1, source_target_pairs={{0,8},{1,9},{2,10},{3,11},{4,12},{5,13},{6,14},{7,15},{8,16},{9,17... | collective-permute-start | bytes 1179656 | tf_op jit(solution)/shard_map/ppermute | solution.py:165
  87.6 14.1 %collective-permute-start.4 = (bf16[16,48,256]{2,1,0:T(8,128)(2,1)S(1)}, bf16[16,48,256]{2,1,0:T(8,128)(2,1)S(1)}, u32[]{:S(2)}, u32[]{:S(2)}) collective-permute-start(bf16[16,48,256]{2,1,0:T(8,128)(2,1)S(1)} %select_add_fusion), channel_id=1, source_target_pairs={{8,0},{9,1},{10,2},{11,3},{12,4},{13,5},{14,6},{15,7},{16,8},{17,9... | collective-permute-start | bytes 1179656 | tf_op jit(solution)/shard_map/ppermute | solution.py:165
  101.7 0.7 copy-start.9
  101.7 0.7 copy-start.10
  101.7 0.8 copy-start.8
  101.7 0.9 copy-start.4
  101.7 1.0 copy-start.5
  109.6 17.4 %collective-permute-start.11 = (bf16[16,48,256]{2,1,0:T(8,128)(2,1)S(1)}, bf16[16,48,256]{2,1,0:T(8,128)(2,1)S(1)}, u32[]{:S(2)}, u32[]{:S(2)}) collective-permute-start(bf16[16,48,256]{2,1,0:T(8,128)(2,1)S(1)} %get-tuple-element.40), channel_id=1, source_target_pairs={{0,8},{1,9},{2,10},{3,11},{4,12},{5,13},{6,14},{7,15},{8,16},{9,17... | collective-permute-start | bytes 1179656 | tf_op jit(solution)/shard_map/ppermute | solution.py:165
  113.6 17.9 %collective-permute-start.9 = (bf16[32,16,256]{2,1,0:T(8,128)(2,1)S(1)}, bf16[32,16,256]{2,1,0:T(8,128)(2,1)S(1)}, u32[]{:S(2)}, u32[]{:S(2)}) collective-permute-start(bf16[32,16,256]{2,1,0:T(8,128)(2,1)S(1)} %get-tuple-element.38), channel_id=1, source_target_pairs={{1,2},{2,1},{3,4},{4,3},{5,6},{6,5},{9,10},{10,9},{11,12},{12,11},... | collective-permute-start | bytes 786440 | tf_op jit(solution)/shard_map/ppermute | solution.py:165
  117.4 14.1 %collective-permute-start.8 = (bf16[16,16,256]{2,1,0:T(8,128)(2,1)S(1)}, bf16[16,16,256]{2,1,0:T(8,128)(2,1)S(1)}, u32[]{:S(2)}, u32[]{:S(2)}) collective-permute-start(bf16[16,16,256]{2,1,0:T(8,128)(2,1)S(1)} %get-tuple-element.50), channel_id=1, source_target_pairs={{1,10},{2,9},{3,12},{4,11},{5,14},{6,13},{9,18},{10,17},{11,20},{1... | collective-permute-start | bytes 393224 | tf_op jit(solution)/shard_map/ppermute | solution.py:165
  119.1 12.5 %collective-permute-start.10 = (bf16[16,16,256]{2,1,0:T(8,128)(2,1)S(1)}, bf16[16,16,256]{2,1,0:T(8,128)(2,1)S(1)}, u32[]{:S(2)}, u32[]{:S(2)}) collective-permute-start(bf16[16,16,256]{2,1,0:T(8,128)(2,1)S(1)} %get-tuple-element.49), channel_id=1, source_target_pairs={{9,2},{10,1},{11,4},{12,3},{13,6},{14,5},{17,10},{18,9},{19,12},{2... | collective-permute-start | bytes 393224 | tf_op jit(solution)/shard_map/ppermute | solution.py:165
  120.4 10.9 %collective-permute-start.12 = (bf16[16,48,256]{2,1,0:T(8,128)(2,1)S(1)}, bf16[16,48,256]{2,1,0:T(8,128)(2,1)S(1)}, u32[]{:S(2)}, u32[]{:S(2)}) collective-permute-start(bf16[16,48,256]{2,1,0:T(8,128)(2,1)S(1)} %get-tuple-element.39), channel_id=1, source_target_pairs={{8,0},{9,1},{10,2},{11,3},{12,4},{13,5},{14,6},{15,7},{16,8},{17,9... | collective-permute-start | bytes 1179656 | tf_op jit(solution)/shard_map/ppermute | solution.py:165
  126.9 6.1 %collective-permute-start.14 = (bf16[32,16,256]{2,1,0:T(8,128)(2,1)S(1)}, bf16[32,16,256]{2,1,0:T(8,128)(2,1)S(1)}, u32[]{:S(2)}, u32[]{:S(2)}) collective-permute-start(bf16[32,16,256]{2,1,0:T(8,128)(2,1)S(1)} %get-tuple-element.37), channel_id=1, source_target_pairs={{0,1},{1,0},{2,3},{3,2},{4,5},{5,4},{6,7},{7,6},{8,9},{9,8},{10,11... | collective-permute-start | bytes 786440 | tf_op jit(solution)/shard_map/ppermute | solution.py:165
  127.1 6.1 %copy-start = (bf16[32,48,256]{2,1,0:T(8,128)(2,1)S(1)}, bf16[32,48,256]{2,1,0:T(8,128)(2,1)}, u32[]{:S(2)}) copy-start(bf16[32,48,256]{2,1,0:T(8,128)(2,1)} %get-tuple-element.25.g_ref) | copy-start | bytes 2359300
  131.4 1.6 collective-permute-start.13
  147.5 6.8 %copy-start.3 = (bf16[9216,128]{1,0:T(8,128)(2,1)S(1)}, bf16[9216,128]{1,0:T(8,128)(2,1)}, u32[]{:S(2)}) copy-start(bf16[9216,128]{1,0:T(8,128)(2,1)} %get-tuple-element.27) | copy-start | bytes 7077892
  149.5 4.8 %collective-permute-start.15 = (bf16[64,152,128]{2,1,0:T(8,128)(2,1)S(1)}, bf16[64,152,128]{2,1,0:T(8,128)(2,1)S(1)}, u32[]{:S(2)}, u32[]{:S(2)}) collective-permute-start(bf16[64,152,128]{2,1,0:T(8,128)(2,1)S(1)} %fusion.2), channel_id=1, source_target_pairs={{0,1},{1,0},{2,3},{3,2},{4,5},{5,4},{6,7},{7,6},{8,9},{9,8},{10,11... | collective-permute-start | bytes 7471112 | tf_op jit(solution)/shard_map/ppermute | solution.py:165
  156.6 50.3 %all-to-all-start.1 = ((bf16[64,152,128]{2,1,0:T(8,128)(2,1)}), bf16[64,152,128]{2,1,0:T(8,128)(2,1)S(1)}, u32[]{:S(2)}, u32[]{:S(2)}) async-start(bf16[64,152,128]{2,1,0:T(8,128)(2,1)} %add_convert_fusion), calls=%async_computation.1 | async-start | bytes 4980736 | tf_op jit(solution)/shard_map/all_to_all | solution.py:281
  207.3 3.6 %collective-permute-start.16 = (f32[74,128]{1,0:T(8,128)S(1)}, f32[74,128]{1,0:T(8,128)S(1)}, u32[]{:S(2)}, u32[]{:S(2)}) collective-permute-start(f32[74,128]{1,0:T(8,128)S(1)} %fusion.4), channel_id=1, source_target_pairs={{0,1},{1,0},{2,3},{3,2},{4,5},{5,4},{6,7},{7,6},{8,9},{9,8},{10,11... | collective-permute-start | bytes 113672 | tf_op jit(solution)/shard_map/ppermute | solution.py:165

commit v2 on v0

v2 whole, which is shorter than its diff:
```python
import jax
import jax.numpy as jnp
import numpy as np
from jax import lax
from jax.experimental import pallas as pl
from jax.experimental.pallas import tpu as pltpu
from jax.sharding import Mesh, PartitionSpec as P

D = 16
CHIPS = ("y", "x", "z")
ALL = ("y", "x", "z", "core")
BF = jnp.bfloat16
F32 = jnp.float32
VMEM_LIMIT = 18 * 1024 * 1024

NN = (((1,), (0,)), ((), ()))
NT = (((1,), (1,)), ((), ()))
TN = (((0,), (0,)), ((), ()))


def dot(a, b, dims=NN):
    return lax.dot_general(a, b, dims, preferred_element_type=F32)


def vmem():
    return pl.BlockSpec(memory_space=pltpu.VMEM)


def params():
    return pltpu.CompilerParams(vmem_limit_bytes=VMEM_LIMIT)


def cost(flops, size):
    return pl.CostEstimate(flops=flops, bytes_accessed=size, transcendentals=0)


def swap(x):
    return jnp.concatenate([x[..., 128:], x[..., :128]], axis=-1)


def tap(mine_ref, other_ref, a, b):
    row = (3 * a + b) * 1024
    first, last = row // 144, -(-(row + 1024) // 144)
    skip = row - 144 * first

    def half(ref):
        return ref[first:last, 0:144, :].reshape((last - first) * 144, 128)[skip : skip + 1024]

    return jnp.concatenate([half(mine_ref), half(other_ref)], axis=1)


def px(ref, r0, r1, c0, c1):
    return ref[r0:r1, c0:c1, :].reshape((r1 - r0) * (c1 - c0), ref.shape[2])


def flip_kernel(f_ref, ft_ref):
    for k in range(6):
        i, j = divmod(k, 3)
        block = px(f_ref, 16 * i, 16 * i + 16, 16 * j, 16 * j + 16)
        ft_ref[:, 256 * k : 256 * k + 256] = block.T


def rows_kernel(core_ref, mine_ref, proj_ref, acc):
    for k in range(64):
        x = mine_ref[k, 144:152, :].astype(F32)
        acc[4 * k : 4 * k + 4, :128] = x[0:4]
        acc[4 * k : 4 * k + 4, 128:] = x[4:8]
    start = pl.multiple_of(128 * core_ref[0], 128)
    proj_ref[0:128] = acc[pl.ds(start, 128), :].astype(BF)
    proj_ref[128:256] = acc[pl.ds(128 - start, 128), :].astype(BF)


def halo_kernel(core_ref, f_ref, mine_ref, other_ref, n_ref, s_ref, inner_ref, outer_ref, cn_ref, cs_ref, sides, acc):
    core = core_ref[0]
    for out, a, r0, block in ((n_ref, 2, 0, 0), (s_ref, 0, 16, 3)):
        acc[...] = jnp.zeros_like(acc)
        for b in range(3):
            c = (2 - b) * D
            acc[:, c : c + 48, :] += dot(px(f_ref, r0, r0 + 16, 0, 48), tap(mine_ref, other_ref, a, b)).reshape(
                16, 48, 256
            )
        sides[0, 16 * block : 16 * block + 16] = acc[:, 0:16, :].astype(BF)
        out[...] = acc[:, 16:64, :].astype(BF)
        sides[1, 16 * block : 16 * block + 16] = acc[:, 64:80, :].astype(BF)
    for side, b, c0 in ((0, 2, 0), (1, 0, 32)):
        mid = dot(px(f_ref, 0, 32, c0, c0 + 16), tap(mine_ref, other_ref, 1, b))
        top = mid[:256] + dot(px(f_ref, 16, 32, c0, c0 + 16), tap(mine_ref, other_ref, 2, b))
        low = mid[256:] + dot(px(f_ref, 0, 16, c0, c0 + 16), tap(mine_ref, other_ref, 0, b))
        sides[side, 16:32] = top.reshape(16, 16, 256).astype(BF)
        sides[side, 32:48] = low.reshape(16, 16, 256).astype(BF)
    inner_ref[...] = sides[1 - core]
    outer_ref[...] = sides[core, 16:48]
    cn_ref[...] = sides[core, 0:16]
    cs_ref[...] = sides[core, 48:64]


def merge_kernel(core_ref, n_ref, s_ref, inner_ref, no_ref, so_ref):
    cols = pl.ds(pl.multiple_of(32 - 32 * core_ref[0], 16), 16)
    for src, dst, r in ((n_ref, no_ref, 0), (s_ref, so_ref, 48)):
        dst[...] = src[...]
        dst[:, cols, :] = (src[:, cols, :].astype(F32) + swap(inner_ref[r : r + 16]).astype(F32)).astype(BF)


def own_kernel(f_ref, mine_ref, other_ref, cot_ref, proj_ref, bias_ref, pre_ref, hg_ref):
    first = dot(px(f_ref, 0, 32, 0, 48), tap(mine_ref, other_ref, 1, 1))
    pre_ref[...] = (first + bias_ref[...]).reshape(32, 48, 256)
    for a, rows in ((0, ((0, 16), (16, 32))), (1, ((0, 32), (0, 32))), (2, ((16, 32), (0, 16)))):
        for b, cols in ((0, ((0, 32), (16, 48))), (1, ((0, 48), (0, 48))), (2, ((16, 48), (0, 32)))):
            if a == 1 and b == 1:
                continue
            (fr, pr), (fc, pc) = rows, cols
            pre_ref[pr[0] : pr[1], pc[0] : pc[1], :] += dot(
                px(f_ref, *fr, *fc), tap(mine_ref, other_ref, a, b)
            ).reshape(pr[1] - pr[0], pc[1] - pc[0], 256)
    hg_ref[...] = dot(px(cot_ref, 0, 32, 0, 48), proj_ref[...], NT).reshape(32, 48, 256)


def point_kernel(
    core_ref, own_ref, hg_ref, n_ref, s_ref, inner_ref, outer_ref, cn_ref, cs_ref,
    hid_ref, top_ref, low_ref, gi_ref, go_ref, ct_ref, cl_ref, pre_ref,
):
    core = core_ref[0]
    inner = pl.ds(pl.multiple_of(32 - 32 * core, 16), 16)
    outer = pl.ds(pl.multiple_of(32 * core, 16), 16)
    pre_ref[0:16] = own_ref[0:16] + n_ref[...].astype(F32)
    pre_ref[16:32] = own_ref[16:32] + s_ref[...].astype(F32)
    pre_ref[:, inner, :] += swap(inner_ref[16:48]).astype(F32)
    pre_ref[:, outer, :] += swap(outer_ref[...]).astype(F32)
    pre_ref[0:16, outer, :] += swap(cn_ref[...]).astype(F32)
    pre_ref[16:32, outer, :] += swap(cs_ref[...]).astype(F32)
    for g_ref, base in ((top_ref, 0), (low_ref, 16)):

        @pl.loop(0, 8)
        def _(k):
            rows = pl.ds(base + 2 * k, 2)
            pre = pre_ref[rows]
            s = jax.nn.sigmoid(pre)
            hid_ref[rows] = (pre * s).astype(BF)
            g_ref[pl.ds(2 * k, 2)] = (hg_ref[rows] * s * (1.0 + pre * (1.0 - s))).astype(BF)

    for g_ref, c_ref, base in ((top_ref, ct_ref, 0), (low_ref, cl_ref, 16)):
        gi_ref[base : base + 16] = g_ref[:, inner, :]
        edge = g_ref[:, outer, :]
        go_ref[base : base + 16] = edge
        c_ref[...] = edge


def proj_kernel(hid_ref, cot_ref, proj_ref, top_ref, low_ref, out_ref, pw_ref, bias_ref):
    hidden = px(hid_ref, 0, 32, 0, 48)
    cot = px(cot_ref, 0, 32, 0, 48)
    out_ref[...] = dot(hidden, proj_ref[...]).astype(BF).reshape(32, 48, 256)
    pw_ref[...] = dot(hidden, cot, TN)
    total = px(top_ref, 0, 16, 0, 48).astype(F32) + px(low_ref, 0, 16, 0, 48).astype(F32)
    bias_ref[...] = jnp.sum(total, axis=0, keepdims=True)


def edge_kernel(core_ref, top_ref, low_ref, edge_ref):
    cols = pl.ds(pl.multiple_of(32 - 32 * core_ref[0], 16), 16)
    edge_ref[0:16] = top_ref[:, cols, :]
    edge_ref[16:32] = low_ref[:, cols, :]


def wgrad_kernel(
    core_ref, ft_ref, gt_ref, gl_ref, ht_ref, hl_ref, hi_ref, ho_ref, ct_ref, cl_ref, edge_ref, em_ref, eo_ref,
    g_ref, mine_ref, other_ref,
):
    core = core_ref[0]
    inner = pl.ds(pl.multiple_of(64 - 64 * core, 16), 16)
    outer = pl.ds(pl.multiple_of(64 * core, 16), 16)
    g_ref[0:16, 16:64, :] = ht_ref[...]
    g_ref[16:32, 16:64, :] = gt_ref[...]
    g_ref[32:48, 16:64, :] = gl_ref[...]
    g_ref[48:64, 16:64, :] = hl_ref[...]
    g_ref[0:16, inner, :] = swap(edge_ref[0:16])
    g_ref[16:48, inner, :] = swap(hi_ref[...])
    g_ref[48:64, inner, :] = swap(edge_ref[16:32])
    g_ref[0:16, outer, :] = swap(ct_ref[...])
    g_ref[16:48, outer, :] = swap(ho_ref[...])
    g_ref[48:64, outer, :] = swap(cl_ref[...])
    wgrad_part(ft_ref, g_ref, em_ref, eo_ref, mine_ref, other_ref, 0)


def wgrad_part(ft_ref, g_ref, em_ref, eo_ref, mine_ref, other_ref, chip0):
    mine_ref[:, 144:152, :] = em_ref[chip0 : chip0 + 32]
    other_ref[:, 144:152, :] = eo_ref[chip0 : chip0 + 32]
    begin, end = 144 * chip0, 144 * chip0 + 4608
    for t in range(9):
        first, last = max(begin, 1024 * t), min(end, 1024 * t + 1024)
        if first >= last:
            continue
        row, col = (2 - t // 3) * D, (2 - t % 3) * D
        blocks = [
            px(g_ref, row + 16 * i, row + 16 * i + 16, col + 16 * j, col + 16 * j + 16)
            for i in range(2)
            for j in range(3)
        ]
        res = dot(ft_ref[first - 1024 * t : last - 1024 * t], jnp.concatenate(blocks, axis=0)).astype(BF)
        at = first
        while at < last:
            chip, r = divmod(at, 144)
            size = min(144 - r, last - at)
            mine_ref[chip - chip0, r : r + size, :] = res[at - first : at - first + size, :128]
            other_ref[chip - chip0, r : r + size, :] = res[at - first : at - first + size, 128:]
            at += size


def wgrad_rest_kernel(ft_ref, g_ref, em_ref, eo_ref, mine_ref, other_ref):
    wgrad_part(ft_ref, g_ref, em_ref, eo_ref, mine_ref, other_ref, 32)


def add_kernel(m_ref, r_ref, out_ref):
    @pl.loop(0, 16)
    def _(k):
        pair = pl.ds(2 * k, 2)
        out_ref[pair] = (m_ref[pair].astype(F32) + r_ref[pair].astype(F32)).astype(BF)


def add_rest_kernel(first_ref, m_ref, r_ref, out_ref):
    @pl.loop(0, 16)
    def _(k):
        pair = pl.ds(2 * k, 2)
        out_ref[pair] = first_ref[pair]
        out_ref[pl.ds(32 + 2 * k, 2)] = (m_ref[pair].astype(F32) + r_ref[pair].astype(F32)).astype(BF)


def fgrad_kernel(g_ref, mine_ref, other_ref, out_ref):
    @pl.loop(0, 4)
    def _(k):
        acc = None
        for t in range(9):
            row, col = (2 - t // 3) * D, (2 - t % 3) * D
            win = g_ref[pl.ds(row + 8 * k, 8), col : col + 48, :].reshape(384, 256)
            term = dot(win, tap(mine_ref, other_ref, t // 3, t % 3), NT)
            acc = term if acc is None else acc + term
        out_ref[pl.ds(8 * k, 8)] = acc.astype(BF).reshape(8, 48, 1024)


def body(features, conv_weight, conv_bias, proj_weight, cotangent):
    core = lax.axis_index("core")
    is0 = core == 0
    core_s = core.astype(jnp.int32).reshape(1)
    smem = pl.BlockSpec(memory_space=pltpu.SMEM)

    def send(x, dr, dc):
        perm = []
        for i in range(128):
            r, c = i // 8 + dr, i % 8 + dc[i % 2]
            if 0 <= r < 16 and 0 <= c < 8:
                perm.append((i, r * 8 + c))
        return lax.ppermute(x, ALL, perm)

    def array(shape, dtype=BF):
        return jax.ShapeDtypeStruct(shape, dtype)

    def call(kernel, name, outs, args, flops, size, scratch=()):
        specs = [smem if a is core_s else vmem() for a in args]
        return pl.pallas_call(
            kernel,
            out_shape=tuple(outs),
            in_specs=specs,
            out_specs=(vmem(),) * len(outs),
            scratch_shapes=list(scratch),
            compiler_params=params(),
            cost_estimate=cost(int(flops), int(size)),
            name=name,
        )(*args)

    SAME, INNER, OUTER = (0, 0), (1, -1), (-1, 1)

    low, high = conv_weight[:, :128], conv_weight[:, 128:]
    own_proj = jnp.concatenate([proj_weight[:, :128], proj_weight[:, 128:]], axis=0)
    got = send(jnp.concatenate([jnp.where(is0, high, low), own_proj], axis=0), 0, INNER)
    keep = jnp.concatenate([jnp.where(is0, low, high), own_proj], axis=0)
    even, odd = jnp.where(is0, keep, got), jnp.where(is0, got, keep)
    chunk = jnp.concatenate([even[:72], odd[:72], even[72:74], odd[72:74], even[74:76], odd[74:76]], axis=0)
    mine = lax.all_to_all(jnp.broadcast_to(chunk[None], (64, 152, 128)), CHIPS, 0, 0)
    (ft,) = call(flip_kernel, "flip", [array((1024, 1536))], [features], 1e6, 6e6)
    mine, ft = lax.optimization_barrier((mine, ft))
    other = send(mine, 0, INNER)
    (proj,) = call(rows_kernel, "rows", [array((256, 256))], [core_s, mine], 1e6, 1e6, [pltpu.VMEM((256, 256), F32)])
    other, proj = lax.optimization_barrier((other, proj))
    bias = jnp.where(is0, conv_bias, jnp.concatenate([conv_bias[128:], conv_bias[:128]])).reshape(1, 256)

    tile, strip, small, side = (32, 48, 256), (16, 48, 256), (16, 16, 256), (32, 16, 256)
    n, s, inner, outer, cn, cs = call(
        halo_kernel,
        "halo",
        [array(strip), array(strip), array((64, 16, 256)), array(side), array(small), array(small)],
        [core_s, features, mine, other],
        3.5e9,
        9e6,
        [pltpu.VMEM((2, 64, 16, 256), BF), pltpu.VMEM((16, 80, 256), F32)],
    )
    inner = send(inner, 0, INNER)
    n, s = call(merge_kernel, "merge", [array(strip), array(strip)], [core_s, n, s, inner], 1e6, 2e6)
    from_s = send(n, -1, SAME)
    from_n = send(s, 1, SAME)
    outer = send(outer, 0, OUTER)
    corner_s = send(cn, -1, OUTER)
    corner_n = send(cs, 1, OUTER)

    own, hg = call(
        own_kernel,
        "own",
        [array(tile, F32), array(tile, F32)],
        [features, mine, other, cotangent, proj, bias],
        4e9,
        12e6,
    )
    hidden, g_top, g_low, gi, go, ct, cl = call(
        point_kernel,
        "point",
        [array(tile), array(strip), array(strip), array(side), array(side), array(small), array(small)],
        [core_s, own, hg, from_n, from_s, inner, outer, corner_n, corner_s],
        1e8,
        6e6,
        [pltpu.VMEM(tile, F32)],
    )

    h_top = send(g_low, 1, SAME)
    h_low = send(g_top, -1, SAME)
    h_outer = send(go, 0, OUTER)
    c_top = send(cl, 1, OUTER)
    c_low = send(ct, -1, OUTER)
    h_inner = send(gi, 0, INNER)

    projected, pw, bias_term = call(
        proj_kernel,
        "proj",
        [array(tile), array((256, 256), F32), array((1, 256), F32)],
        [hidden, cotangent, proj, g_top, g_low],
        4e8,
        4e6,
    )
    pw = jnp.where(is0, pw, jnp.concatenate([pw[128:], pw[:128]], axis=0)).astype(BF)
    bias_term = jnp.where(is0, bias_term, jnp.concatenate([bias_term[:, 128:], bias_term[:, :128]], axis=1))
    bias_rows = jnp.pad(bias_term.astype(BF).reshape(64, 1, 4), ((0, 0), (0, 3), (0, 124)))

    def extra(p):
        return jnp.concatenate([p.reshape(64, 4, 128), bias_rows], axis=1)

    e_mine = extra(jnp.where(is0, pw[:, :128], pw[:, 128:]))
    e_other = extra(jnp.where(is0, pw[:, 128:], pw[:, :128]))

    h_top, h_low, c_top, c_low, h_outer = lax.optimization_barrier((h_top, h_low, c_top, c_low, h_outer))
    (edge,) = call(edge_kernel, "edge", [array(side)], [core_s, h_top, h_low], 1e6, 1e6)
    edge = send(edge, 0, INNER)
    half = array((32, 152, 128))
    g, m1, o1 = call(
        wgrad_kernel,
        "wgrad",
        [array((64, 80, 256)), half, half],
        [core_s, ft, g_top, g_low, h_top, h_low, h_inner, h_outer, c_top, c_low, edge, e_mine, e_other],
        3.6e9,
        8e6,
    )
    r1 = send(o1, 0, INNER)
    m2, o2 = call(wgrad_rest_kernel, "wgrad2", [half, half], [ft, g, e_mine, e_other], 3.6e9, 8e6)
    r2 = send(o2, 0, INNER)
    (t1,) = call(add_kernel, "add", [half], [m1, r1], 1e6, 4e6)
    (total,) = call(add_rest_kernel, "add2", [array((64, 152, 128))], [t1, m2, r2], 1e6, 7e6)
    pieces = lax.all_to_all(total, CHIPS, 0, 0)

    (features_grad,) = call(fgrad_kernel, "fgrad", [array((32, 48, 1024))], [g, mine, other], 7.2e9, 12e6)

    sums = jnp.sum(pieces.astype(F32), axis=0)
    lo, hi = jnp.concatenate([sums[:72], sums[144:146]], 0), jnp.concatenate([sums[72:144], sums[146:148]], 0)
    keep = jnp.where(is0, lo, hi)
    got = send(jnp.where(is0, hi, lo), 0, INNER)
    both = jnp.concatenate([jnp.where(is0, keep, got), jnp.where(is0, got, keep)], axis=1)
    bias_grad = jnp.where(is0, sums[148, 0:2], sums[148, 2:4])
    return projected, features_grad, both[:72], both[72:74], bias_grad


def solution(mesh):
    fine = Mesh(mesh.devices.reshape(4, 4, 4, 2), ALL)
    tile = P(("y", "x"), ("z", "core"), None)
    rows = P(ALL, None)
    return jax.shard_map(
        body,
        mesh=fine,
        in_specs=(tile, rows, P(), rows, tile),
        out_specs=(tile, tile, rows, rows, P(ALL)),
        check_vma=False,
    )
```

time: 541 us -> 183 us (0.34)
  waiting for transfers between devices: 259 us -> 66.3 us
  blocking collectives: 126 us -> 0 us
  matrix products: 88.3 us -> 0 us
  starting transfers between devices: 21.4 us -> 59.4 us
  Pallas kernels: 0 us -> 32.9 us
  between operations: 14.1 us -> 1 us
  other arithmetic: 16.2 us -> 6.49 us
    reduce_scatter x1 -> x0, waiting for transfers between devices: 163 us -> none  [body(): lax.psum_scatter(weight_term, ('row', 'col'), scatter_dimension=0, tiled=...]
    dot_general x30 -> x0, matrix products: 88.3 us -> none  [the longest x9 50.8 us: body(): lax.dot_general(back, conv_full[tap * in_channels:(tap + 1) * in_channels...]
    unnamed x1 -> x0, blocking collectives: 67.1 us -> none
    unnamed x4 -> x0, waiting for transfers between devices: 59.2 us -> none
    all_gather x1 -> x0, blocking collectives: 58.4 us -> none  [body(): lax.all_gather(proj_weight, ('row', 'col'), axis=0, tiled=True)]
    all_to_all x0 -> x2, waiting for transfers between devices: none -> 47.1 us  [the longest x1 27.9 us: body(): lax.all_to_all(jnp.broadcast_to(chunk[None], (64, 152, 128)), CHIPS, 0, 0)]
    pallas_call x0 -> x13, Pallas kernels: none -> 32.9 us  [call(): pl.pallas_call(kernel, out_shape=tuple(outs), in_specs=specs, out_specs=(...]
    all_to_all x0 -> x2, starting transfers between devices: none -> 25.1 us  [the longest x1 13.9 us: body(): pieces = lax.all_to_all(total, CHIPS, 0, 0)]
  transfers between devices with their start and end apart: 11 -> 20, of which waited for: 4 -> 10; matrix products, arithmetic and copies ran while one was open for 15% -> 2% of each run, Pallas kernels for 0% -> 12%
where the time goes in v2:
time: 183 us; the launch traced here: 182 us
  waiting for transfers between devices  66.3 us (36%)
  starting transfers between devices  59.4 us (32%)
  Pallas kernels  32.9 us (18%)
  local copies, waits for them, and re-layouts  16.2 us (9%)
  other arithmetic  6.49 us (4%)
    ppermute x18, starting transfers between devices, send(): return lax.ppermute(x, ALL, perm)  34.3 us
    pallas_call x13, Pallas kernels, call(): pl.pallas_call(kernel, out_shape=tuple(outs), in_specs=specs, out_specs=(...  32.9 us
    all_to_all x1, waiting for transfers between devices, body(): lax.all_to_all(jnp.broadcast_to(chunk[None], (64, 152, 128)), CHIPS, 0, 0)  27.9 us
    ppermute x18, waiting for transfers between devices, send(): return lax.ppermute(x, ALL, perm)  19.2 us
    all_to_all x1, waiting for transfers between devices, body(): pieces = lax.all_to_all(total, CHIPS, 0, 0)  19.2 us
    all_to_all x1, starting transfers between devices, body(): pieces = lax.all_to_all(total, CHIPS, 0, 0)  13.9 us
    unnamed x30, local copies, waits for them, and re-layouts  12.2 us
    all_to_all x1, starting transfers between devices, body(): lax.all_to_all(jnp.broadcast_to(chunk[None], (64, 152, 128)), CHIPS, 0, 0)  11.2 us
  transfers between devices with their start and end apart: 20, of which 10 were waited for; matrix products, arithmetic and copies ran while one was open for 2% of the time, Pallas kernels for 12%

profile of v2, /device:TPU:1, one launch (start us, length us, event | category | flops | bytes accessed | tf_op | source)
XLA Modules:
  0.0 182.3 jit_solution(14598698808832616118)
XLA Ops:
  0.6 0.7 fusion.17
  1.3 0.8 broadcast_select_fusion.7
  2.1 1.5 collective-permute-start
  3.6 0.8 collective-permute-done
  4.5 1.8 broadcast_in_dim.2
  6.3 11.2 %all-to-all-start = ((bf16[64,152,128]{2,1,0:T(8,128)(2,1)}), bf16[64,152,128]{2,1,0:T(8,128)(2,1)S(1)}, u32[]{:S(2)}, u32[]{:S(2)}) async-start(bf16[64,152,128]{2,1,0:T(8,128)(2,1)} %broadcast_in_dim.2), calls=%async_computation | async-start | bytes 4980736 | tf_op jit(solution)/shard_map/all_to_all | solution.py:276
  17.5 1.9 %copy-done.1 = bf16[32,48,1024]{2,1,0:T(8,128)(2,1)S(1)} copy-done((bf16[32,48,1024]{2,1,0:T(8,128)(2,1)S(1)}, bf16[32,48,1024]{2,1,0:T(8,128)(2,1)}, u32[]{:S(2)}) %copy-start.1) | copy-done | bytes 3145752
  19.4 0.9 flip.1.ft_ref
  20.3 1.7 copy-done.4
  22.0 27.9 %all-to-all-done.mine_ref = bf16[64,152,128]{2,1,0:T(8,128)(2,1)S(1)} async-done(((bf16[64,152,128]{2,1,0:T(8,128)(2,1)}), bf16[64,152,128]{2,1,0:T(8,128)(2,1)S(1)}, u32[]{:S(2)}, u32[]{:S(2)}) %all-to-all-start) | async-done | bytes 2490400 | tf_op jit(solution)/shard_map/all_to_all | solution.py:276
  49.8 2.3 %collective-permute-start.1 = (bf16[64,152,128]{2,1,0:T(8,128)(2,1)S(1)}, bf16[64,152,128]{2,1,0:T(8,128)(2,1)S(1)}, u32[]{:S(2)}, u32[]{:S(2)}) collective-permute-start(bf16[64,152,128]{2,1,0:T(8,128)(2,1)S(1)} %all-to-all-done.mine_ref), channel_id=1, source_target_pairs={{0,1},{1,0},{2,3},{3,2},{4,5},{5,4},{6,7},{7,6},{8,9},{9,8},{10,11... | collective-permute-start | bytes 7471112 | tf_op jit(solution)/shard_map/ppermute | solution.py:250
  52.2 4.3 %collective-permute-done.1.other_ref = bf16[64,152,128]{2,1,0:T(8,128)(2,1)S(1)} collective-permute-done((bf16[64,152,128]{2,1,0:T(8,128)(2,1)S(1)}, bf16[64,152,128]{2,1,0:T(8,128)(2,1)S(1)}, u32[]{:S(2)}, u32[]{:S(2)}) %collective-permute-start.1) | collective-permute-done | bytes 2490400 | tf_op jit(solution)/shard_map/ppermute | solution.py:250
  56.5 1.9 %copy-done.2 = bf16[32,48,1024]{2,1,0:T(8,128)(2,1)S(1)} copy-done((bf16[32,48,1024]{2,1,0:T(8,128)(2,1)S(1)}, bf16[32,48,1024]{2,1,0:T(8,128)(2,1)}, u32[]{:S(2)}) %copy-start.2) | copy-done | bytes 3145752
  58.4 3.8 %halo.1 = (bf16[16,48,256]{2,1,0:T(8,128)(2,1)S(1)}, bf16[16,48,256]{2,1,0:T(8,128)(2,1)S(1)}, bf16[64,16,256]{2,1,0:T(8,128)(2,1)S(1)}, bf16[32,16,256]{2,1,0:T...) custom-call(s32[1]{0:T(128)} %bitcast.core_ref, ...), custom_call_target="tpu_custom_call" | custom-call | flops 3500000000 | bytes 9000000 | tf_op jit(solution)/shard_map/halo/pallas_call | solution.py:257
  62.6 1.5 collective-permute-done.2.inner_ref
  64.3 2.5 %collective-permute-start.3 = (bf16[16,48,256]{2,1,0:T(8,128)(2,1)S(1)}, bf16[16,48,256]{2,1,0:T(8,128)(2,1)S(1)}, u32[]{:S(2)}, u32[]{:S(2)}) collective-permute-start(bf16[16,48,256]{2,1,0:T(8,128)(2,1)S(1)} %get-tuple-element.47), channel_id=1, source_target_pairs={{0,8},{1,9},{2,10},{3,11},{4,12},{5,13},{6,14},{7,15},{8,16},{9,17... | collective-permute-start | bytes 1179656 | tf_op jit(solution)/shard_map/ppermute | solution.py:250
  66.8 1.3 collective-permute-start.4
  68.1 3.5 %collective-permute-start.5 = (bf16[32,16,256]{2,1,0:T(8,128)(2,1)S(1)}, bf16[32,16,256]{2,1,0:T(8,128)(2,1)S(1)}, u32[]{:S(2)}, u32[]{:S(2)}) collective-permute-start(bf16[32,16,256]{2,1,0:T(8,128)(2,1)S(1)} %get-tuple-element.49), channel_id=1, source_target_pairs={{1,2},{2,1},{3,4},{4,3},{5,6},{6,5},{9,10},{10,9},{11,12},{12,11},... | collective-permute-start | bytes 786440 | tf_op jit(solution)/shard_map/ppermute | solution.py:250
  71.7 4.0 %collective-permute-start.6 = (bf16[16,16,256]{2,1,0:T(8,128)(2,1)S(1)}, bf16[16,16,256]{2,1,0:T(8,128)(2,1)S(1)}, u32[]{:S(2)}, u32[]{:S(2)}) collective-permute-start(bf16[16,16,256]{2,1,0:T(8,128)(2,1)S(1)} %get-tuple-element.50), channel_id=1, source_target_pairs={{1,10},{2,9},{3,12},{4,11},{5,14},{6,13},{9,18},{10,17},{11,20},{1... | collective-permute-start | bytes 393224 | tf_op jit(solution)/shard_map/ppermute | solution.py:250
  75.7 1.3 collective-permute-start.7
  77.0 4.2 %own.1 = (f32[32,48,256]{2,1,0:T(8,128)S(1)}, f32[32,48,256]{2,1,0:T(8,128)S(1)}) custom-call(bf16[32,48,1024]{2,1,0:T(8,128)(2,1)S(1)} %copy-done.3, bf16[64,152,128]{2,1,0:T(8,128)(2,1)S(1)} %all-to-all-done.mine_ref, bf16[64,152,128]{2,1,0:T(8,128)(2,1)S(1)} %collective-permute-done.1.other_ref, bf16[32,48,256]{2,1,0:T(8,128)(2,1)S(1)} %copy-done.6, ...), custom_call_target="tpu_custom_call" | custom-call | flops 4000000000 | bytes 12000000 | tf_op jit(solution)/shard_map/own/pallas_call | solution.py:257
  81.2 2.0 %collective-permute-done.7.cs_ref = bf16[16,16,256]{2,1,0:T(8,128)(2,1)S(1)} collective-permute-done((bf16[16,16,256]{2,1,0:T(8,128)(2,1)S(1)}, bf16[16,16,256]{2,1,0:T(8,128)(2,1)S(1)}, u32[]{:S(2)}, u32[]{:S(2)}) %collective-permute-start.7) | collective-permute-done | bytes 131104 | tf_op jit(solution)/shard_map/ppermute | solution.py:250
  83.2 1.8 point.1
  84.9 4.3 %collective-permute-start.8 = (bf16[16,48,256]{2,1,0:T(8,128)(2,1)S(1)}, bf16[16,48,256]{2,1,0:T(8,128)(2,1)}, u32[]{:S(2)}, u32[]{:S(2)}) collective-permute-start(bf16[16,48,256]{2,1,0:T(8,128)(2,1)S(1)} %get-tuple-element.54.low_ref.gl_ref), channel_id=1, source_target_pairs={{0,8},{1,9},{2,10},{3,11},{4,12},{5,13},{6,14},{7,15},{8,16},{9,17... | collective-permute-start | bytes 1179656 | tf_op jit(solution)/shard_map/ppermute | solution.py:250
  89.2 1.3 collective-permute-start.9
  90.5 1.5 proj.1
  92.0 0.7 fusion.10
  92.6 2.2 %collective-permute-start.12 = (bf16[32,16,256]{2,1,0:T(8,128)(2,1)}, bf16[32,16,256]{2,1,0:T(8,128)(2,1)}, u32[]{:S(2)}, u32[]{:S(2)}) collective-permute-start(bf16[32,16,256]{2,1,0:T(8,128)(2,1)} %get-tuple-element.59), channel_id=1, source_target_pairs={{1,2},{2,1},{3,4},{4,3},{5,6},{6,5},{9,10},{10,9},{11,12},{12,11},... | collective-permute-start | bytes 786440 | tf_op jit(solution)/shard_map/ppermute | solution.py:250
  94.9 0.7 reshape.33
  95.6 5.1 %collective-permute-start.10 = (bf16[16,16,256]{2,1,0:T(8,128)(2,1)}, bf16[16,16,256]{2,1,0:T(8,128)(2,1)S(1)}, u32[]{:S(2)}, u32[]{:S(2)}) collective-permute-start(bf16[16,16,256]{2,1,0:T(8,128)(2,1)} %copy-done.11), channel_id=1, source_target_pairs={{1,10},{2,9},{3,12},{4,11},{5,14},{6,13},{9,18},{10,17},{11,20},{1... | collective-permute-start | bytes 393224 | tf_op jit(solution)/shard_map/ppermute | solution.py:250
  100.8 1.3 collective-permute-start.11
  102.1 0.9 fusion
  103.1 7.4 %collective-permute-done.11.cl_ref = bf16[16,16,256]{2,1,0:T(8,128)(2,1)S(1)} collective-permute-done((bf16[16,16,256]{2,1,0:T(8,128)(2,1)}, bf16[16,16,256]{2,1,0:T(8,128)(2,1)S(1)}, u32[]{:S(2)}, u32[]{:S(2)}) %collective-permute-start.11) | collective-permute-done | bytes 131104 | tf_op jit(solution)/shard_map/ppermute | solution.py:250
  110.5 1.1 edge.1
  111.9 0.9 fusion.3
  113.4 1.9 %copy-done.5 = bf16[1024,1536]{1,0:T(8,128)(2,1)S(1)} copy-done((bf16[1024,1536]{1,0:T(8,128)(2,1)S(1)}, bf16[1024,1536]{1,0:T(8,128)(2,1)}, u32[]{:S(2)}) %copy-start.5) | copy-done | bytes 3145752
  115.3 5.2 %wgrad.1 = (bf16[64,80,256]{2,1,0:T(8,128)(2,1)S(1)}, bf16[32,152,128]{2,1,0:T(8,128)(2,1)S(1)}, bf16[32,152,128]{2,1,0:T(8,128)(2,1)S(1)}) custom-call(s32[1]{0:T(128)} %bitcast.core_ref, bf16[1024,1536]{1,0:T(8,128)(2,1)S(1)} %copy-done.5, bf16[16,48,256]{2,1,0:T(8,128)(2,1)S(1)} %get-tuple-element.53.top_ref.gt_ref, ...), custom_call_target="tpu_custom_call" | custom-call | flops 3600000000 | bytes 8000000 | tf_op jit(solution)/shard_map/wgrad/pallas_call | solution.py:257
  120.8 3.8 %wgrad2.1 = (bf16[32,152,128]{2,1,0:T(8,128)(2,1)S(1)}, bf16[32,152,128]{2,1,0:T(8,128)(2,1)S(1)}) custom-call(bf16[1024,1536]{1,0:T(8,128)(2,1)S(1)} %copy-done.5, bf16[64,80,256]{2,1,0:T(8,128)(2,1)S(1)} %get-tuple-element.68.g_ref, bf16[64,8,128]{2,1,0:T(8,128)(2,1)S(1)} %get-tuple-element.88.em_ref, bf16[64,8,128]{2,1,0:T(8,128)(2,1)S(1)} %get-tuple-element.87.eo_ref), custom_call_target="tpu_custom_call" | custom-call | flops 3600000000 | bytes 8000000 | tf_op jit(solution)/shard_map/wgrad2/pallas_call | solution.py:257
  125.5 2.2 %collective-permute-done.16.r_ref = bf16[32,152,128]{2,1,0:T(8,128)(2,1)S(1)} collective-permute-done((bf16[32,152,128]{2,1,0:T(8,128)(2,1)S(1)}, bf16[32,152,128]{2,1,0:T(8,128)(2,1)S(1)}, u32[]{:S(2)}, u32[]{:S(2)}) %collective-permute-start.16) | collective-permute-done | bytes 1245216 | tf_op jit(solution)/shard_map/ppermute | solution.py:250
  128.1 1.4 copy-done
  129.6 13.9 %all-to-all-start.1 = ((bf16[64,152,128]{2,1,0:T(8,128)(2,1)}), bf16[64,152,128]{2,1,0:T(8,128)(2,1)}, u32[]{:S(2)}, u32[]{:S(2)}) async-start(bf16[64,152,128]{2,1,0:T(8,128)(2,1)} %copy-done), calls=%async_computation.1 | async-start | bytes 4980736 | tf_op jit(solution)/shard_map/all_to_all | solution.py:362
  143.5 1.7 copy-done.8
  145.2 1.7 copy-done.13
  146.9 9.8 %fgrad.1 = bf16[32,48,1024]{2,1,0:T(8,128)(2,1)} custom-call(bf16[64,80,256]{2,1,0:T(8,128)(2,1)S(1)} %copy-done.13, bf16[64,152,128]{2,1,0:T(8,128)(2,1)S(1)} %all-to-all-done.mine_ref, bf16[64,152,128]{2,1,0:T(8,128)(2,1)S(1)} %copy-done.8), custom_call_target="tpu_custom_call" | custom-call | flops 7200000000 | bytes 12000000 | tf_op jit(solution)/shard_map/fgrad/pallas_call | solution.py:257
  156.7 19.2 %all-to-all-done.1 = bf16[64,152,128]{2,1,0:T(8,128)(2,1)} async-done(((bf16[64,152,128]{2,1,0:T(8,128)(2,1)}), bf16[64,152,128]{2,1,0:T(8,128)(2,1)}, u32[]{:S(2)}, u32[]{:S(2)}) %all-to-all-start.1) | async-done | bytes 2490400 | tf_op jit(solution)/shard_map/all_to_all | solution.py:362
  175.9 2.1 %convert_reduce_fusion = f32[152,128]{1,0:T(8,128)S(1)} fusion(bf16[64,152,128]{2,1,0:T(8,128)(2,1)} %all-to-all-done.1), kind=kLoop, calls=%fused_computation | loop fusion | flops 2470912 | bytes 2568192 | tf_op jit(solution)/shard_map/reduce_sum | solution.py:366
  178.0 2.2 %collective-permute-start.17 = (f32[74,128]{1,0:T(8,128)S(1)}, f32[74,128]{1,0:T(8,128)S(1)}, u32[]{:S(2)}, u32[]{:S(2)}) collective-permute-start(f32[74,128]{1,0:T(8,128)S(1)} %fusion.5), channel_id=1, source_target_pairs={{0,1},{1,0},{2,3},{3,2},{4,5},{5,4},{6,7},{7,6},{8,9},{9,8},{10,11... | collective-permute-start | bytes 113672 | tf_op jit(solution)/shard_map/ppermute | solution.py:250
  181.7 0.6 fusion.4
  (61 shorter events, 4.7 us)
Async XLA Ops:
  2.1 2.3 %collective-permute-start = (bf16[76,128]{1,0:T(8,128)(2,1)S(1)}, bf16[76,128]{1,0:T(8,128)(2,1)S(1)}, u32[]{:S(2)}, u32[]{:S(2)}) collective-permute-start(bf16[76,128]{1,0:T(8,128)(2,1)S(1)} %pad_maximum_fusion.2), channel_id=1, source_target_pairs={{0,1},{1,0},{2,3},{3,2},{4,5},{5,4},{6,7},{7,6},{8,9},{9,8},{10,11... | collective-permute-start | bytes 58376 | tf_op jit(solution)/shard_map/ppermute | solution.py:250
  6.3 43.5 %all-to-all-start = ((bf16[64,152,128]{2,1,0:T(8,128)(2,1)}), bf16[64,152,128]{2,1,0:T(8,128)(2,1)S(1)}, u32[]{:S(2)}, u32[]{:S(2)}) async-start(bf16[64,152,128]{2,1,0:T(8,128)(2,1)} %broadcast_in_dim.2), calls=%async_computation | async-start | bytes 4980736 | tf_op jit(solution)/shard_map/all_to_all | solution.py:276
  17.5 1.9 %copy-start.1 = (bf16[32,48,1024]{2,1,0:T(8,128)(2,1)S(1)}, bf16[32,48,1024]{2,1,0:T(8,128)(2,1)}, u32[]{:S(2)}) copy-start(bf16[32,48,1024]{2,1,0:T(8,128)(2,1)} %f_ref.5) | copy-start | bytes 9437188
  20.3 1.7 copy-start.4
  49.8 6.7 %collective-permute-start.1 = (bf16[64,152,128]{2,1,0:T(8,128)(2,1)S(1)}, bf16[64,152,128]{2,1,0:T(8,128)(2,1)S(1)}, u32[]{:S(2)}, u32[]{:S(2)}) collective-permute-start(bf16[64,152,128]{2,1,0:T(8,128)(2,1)S(1)} %all-to-all-done.mine_ref), channel_id=1, source_target_pairs={{0,1},{1,0},{2,3},{3,2},{4,5},{5,4},{6,7},{7,6},{8,9},{9,8},{10,11... | collective-permute-start | bytes 7471112 | tf_op jit(solution)/shard_map/ppermute | solution.py:250
  56.5 1.9 %copy-start.2 = (bf16[32,48,1024]{2,1,0:T(8,128)(2,1)S(1)}, bf16[32,48,1024]{2,1,0:T(8,128)(2,1)}, u32[]{:S(2)}) copy-start(bf16[32,48,1024]{2,1,0:T(8,128)(2,1)} %f_ref.5) | copy-start | bytes 9437188
  58.4 18.6 %copy-start.7 = (bf16[64,152,128]{2,1,0:T(8,128)(2,1)}, bf16[64,152,128]{2,1,0:T(8,128)(2,1)S(1)}, u32[]{:S(2)}) copy-start(bf16[64,152,128]{2,1,0:T(8,128)(2,1)S(1)} %collective-permute-done.1.other_ref) | copy-start | bytes 7471108
  58.4 4.2 %copy-start.14 = (f32[256]{0:T(256)S(1)}, f32[256]{0:T(256)}, u32[]{:S(2)}) copy-start(f32[256]{0:T(256)} %param.7) | copy-start | bytes 3076
  58.4 18.6 %copy-start.3 = (bf16[32,48,1024]{2,1,0:T(8,128)(2,1)S(1)}, bf16[32,48,1024]{2,1,0:T(8,128)(2,1)}, u32[]{:S(2)}) copy-start(bf16[32,48,1024]{2,1,0:T(8,128)(2,1)} %f_ref.5) | copy-start | bytes 9437188
  58.4 18.6 %copy-start.6 = (bf16[32,48,256]{2,1,0:T(8,128)(2,1)S(1)}, bf16[32,48,256]{2,1,0:T(8,128)(2,1)}, u32[]{:S(2)}) copy-start(bf16[32,48,256]{2,1,0:T(8,128)(2,1)} %cot_ref.3) | copy-start | bytes 2359300
  62.2 2.0 %collective-permute-start.2 = (bf16[64,16,256]{2,1,0:T(8,128)(2,1)S(1)}, bf16[64,16,256]{2,1,0:T(8,128)(2,1)S(1)}, u32[]{:S(2)}, u32[]{:S(2)}) collective-permute-start(bf16[64,16,256]{2,1,0:T(8,128)(2,1)S(1)} %get-tuple-element.46), channel_id=1, source_target_pairs={{0,1},{1,0},{2,3},{3,2},{4,5},{5,4},{6,7},{7,6},{8,9},{9,8},{10,11... | collective-permute-start | bytes 1572872 | tf_op jit(solution)/shard_map/ppermute | solution.py:250
  64.3 18.9 %collective-permute-start.3 = (bf16[16,48,256]{2,1,0:T(8,128)(2,1)S(1)}, bf16[16,48,256]{2,1,0:T(8,128)(2,1)S(1)}, u32[]{:S(2)}, u32[]{:S(2)}) collective-permute-start(bf16[16,48,256]{2,1,0:T(8,128)(2,1)S(1)} %get-tuple-element.47), channel_id=1, source_target_pairs={{0,8},{1,9},{2,10},{3,11},{4,12},{5,13},{6,14},{7,15},{8,16},{9,17... | collective-permute-start | bytes 1179656 | tf_op jit(solution)/shard_map/ppermute | solution.py:250
  66.8 16.3 %collective-permute-start.4 = (bf16[16,48,256]{2,1,0:T(8,128)(2,1)S(1)}, bf16[16,48,256]{2,1,0:T(8,128)(2,1)S(1)}, u32[]{:S(2)}, u32[]{:S(2)}) collective-permute-start(bf16[16,48,256]{2,1,0:T(8,128)(2,1)S(1)} %get-tuple-element.48), channel_id=1, source_target_pairs={{8,0},{9,1},{10,2},{11,3},{12,4},{13,5},{14,6},{15,7},{16,8},{17,9... | collective-permute-start | bytes 1179656 | tf_op jit(solution)/shard_map/ppermute | solution.py:250
  68.1 15.0 %collective-permute-start.5 = (bf16[32,16,256]{2,1,0:T(8,128)(2,1)S(1)}, bf16[32,16,256]{2,1,0:T(8,128)(2,1)S(1)}, u32[]{:S(2)}, u32[]{:S(2)}) collective-permute-start(bf16[32,16,256]{2,1,0:T(8,128)(2,1)S(1)} %get-tuple-element.49), channel_id=1, source_target_pairs={{1,2},{2,1},{3,4},{4,3},{5,6},{6,5},{9,10},{10,9},{11,12},{12,11},... | collective-permute-start | bytes 786440 | tf_op jit(solution)/shard_map/ppermute | solution.py:250
  71.7 9.5 %collective-permute-start.6 = (bf16[16,16,256]{2,1,0:T(8,128)(2,1)S(1)}, bf16[16,16,256]{2,1,0:T(8,128)(2,1)S(1)}, u32[]{:S(2)}, u32[]{:S(2)}) collective-permute-start(bf16[16,16,256]{2,1,0:T(8,128)(2,1)S(1)} %get-tuple-element.50), channel_id=1, source_target_pairs={{1,10},{2,9},{3,12},{4,11},{5,14},{6,13},{9,18},{10,17},{11,20},{1... | collective-permute-start | bytes 393224 | tf_op jit(solution)/shard_map/ppermute | solution.py:250
  75.7 7.5 %collective-permute-start.7 = (bf16[16,16,256]{2,1,0:T(8,128)(2,1)S(1)}, bf16[16,16,256]{2,1,0:T(8,128)(2,1)S(1)}, u32[]{:S(2)}, u32[]{:S(2)}) collective-permute-start(bf16[16,16,256]{2,1,0:T(8,128)(2,1)S(1)} %get-tuple-element.51), channel_id=1, source_target_pairs={{9,2},{10,1},{11,4},{12,3},{13,6},{14,5},{17,10},{18,9},{19,12},{2... | collective-permute-start | bytes 393224 | tf_op jit(solution)/shard_map/ppermute | solution.py:250
  84.9 7.0 %copy-start.9 = (bf16[32,16,256]{2,1,0:T(8,128)(2,1)}, bf16[32,16,256]{2,1,0:T(8,128)(2,1)S(1)}, u32[]{:S(2)}) copy-start(bf16[32,16,256]{2,1,0:T(8,128)(2,1)S(1)} %get-tuple-element.62) | copy-start | bytes 786436
  84.9 7.0 %copy-start.10 = (bf16[16,16,256]{2,1,0:T(8,128)(2,1)}, bf16[16,16,256]{2,1,0:T(8,128)(2,1)S(1)}, u32[]{:S(2)}) copy-start(bf16[16,16,256]{2,1,0:T(8,128)(2,1)S(1)} %get-tuple-element.58) | copy-start | bytes 393220
  84.9 7.7 %copy-start.11 = (bf16[16,16,256]{2,1,0:T(8,128)(2,1)}, bf16[16,16,256]{2,1,0:T(8,128)(2,1)S(1)}, u32[]{:S(2)}) copy-start(bf16[16,16,256]{2,1,0:T(8,128)(2,1)S(1)} %get-tuple-element.57) | copy-start | bytes 393220
  84.9 25.6 %collective-permute-start.8 = (bf16[16,48,256]{2,1,0:T(8,128)(2,1)S(1)}, bf16[16,48,256]{2,1,0:T(8,128)(2,1)}, u32[]{:S(2)}, u32[]{:S(2)}) collective-permute-start(bf16[16,48,256]{2,1,0:T(8,128)(2,1)S(1)} %get-tuple-element.54.low_ref.gl_ref), channel_id=1, source_target_pairs={{0,8},{1,9},{2,10},{3,11},{4,12},{5,13},{6,14},{7,15},{8,16},{9,17... | collective-permute-start | bytes 1179656 | tf_op jit(solution)/shard_map/ppermute | solution.py:250
  89.2 21.3 %collective-permute-start.9 = (bf16[16,48,256]{2,1,0:T(8,128)(2,1)S(1)}, bf16[16,48,256]{2,1,0:T(8,128)(2,1)}, u32[]{:S(2)}, u32[]{:S(2)}) collective-permute-start(bf16[16,48,256]{2,1,0:T(8,128)(2,1)S(1)} %get-tuple-element.53.top_ref.gt_ref), channel_id=1, source_target_pairs={{8,0},{9,1},{10,2},{11,3},{12,4},{13,5},{14,6},{15,7},{16,8},{17,9... | collective-permute-start | bytes 1179656 | tf_op jit(solution)/shard_map/ppermute | solution.py:250
  92.6 17.9 %collective-permute-start.12 = (bf16[32,16,256]{2,1,0:T(8,128)(2,1)}, bf16[32,16,256]{2,1,0:T(8,128)(2,1)}, u32[]{:S(2)}, u32[]{:S(2)}) collective-permute-start(bf16[32,16,256]{2,1,0:T(8,128)(2,1)} %get-tuple-element.59), channel_id=1, source_target_pairs={{1,2},{2,1},{3,4},{4,3},{5,6},{6,5},{9,10},{10,9},{11,12},{12,11},... | collective-permute-start | bytes 786440 | tf_op jit(solution)/shard_map/ppermute | solution.py:250
  95.6 7.4 %collective-permute-start.10 = (bf16[16,16,256]{2,1,0:T(8,128)(2,1)}, bf16[16,16,256]{2,1,0:T(8,128)(2,1)S(1)}, u32[]{:S(2)}, u32[]{:S(2)}) collective-permute-start(bf16[16,16,256]{2,1,0:T(8,128)(2,1)} %copy-done.11), channel_id=1, source_target_pairs={{1,10},{2,9},{3,12},{4,11},{5,14},{6,13},{9,18},{10,17},{11,20},{1... | collective-permute-start | bytes 393224 | tf_op jit(solution)/shard_map/ppermute | solution.py:250
  100.8 9.7 %collective-permute-start.11 = (bf16[16,16,256]{2,1,0:T(8,128)(2,1)}, bf16[16,16,256]{2,1,0:T(8,128)(2,1)S(1)}, u32[]{:S(2)}, u32[]{:S(2)}) collective-permute-start(bf16[16,16,256]{2,1,0:T(8,128)(2,1)} %copy-done.10), channel_id=1, source_target_pairs={{9,2},{10,1},{11,4},{12,3},{13,6},{14,5},{17,10},{18,9},{19,12},{2... | collective-permute-start | bytes 393224 | tf_op jit(solution)/shard_map/ppermute | solution.py:250
  103.0 9.8 %collective-permute-start.13 = (bf16[32,16,256]{2,1,0:T(8,128)(2,1)}, bf16[32,16,256]{2,1,0:T(8,128)(2,1)S(1)}, u32[]{:S(2)}, u32[]{:S(2)}) collective-permute-start(bf16[32,16,256]{2,1,0:T(8,128)(2,1)} %copy-done.9), channel_id=1, source_target_pairs={{0,1},{1,0},{2,3},{3,2},{4,5},{5,4},{6,7},{7,6},{8,9},{9,8},{10,11... | collective-permute-start | bytes 786440 | tf_op jit(solution)/shard_map/ppermute | solution.py:250
  111.7 1.8 collective-permute-start.14
  113.4 1.9 %copy-start.5 = (bf16[1024,1536]{1,0:T(8,128)(2,1)S(1)}, bf16[1024,1536]{1,0:T(8,128)(2,1)}, u32[]{:S(2)}) copy-start(bf16[1024,1536]{1,0:T(8,128)(2,1)} %copy-done.4) | copy-start | bytes 9437188
  120.6 4.1 %copy-start.12 = (bf16[64,80,256]{2,1,0:T(8,128)(2,1)}, bf16[64,80,256]{2,1,0:T(8,128)(2,1)S(1)}, u32[]{:S(2)}) copy-start(bf16[64,80,256]{2,1,0:T(8,128)(2,1)S(1)} %get-tuple-element.68.g_ref) | copy-start | bytes 7864324
  120.6 4.5 %collective-permute-start.15 = (bf16[32,152,128]{2,1,0:T(8,128)(2,1)S(1)}, bf16[32,152,128]{2,1,0:T(8,128)(2,1)S(1)}, u32[]{:S(2)}, u32[]{:S(2)}) collective-permute-start(bf16[32,152,128]{2,1,0:T(8,128)(2,1)S(1)} %get-tuple-element.70), channel_id=1, source_target_pairs={{0,1},{1,0},{2,3},{3,2},{4,5},{5,4},{6,7},{7,6},{8,9},{9,8},{10,11... | collective-permute-start | bytes 3735560 | tf_op jit(solution)/shard_map/ppermute | solution.py:250
  124.7 3.0 %collective-permute-start.16 = (bf16[32,152,128]{2,1,0:T(8,128)(2,1)S(1)}, bf16[32,152,128]{2,1,0:T(8,128)(2,1)S(1)}, u32[]{:S(2)}, u32[]{:S(2)}) collective-permute-start(bf16[32,152,128]{2,1,0:T(8,128)(2,1)S(1)} %get-tuple-element.72), channel_id=1, source_target_pairs={{0,1},{1,0},{2,3},{3,2},{4,5},{5,4},{6,7},{7,6},{8,9},{9,8},{10,11... | collective-permute-start | bytes 3735560 | tf_op jit(solution)/shard_map/ppermute | solution.py:250
  128.1 1.5 copy-start
  129.6 46.3 %all-to-all-start.1 = ((bf16[64,152,128]{2,1,0:T(8,128)(2,1)}), bf16[64,152,128]{2,1,0:T(8,128)(2,1)}, u32[]{:S(2)}, u32[]{:S(2)}) async-start(bf16[64,152,128]{2,1,0:T(8,128)(2,1)} %copy-done), calls=%async_computation.1 | async-start | bytes 4980736 | tf_op jit(solution)/shard_map/all_to_all | solution.py:362
  143.5 1.7 copy-start.8
  145.2 1.7 copy-start.13
  178.0 3.1 %collective-permute-start.17 = (f32[74,128]{1,0:T(8,128)S(1)}, f32[74,128]{1,0:T(8,128)S(1)}, u32[]{:S(2)}, u32[]{:S(2)}) collective-permute-start(f32[74,128]{1,0:T(8,128)S(1)} %fusion.5), channel_id=1, source_target_pairs={{0,1},{1,0},{2,3},{3,2},{4,5},{5,4},{6,7},{7,6},{8,9},{9,8},{10,11... | collective-permute-start | bytes 113672 | tf_op jit(solution)/shard_map/ppermute | solution.py:250

commit v3 on v2

--- a/solution.py
+++ b/solution.py
@@ -51,6 +51,36 @@
 
 def px(ref, r0, r1, c0, c1):
     return ref[r0:r1, c0:c1, :].reshape((r1 - r0) * (c1 - c0), ref.shape[2])
+
+
+def give_kernel(core_ref, conv_ref, proj_ref, keep_ref, give_ref, acc):
+    first = core_ref[0] == 0
+    low, high = conv_ref[:, :128].astype(F32), conv_ref[:, 128:].astype(F32)
+    proj = proj_ref[...].astype(F32)
+    acc[...] = jnp.zeros_like(acc)
+    acc[72:74] = proj[:, :128]
+    acc[74:76] = proj[:, 128:]
+    acc[0:72] = jnp.where(first, low, high)
+    keep_ref[...] = acc[...].astype(BF)
+    acc[0:72] = jnp.where(first, high, low)
+    give_ref[...] = acc[...].astype(BF)
+
+
+def spread_kernel(core_ref, keep_ref, got_ref, out_ref, acc):
+    first = core_ref[0] == 0
+    keep, got = keep_ref[...].astype(F32), got_ref[...].astype(F32)
+    even, odd = jnp.where(first, keep, got), jnp.where(first, got, keep)
+    acc[0:72] = even[0:72]
+    acc[72:144] = odd[0:72]
+    acc[144:146] = even[72:74]
+    acc[146:148] = odd[72:74]
+    acc[148:150] = even[74:76]
+    acc[150:152] = odd[74:76]
+    chunk = acc[...].astype(BF)
+
+    @pl.loop(0, 64)
+    def _(k):
+        out_ref[k] = chunk
 
 
 def flip_kernel(f_ref, ft_ref):
@@ -101,9 +131,11 @@
         dst[:, cols, :] = (src[:, cols, :].astype(F32) + swap(inner_ref[r : r + 16]).astype(F32)).astype(BF)
 
 
-def own_kernel(f_ref, mine_ref, other_ref, cot_ref, proj_ref, bias_ref, pre_ref, hg_ref):
+def own_kernel(core_ref, f_ref, mine_ref, other_ref, cot_ref, proj_ref, bias_ref, pre_ref, hg_ref):
     first = dot(px(f_ref, 0, 32, 0, 48), tap(mine_ref, other_ref, 1, 1))
-    pre_ref[...] = (first + bias_ref[...]).reshape(32, 48, 256)
+    bias = bias_ref[...]
+    bias = jnp.where(core_ref[0] == 0, bias, swap(bias))
+    pre_ref[...] = (first + bias).reshape(32, 48, 256)
     for a, rows in ((0, ((0, 16), (16, 32))), (1, ((0, 32), (0, 32))), (2, ((16, 32), (0, 16)))):
         for b, cols in ((0, ((0, 32), (16, 48))), (1, ((0, 48), (0, 48))), (2, ((16, 48), (0, 32)))):
             if a == 1 and b == 1:
@@ -145,13 +177,24 @@
         c_ref[...] = edge
 
 
-def proj_kernel(hid_ref, cot_ref, proj_ref, top_ref, low_ref, out_ref, pw_ref, bias_ref):
+def proj_kernel(core_ref, hid_ref, cot_ref, proj_ref, top_ref, low_ref, out_ref, em_ref, eo_ref, pw, ext):
+    first = core_ref[0] == 0
+    start = pl.multiple_of(128 * core_ref[0], 128)
     hidden = px(hid_ref, 0, 32, 0, 48)
     cot = px(cot_ref, 0, 32, 0, 48)
     out_ref[...] = dot(hidden, proj_ref[...]).astype(BF).reshape(32, 48, 256)
-    pw_ref[...] = dot(hidden, cot, TN)
+    term = dot(hidden, cot, TN)
+    term = jnp.where(first, term, swap(term))
+    pw[pl.ds(start, 128), :] = term[0:128]
+    pw[pl.ds(128 - start, 128), :] = term[128:256]
     total = px(top_ref, 0, 16, 0, 48).astype(F32) + px(low_ref, 0, 16, 0, 48).astype(F32)
-    bias_ref[...] = jnp.sum(total, axis=0, keepdims=True)
+    bias = jnp.sum(total, axis=0, keepdims=True)
+    bias = jnp.where(first, bias, swap(bias))
+    for e_ref, c in ((em_ref, 0), (eo_ref, 128)):
+        for k in range(64):
+            ext[k, 0:4] = pw[4 * k : 4 * k + 4, c : c + 128]
+            ext[k, 4:8] = jnp.broadcast_to(bias[:, 128 * (k // 32) : 128 * (k // 32) + 128], (4, 128))
+        e_ref[...] = ext[...].astype(BF)
 
 
 def edge_kernel(core_ref, top_ref, low_ref, edge_ref):
@@ -223,6 +266,27 @@
         out_ref[pl.ds(32 + 2 * k, 2)] = (m_ref[pair].astype(F32) + r_ref[pair].astype(F32)).astype(BF)
 
 
+def sum_kernel(core_ref, in_ref, keep_ref, give_ref, bias_ref, acc):
+    acc[...] = in_ref[0].astype(F32)
+
+    @pl.loop(1, 64)
+    def _(k):
+        acc[...] += in_ref[k].astype(F32)
+
+    bias_ref[...] = acc[148:149]
+    for out, c in ((keep_ref, core_ref[0]), (give_ref, 1 - core_ref[0])):
+        out[0:72] = acc[pl.ds(pl.multiple_of(72 * c, 8), 72)]
+        out[72:80] = jnp.where(c == 0, acc[144:152], pltpu.roll(acc[144:152], 6, 0))
+
+
+def join_kernel(core_ref, keep_ref, got_ref, conv_ref, proj_ref):
+    first = core_ref[0] == 0
+    keep, got = keep_ref[...], got_ref[...]
+    both = jnp.concatenate([jnp.where(first, keep, got), jnp.where(first, got, keep)], axis=1)
+    conv_ref[...] = both[0:72]
+    proj_ref[...] = both[72:74]
+
+
 def fgrad_kernel(g_ref, mine_ref, other_ref, out_ref):
     @pl.loop(0, 4)
     def _(k):
@@ -237,7 +301,6 @@
 
 def body(features, conv_weight, conv_bias, proj_weight, cotangent):
     core = lax.axis_index("core")
-    is0 = core == 0
     core_s = core.astype(jnp.int32).reshape(1)
     smem = pl.BlockSpec(memory_space=pltpu.SMEM)
 
@@ -267,20 +330,26 @@
 
     SAME, INNER, OUTER = (0, 0), (1, -1), (-1, 1)
 
-    low, high = conv_weight[:, :128], conv_weight[:, 128:]
-    own_proj = jnp.concatenate([proj_weight[:, :128], proj_weight[:, 128:]], axis=0)
-    got = send(jnp.concatenate([jnp.where(is0, high, low), own_proj], axis=0), 0, INNER)
-    keep = jnp.concatenate([jnp.where(is0, low, high), own_proj], axis=0)
-    even, odd = jnp.where(is0, keep, got), jnp.where(is0, got, keep)
-    chunk = jnp.concatenate([even[:72], odd[:72], even[72:74], odd[72:74], even[74:76], odd[74:76]], axis=0)
-    mine = lax.all_to_all(jnp.broadcast_to(chunk[None], (64, 152, 128)), CHIPS, 0, 0)
+    pack = array((80, 128))
+    keep, give = call(
+        give_kernel, "give", [pack, pack], [core_s, conv_weight, proj_weight], 1e5, 1e5, [pltpu.VMEM((80, 128), F32)]
+    )
+    got = send(give, 0, INNER)
+    (spread,) = call(
+        spread_kernel,
+        "spread",
+        [array((64, 152, 128))],
+        [core_s, keep, got],
+        1e5,
+        3e6,
+        [pltpu.VMEM((152, 128), F32)],
+    )
+    mine = lax.all_to_all(spread, CHIPS, 0, 0)
     (ft,) = call(flip_kernel, "flip", [array((1024, 1536))], [features], 1e6, 6e6)
     mine, ft = lax.optimization_barrier((mine, ft))
     other = send(mine, 0, INNER)
     (proj,) = call(rows_kernel, "rows", [array((256, 256))], [core_s, mine], 1e6, 1e6, [pltpu.VMEM((256, 256), F32)])
     other, proj = lax.optimization_barrier((other, proj))
-    bias = jnp.where(is0, conv_bias, jnp.concatenate([conv_bias[128:], conv_bias[:128]])).reshape(1, 256)
-
     tile, strip, small, side = (32, 48, 256), (16, 48, 256), (16, 16, 256), (32, 16, 256)
     n, s, inner, outer, cn, cs = call(
         halo_kernel,
@@ -303,7 +372,7 @@
         own_kernel,
         "own",
         [array(tile, F32), array(tile, F32)],
-        [features, mine, other, cotangent, proj, bias],
+        [core_s, features, mine, other, cotangent, proj, conv_bias.reshape(1, 256)],
         4e9,
         12e6,
     )
@@ -324,24 +393,16 @@
     c_low = send(ct, -1, OUTER)
     h_inner = send(gi, 0, INNER)
 
-    projected, pw, bias_term = call(
+    ends = array((64, 8, 128))
+    projected, e_mine, e_other = call(
         proj_kernel,
         "proj",
-        [array(tile), array((256, 256), F32), array((1, 256), F32)],
-        [hidden, cotangent, proj, g_top, g_low],
-        4e8,
+        [array(tile), ends, ends],
+        [core_s, hidden, cotangent, proj, g_top, g_low],
+        4e9,
         4e6,
-    )
-    pw = jnp.where(is0, pw, jnp.concatenate([pw[128:], pw[:128]], axis=0)).astype(BF)
-    bias_term = jnp.where(is0, bias_term, jnp.concatenate([bias_term[:, 128:], bias_term[:, :128]], axis=1))
-    bias_rows = jnp.pad(bias_term.astype(BF).reshape(64, 1, 4), ((0, 0), (0, 3), (0, 124)))
-
-    def extra(p):
-        return jnp.concatenate([p.reshape(64, 4, 128), bias_rows], axis=1)
-
-    e_mine = extra(jnp.where(is0, pw[:, :128], pw[:, 128:]))
-    e_other = extra(jnp.where(is0, pw[:, 128:], pw[:, :128]))
-
+        [pltpu.VMEM((256, 256), F32), pltpu.VMEM((64, 8, 128), F32)],
+    )
     h_top, h_low, c_top, c_low, h_outer = lax.optimization_barrier((h_top, h_low, c_top, c_low, h_outer))
     (edge,) = call(edge_kernel, "edge", [array(side)], [core_s, h_top, h_low], 1e6, 1e6)
     edge = send(edge, 0, INNER)
@@ -363,13 +424,23 @@
 
     (features_grad,) = call(fgrad_kernel, "fgrad", [array((32, 48, 1024))], [g, mine, other], 7.2e9, 12e6)
 
-    sums = jnp.sum(pieces.astype(F32), axis=0)
-    lo, hi = jnp.concatenate([sums[:72], sums[144:146]], 0), jnp.concatenate([sums[72:144], sums[146:148]], 0)
-    keep = jnp.where(is0, lo, hi)
-    got = send(jnp.where(is0, hi, lo), 0, INNER)
-    both = jnp.concatenate([jnp.where(is0, keep, got), jnp.where(is0, got, keep)], axis=1)
-    bias_grad = jnp.where(is0, sums[148, 0:2], sums[148, 2:4])
-    return projected, features_grad, both[:72], both[72:74], bias_grad
+    pack = array((80, 128), F32)
+    keep, give, bias_row = call(
+        sum_kernel,
+        "sum",
+        [pack, pack, array((1, 128), F32)],
+        [core_s, pieces],
+        1e6,
+        3e6,
+        [pltpu.VMEM((152, 128), F32)],
+    )
+    got = send(give, 0, INNER)
+    conv_grad, proj_grad = call(
+        join_kernel, "join", [array((72, 256), F32), array((2, 256), F32)], [core_s, keep, got], 1e5, 1e5
+    )
+    here = 2 * lax.axis_index(ALL) % 128
+    bias_grad = lax.dynamic_slice(bias_row.reshape(128), (here,), (2,))
+    return projected, features_grad, conv_grad, proj_grad, bias_grad
 
 
 def solution(mesh):

time: 183 us -> 176 us (0.962)
  other arithmetic: 6.49 us -> 0 us
    concatenate x4 -> x0, other arithmetic: 2.11 us -> none  [the longest x2 1.22 us: body(): jnp.concatenate([jnp.where(is0, keep, got), jnp.where(is0, got, keep)], a...]
    reduce_sum x1 -> x0, other arithmetic: 2.07 us -> none  [body(): sums = jnp.sum(pieces.astype(F32), axis=0)]
    pallas_call x13 -> x17, Pallas kernels: 32.9 us -> 33.6 us  [call(): pl.pallas_call(kernel, out_shape=tuple(outs), in_specs=specs, out_specs=(...]
  transfers between devices with their start and end apart: 20 -> 20, of which waited for: 10 -> 10; matrix products, arithmetic and copies ran while one was open for 2% -> 0% of each run, Pallas kernels for 12% -> 12%
where the time goes in v3:
time: 176 us; the launch traced here: 175 us
  waiting for transfers between devices  66.7 us (38%)
  starting transfers between devices  59.1 us (34%)
  Pallas kernels  33.6 us (19%)
  local copies, waits for them, and re-layouts  14.5 us (8%)
    ppermute x18, starting transfers between devices, send(): return lax.ppermute(x, ALL, perm)  34.2 us
    pallas_call x17, Pallas kernels, call(): pl.pallas_call(kernel, out_shape=tuple(outs), in_specs=specs, out_specs=(...  33.6 us
    all_to_all x1, waiting for transfers between devices, body(): mine = lax.all_to_all(spread, CHIPS, 0, 0)  27.9 us
    ppermute x18, waiting for transfers between devices, send(): return lax.ppermute(x, ALL, perm)  20.2 us
    all_to_all x1, waiting for transfers between devices, body(): pieces = lax.all_to_all(total, CHIPS, 0, 0)  18.6 us
    unnamed x30, local copies, waits for them, and re-layouts  13.9 us
    all_to_all x1, starting transfers between devices, body(): pieces = lax.all_to_all(total, CHIPS, 0, 0)  13.6 us
    all_to_all x1, starting transfers between devices, body(): mine = lax.all_to_all(spread, CHIPS, 0, 0)  11.2 us
  transfers between devices with their start and end apart: 20, of which 10 were waited for; matrix products, arithmetic and copies ran while one was open for 0% of the time, Pallas kernels for 12%

profile of v3, /device:TPU:1, one launch (start us, length us, event | category | flops | bytes accessed | tf_op | source)
XLA Modules:
  0.0 174.8 jit_solution(9516113504796189582)
XLA Ops:
  0.6 0.8 copy-done.7
  1.4 0.7 copy-done.8
  2.1 1.5 collective-permute-start
  3.6 0.8 collective-permute-done.got_ref
  4.8 1.4 copy-done.1
  6.3 11.2 %all-to-all-start = ((bf16[64,152,128]{2,1,0:T(8,128)(2,1)}), bf16[64,152,128]{2,1,0:T(8,128)(2,1)S(1)}, u32[]{:S(2)}, u32[]{:S(2)}) async-start(bf16[64,152,128]{2,1,0:T(8,128)(2,1)} %copy-done.1), calls=%async_computation | async-start | bytes 4980736 | tf_op jit(solution)/shard_map/all_to_all | solution.py:347
  17.5 1.9 %copy-done.2 = bf16[32,48,1024]{2,1,0:T(8,128)(2,1)S(1)} copy-done((bf16[32,48,1024]{2,1,0:T(8,128)(2,1)S(1)}, bf16[32,48,1024]{2,1,0:T(8,128)(2,1)}, u32[]{:S(2)}) %copy-start.2) | copy-done | bytes 3145752
  19.4 0.9 flip.1.ft_ref
  20.2 1.7 copy-done.5
  21.9 27.9 %all-to-all-done.mine_ref = bf16[64,152,128]{2,1,0:T(8,128)(2,1)S(1)} async-done(((bf16[64,152,128]{2,1,0:T(8,128)(2,1)}), bf16[64,152,128]{2,1,0:T(8,128)(2,1)S(1)}, u32[]{:S(2)}, u32[]{:S(2)}) %all-to-all-start) | async-done | bytes 2490400 | tf_op jit(solution)/shard_map/all_to_all | solution.py:347
  49.8 2.3 %collective-permute-start.1 = (bf16[64,152,128]{2,1,0:T(8,128)(2,1)S(1)}, bf16[64,152,128]{2,1,0:T(8,128)(2,1)S(1)}, u32[]{:S(2)}, u32[]{:S(2)}) collective-permute-start(bf16[64,152,128]{2,1,0:T(8,128)(2,1)S(1)} %all-to-all-done.mine_ref), channel_id=1, source_target_pairs={{0,1},{1,0},{2,3},{3,2},{4,5},{5,4},{6,7},{7,6},{8,9},{9,8},{10,11... | collective-permute-start | bytes 7471112 | tf_op jit(solution)/shard_map/ppermute | solution.py:313
  52.2 4.3 %collective-permute-done.1.other_ref = bf16[64,152,128]{2,1,0:T(8,128)(2,1)S(1)} collective-permute-done((bf16[64,152,128]{2,1,0:T(8,128)(2,1)S(1)}, bf16[64,152,128]{2,1,0:T(8,128)(2,1)S(1)}, u32[]{:S(2)}, u32[]{:S(2)}) %collective-permute-start.1) | collective-permute-done | bytes 2490400 | tf_op jit(solution)/shard_map/ppermute | solution.py:313
  56.5 1.9 %copy-done.3 = bf16[32,48,1024]{2,1,0:T(8,128)(2,1)S(1)} copy-done((bf16[32,48,1024]{2,1,0:T(8,128)(2,1)S(1)}, bf16[32,48,1024]{2,1,0:T(8,128)(2,1)}, u32[]{:S(2)}) %copy-start.3) | copy-done | bytes 3145752
  58.4 3.8 %halo.1 = (bf16[16,48,256]{2,1,0:T(8,128)(2,1)S(1)}, bf16[16,48,256]{2,1,0:T(8,128)(2,1)S(1)}, bf16[64,16,256]{2,1,0:T(8,128)(2,1)S(1)}, bf16[32,16,256]{2,1,0:T...) custom-call(s32[1]{0:T(128)} %bitcast.core_ref, ...), custom_call_target="tpu_custom_call" | custom-call | flops 3500000000 | bytes 9000000 | tf_op jit(solution)/shard_map/halo/pallas_call | solution.py:320
  62.2 0.4 collective-permute-start.2
  62.6 1.5 collective-permute-done.2.inner_ref
  64.3 2.5 %collective-permute-start.3 = (bf16[16,48,256]{2,1,0:T(8,128)(2,1)S(1)}, bf16[16,48,256]{2,1,0:T(8,128)(2,1)S(1)}, u32[]{:S(2)}, u32[]{:S(2)}) collective-permute-start(bf16[16,48,256]{2,1,0:T(8,128)(2,1)S(1)} %get-tuple-element.56), channel_id=1, source_target_pairs={{0,8},{1,9},{2,10},{3,11},{4,12},{5,13},{6,14},{7,15},{8,16},{9,17... | collective-permute-start | bytes 1179656 | tf_op jit(solution)/shard_map/ppermute | solution.py:313
  66.8 1.3 collective-permute-start.4
  68.1 3.5 %collective-permute-start.5 = (bf16[32,16,256]{2,1,0:T(8,128)(2,1)S(1)}, bf16[32,16,256]{2,1,0:T(8,128)(2,1)S(1)}, u32[]{:S(2)}, u32[]{:S(2)}) collective-permute-start(bf16[32,16,256]{2,1,0:T(8,128)(2,1)S(1)} %get-tuple-element.58), channel_id=1, source_target_pairs={{1,2},{2,1},{3,4},{4,3},{5,6},{6,5},{9,10},{10,9},{11,12},{12,11},... | collective-permute-start | bytes 786440 | tf_op jit(solution)/shard_map/ppermute | solution.py:313
  71.6 4.0 %collective-permute-start.6 = (bf16[16,16,256]{2,1,0:T(8,128)(2,1)S(1)}, bf16[16,16,256]{2,1,0:T(8,128)(2,1)S(1)}, u32[]{:S(2)}, u32[]{:S(2)}) collective-permute-start(bf16[16,16,256]{2,1,0:T(8,128)(2,1)S(1)} %get-tuple-element.59), channel_id=1, source_target_pairs={{1,10},{2,9},{3,12},{4,11},{5,14},{6,13},{9,18},{10,17},{11,20},{1... | collective-permute-start | bytes 393224 | tf_op jit(solution)/shard_map/ppermute | solution.py:313
  75.7 1.3 collective-permute-start.7
  77.0 4.3 %own.1 = (f32[32,48,256]{2,1,0:T(8,128)S(1)}, f32[32,48,256]{2,1,0:T(8,128)S(1)}) custom-call(s32[1]{0:T(128)} %bitcast.core_ref, bf16[32,48,1024]{2,1,0:T(8,128)(2,1)S(1)} %copy-done.4, bf16[64,152,128]{2,1,0:T(8,128)(2,1)S(1)} %all-to-all-done.mine_ref, bf16[64,152,128]{2,1,0:T(8,128)(2,1)S(1)} %collective-permute-done.1.other_ref, ...), custom_call_target="tpu_custom_call" | custom-call | flops 4000000000 | bytes 12000000 | tf_op jit(solution)/shard_map/own/pallas_call | solution.py:320
  81.3 1.9 %collective-permute-done.7.cs_ref = bf16[16,16,256]{2,1,0:T(8,128)(2,1)S(1)} collective-permute-done((bf16[16,16,256]{2,1,0:T(8,128)(2,1)S(1)}, bf16[16,16,256]{2,1,0:T(8,128)(2,1)S(1)}, u32[]{:S(2)}, u32[]{:S(2)}) %collective-permute-start.7) | collective-permute-done | bytes 131104 | tf_op jit(solution)/shard_map/ppermute | solution.py:313
  83.2 1.1 point.1
  84.3 3.6 %collective-permute-start.8 = (bf16[16,48,256]{2,1,0:T(8,128)(2,1)S(1)}, bf16[16,48,256]{2,1,0:T(8,128)(2,1)S(1)}, u32[]{:S(2)}, u32[]{:S(2)}) collective-permute-start(bf16[16,48,256]{2,1,0:T(8,128)(2,1)S(1)} %get-tuple-element.63.low_ref.gl_ref), channel_id=1, source_target_pairs={{0,8},{1,9},{2,10},{3,11},{4,12},{5,13},{6,14},{7,15},{8,16},{9,17... | collective-permute-start | bytes 1179656 | tf_op jit(solution)/shard_map/ppermute | solution.py:313
  87.9 1.3 collective-permute-start.9
  89.2 2.2 %collective-permute-start.12 = (bf16[32,16,256]{2,1,0:T(8,128)(2,1)S(1)}, bf16[32,16,256]{2,1,0:T(8,128)(2,1)S(1)}, u32[]{:S(2)}, u32[]{:S(2)}) collective-permute-start(bf16[32,16,256]{2,1,0:T(8,128)(2,1)S(1)} %get-tuple-element.68), channel_id=1, source_target_pairs={{1,2},{2,1},{3,4},{4,3},{5,6},{6,5},{9,10},{10,9},{11,12},{12,11},... | collective-permute-start | bytes 786440 | tf_op jit(solution)/shard_map/ppermute | solution.py:313
  91.4 5.3 %collective-permute-start.10 = (bf16[16,16,256]{2,1,0:T(8,128)(2,1)S(1)}, bf16[16,16,256]{2,1,0:T(8,128)(2,1)S(1)}, u32[]{:S(2)}, u32[]{:S(2)}) collective-permute-start(bf16[16,16,256]{2,1,0:T(8,128)(2,1)S(1)} %get-tuple-element.66), channel_id=1, source_target_pairs={{1,10},{2,9},{3,12},{4,11},{5,14},{6,13},{9,18},{10,17},{11,20},{1... | collective-permute-start | bytes 393224 | tf_op jit(solution)/shard_map/ppermute | solution.py:313
  96.7 1.3 collective-permute-start.11
  98.0 0.6 collective-permute-done.10.ct_ref
  98.6 8.1 %collective-permute-done.11.cl_ref = bf16[16,16,256]{2,1,0:T(8,128)(2,1)S(1)} collective-permute-done((bf16[16,16,256]{2,1,0:T(8,128)(2,1)S(1)}, bf16[16,16,256]{2,1,0:T(8,128)(2,1)S(1)}, u32[]{:S(2)}, u32[]{:S(2)}) %collective-permute-start.11) | collective-permute-done | bytes 131104 | tf_op jit(solution)/shard_map/ppermute | solution.py:313
  107.0 1.5 proj.1
  108.6 0.7 copy-done.6
  109.2 4.1 %wgrad.1 = (bf16[64,80,256]{2,1,0:T(8,128)(2,1)S(1)}, bf16[32,152,128]{2,1,0:T(8,128)(2,1)S(1)}, bf16[32,152,128]{2,1,0:T(8,128)(2,1)S(1)}) custom-call(s32[1]{0:T(128)} %bitcast.core_ref, bf16[1024,1536]{1,0:T(8,128)(2,1)S(1)} %copy-done.6, bf16[16,48,256]{2,1,0:T(8,128)(2,1)S(1)} %get-tuple-element.62.top_ref.gt_ref, ...), custom_call_target="tpu_custom_call" | custom-call | flops 3600000000 | bytes 8000000 | tf_op jit(solution)/shard_map/wgrad/pallas_call | solution.py:320
  113.3 0.6 collective-permute-start.15
  113.9 3.8 %wgrad2.1 = (bf16[32,152,128]{2,1,0:T(8,128)(2,1)S(1)}, bf16[32,152,128]{2,1,0:T(8,128)(2,1)S(1)}) custom-call(bf16[1024,1536]{1,0:T(8,128)(2,1)S(1)} %copy-done.6, bf16[64,80,256]{2,1,0:T(8,128)(2,1)S(1)} %get-tuple-element.77.g_ref, bf16[64,8,128]{2,1,0:T(8,128)(2,1)S(1)} %get-tuple-element.75.em_ref, bf16[64,8,128]{2,1,0:T(8,128)(2,1)S(1)} %get-tuple-element.76.eo_ref), custom_call_target="tpu_custom_call" | custom-call | flops 3600000000 | bytes 8000000 | tf_op jit(solution)/shard_map/wgrad2/pallas_call | solution.py:320
  118.2 2.6 %collective-permute-done.16.r_ref = bf16[32,152,128]{2,1,0:T(8,128)(2,1)S(1)} collective-permute-done((bf16[32,152,128]{2,1,0:T(8,128)(2,1)S(1)}, bf16[32,152,128]{2,1,0:T(8,128)(2,1)S(1)}, u32[]{:S(2)}, u32[]{:S(2)}) %collective-permute-start.16) | collective-permute-done | bytes 1245216 | tf_op jit(solution)/shard_map/ppermute | solution.py:313
  120.7 0.4 add2.1
  121.2 1.4 copy-done
  122.6 13.6 %all-to-all-start.1 = ((bf16[64,152,128]{2,1,0:T(8,128)(2,1)}), bf16[64,152,128]{2,1,0:T(8,128)(2,1)}, u32[]{:S(2)}, u32[]{:S(2)}) async-start(bf16[64,152,128]{2,1,0:T(8,128)(2,1)} %copy-done), calls=%async_computation.1 | async-start | bytes 4980736 | tf_op jit(solution)/shard_map/all_to_all | solution.py:423
  136.2 1.7 copy-done.10
  137.9 1.7 copy-done.14
  139.7 9.8 %fgrad.1 = bf16[32,48,1024]{2,1,0:T(8,128)(2,1)} custom-call(bf16[64,80,256]{2,1,0:T(8,128)(2,1)S(1)} %copy-done.14, bf16[64,152,128]{2,1,0:T(8,128)(2,1)S(1)} %all-to-all-done.mine_ref, bf16[64,152,128]{2,1,0:T(8,128)(2,1)S(1)} %copy-done.10), custom_call_target="tpu_custom_call" | custom-call | flops 7200000000 | bytes 12000000 | tf_op jit(solution)/shard_map/fgrad/pallas_call | solution.py:320
  149.4 18.6 %all-to-all-done.1.in_ref = bf16[64,152,128]{2,1,0:T(8,128)(2,1)} async-done(((bf16[64,152,128]{2,1,0:T(8,128)(2,1)}), bf16[64,152,128]{2,1,0:T(8,128)(2,1)}, u32[]{:S(2)}, u32[]{:S(2)}) %all-to-all-start.1) | async-done | bytes 2490400 | tf_op jit(solution)/shard_map/all_to_all | solution.py:423
  168.1 2.5 %sum.1 = (f32[80,128]{1,0:T(8,128)S(1)}, f32[80,128]{1,0:T(8,128)S(1)}, f32[1,128]{1,0:T(1,128)S(1)}) custom-call(s32[1]{0:T(128)} %bitcast.core_ref, bf16[64,152,128]{2,1,0:T(8,128)(2,1)} %all-to-all-done.1.in_ref), custom_call_target="tpu_custom_call" | custom-call | flops 1000000 | bytes 3000000 | tf_op jit(solution)/shard_map/sum/pallas_call | solution.py:320
  170.6 2.7 %collective-permute-start.17 = (f32[80,128]{1,0:T(8,128)S(1)}, f32[80,128]{1,0:T(8,128)S(1)}, u32[]{:S(2)}, u32[]{:S(2)}) collective-permute-start(f32[80,128]{1,0:T(8,128)S(1)} %get-tuple-element.83), channel_id=1, source_target_pairs={{0,1},{1,0},{2,3},{3,2},{4,5},{5,4},{6,7},{7,6},{8,9},{9,8},{10,11... | collective-permute-start | bytes 122888 | tf_op jit(solution)/shard_map/ppermute | solution.py:313
  173.3 0.6 dynamic-slice_bitcast_fusion
  174.2 0.6 join.1
  (40 shorter events, 1.7 us)
Async XLA Ops:
  0.6 0.8 copy-start.7
  1.4 0.7 copy-start.8
  2.1 2.3 %collective-permute-start = (bf16[80,128]{1,0:T(8,128)(2,1)S(1)}, bf16[80,128]{1,0:T(8,128)(2,1)S(1)}, u32[]{:S(2)}, u32[]{:S(2)}) collective-permute-start(bf16[80,128]{1,0:T(8,128)(2,1)S(1)} %get-tuple-element.47), channel_id=1, source_target_pairs={{0,1},{1,0},{2,3},{3,2},{4,5},{5,4},{6,7},{7,6},{8,9},{9,8},{10,11... | collective-permute-start | bytes 61448 | tf_op jit(solution)/shard_map/ppermute | solution.py:313
  4.8 1.5 copy-start.1
  6.3 43.5 %all-to-all-start = ((bf16[64,152,128]{2,1,0:T(8,128)(2,1)}), bf16[64,152,128]{2,1,0:T(8,128)(2,1)S(1)}, u32[]{:S(2)}, u32[]{:S(2)}) async-start(bf16[64,152,128]{2,1,0:T(8,128)(2,1)} %copy-done.1), calls=%async_computation | async-start | bytes 4980736 | tf_op jit(solution)/shard_map/all_to_all | solution.py:347
  17.5 1.9 %copy-start.2 = (bf16[32,48,1024]{2,1,0:T(8,128)(2,1)S(1)}, bf16[32,48,1024]{2,1,0:T(8,128)(2,1)}, u32[]{:S(2)}) copy-start(bf16[32,48,1024]{2,1,0:T(8,128)(2,1)} %f_ref.5) | copy-start | bytes 9437188
  20.2 1.7 copy-start.5
  49.8 6.7 %collective-permute-start.1 = (bf16[64,152,128]{2,1,0:T(8,128)(2,1)S(1)}, bf16[64,152,128]{2,1,0:T(8,128)(2,1)S(1)}, u32[]{:S(2)}, u32[]{:S(2)}) collective-permute-start(bf16[64,152,128]{2,1,0:T(8,128)(2,1)S(1)} %all-to-all-done.mine_ref), channel_id=1, source_target_pairs={{0,1},{1,0},{2,3},{3,2},{4,5},{5,4},{6,7},{7,6},{8,9},{9,8},{10,11... | collective-permute-start | bytes 7471112 | tf_op jit(solution)/shard_map/ppermute | solution.py:313
  56.5 1.9 %copy-start.3 = (bf16[32,48,1024]{2,1,0:T(8,128)(2,1)S(1)}, bf16[32,48,1024]{2,1,0:T(8,128)(2,1)}, u32[]{:S(2)}) copy-start(bf16[32,48,1024]{2,1,0:T(8,128)(2,1)} %f_ref.5) | copy-start | bytes 9437188
  58.4 18.6 %copy-start.9 = (bf16[64,152,128]{2,1,0:T(8,128)(2,1)}, bf16[64,152,128]{2,1,0:T(8,128)(2,1)S(1)}, u32[]{:S(2)}) copy-start(bf16[64,152,128]{2,1,0:T(8,128)(2,1)S(1)} %collective-permute-done.1.other_ref) | copy-start | bytes 7471108
  58.4 18.6 %copy-start.4 = (bf16[32,48,1024]{2,1,0:T(8,128)(2,1)S(1)}, bf16[32,48,1024]{2,1,0:T(8,128)(2,1)}, u32[]{:S(2)}) copy-start(bf16[32,48,1024]{2,1,0:T(8,128)(2,1)} %f_ref.5) | copy-start | bytes 9437188
  58.4 18.6 %copy-start.11 = (bf16[32,48,256]{2,1,0:T(8,128)(2,1)S(1)}, bf16[32,48,256]{2,1,0:T(8,128)(2,1)}, u32[]{:S(2)}) copy-start(bf16[32,48,256]{2,1,0:T(8,128)(2,1)} %cot_ref.3) | copy-start | bytes 2359300
  58.4 18.6 %copy-start.12 = (f32[256]{0:T(256)S(1)}, f32[256]{0:T(256)}, u32[]{:S(2)}) copy-start(f32[256]{0:T(256)} %param.7) | copy-start | bytes 3076
  62.2 2.0 %collective-permute-start.2 = (bf16[64,16,256]{2,1,0:T(8,128)(2,1)S(1)}, bf16[64,16,256]{2,1,0:T(8,128)(2,1)S(1)}, u32[]{:S(2)}, u32[]{:S(2)}) collective-permute-start(bf16[64,16,256]{2,1,0:T(8,128)(2,1)S(1)} %get-tuple-element.55), channel_id=1, source_target_pairs={{0,1},{1,0},{2,3},{3,2},{4,5},{5,4},{6,7},{7,6},{8,9},{9,8},{10,11... | collective-permute-start | bytes 1572872 | tf_op jit(solution)/shard_map/ppermute | solution.py:313
  64.3 18.9 %collective-permute-start.3 = (bf16[16,48,256]{2,1,0:T(8,128)(2,1)S(1)}, bf16[16,48,256]{2,1,0:T(8,128)(2,1)S(1)}, u32[]{:S(2)}, u32[]{:S(2)}) collective-permute-start(bf16[16,48,256]{2,1,0:T(8,128)(2,1)S(1)} %get-tuple-element.56), channel_id=1, source_target_pairs={{0,8},{1,9},{2,10},{3,11},{4,12},{5,13},{6,14},{7,15},{8,16},{9,17... | collective-permute-start | bytes 1179656 | tf_op jit(solution)/shard_map/ppermute | solution.py:313
  66.8 16.3 %collective-permute-start.4 = (bf16[16,48,256]{2,1,0:T(8,128)(2,1)S(1)}, bf16[16,48,256]{2,1,0:T(8,128)(2,1)S(1)}, u32[]{:S(2)}, u32[]{:S(2)}) collective-permute-start(bf16[16,48,256]{2,1,0:T(8,128)(2,1)S(1)} %get-tuple-element.57), channel_id=1, source_target_pairs={{8,0},{9,1},{10,2},{11,3},{12,4},{13,5},{14,6},{15,7},{16,8},{17,9... | collective-permute-start | bytes 1179656 | tf_op jit(solution)/shard_map/ppermute | solution.py:313
  68.1 15.0 %collective-permute-start.5 = (bf16[32,16,256]{2,1,0:T(8,128)(2,1)S(1)}, bf16[32,16,256]{2,1,0:T(8,128)(2,1)S(1)}, u32[]{:S(2)}, u32[]{:S(2)}) collective-permute-start(bf16[32,16,256]{2,1,0:T(8,128)(2,1)S(1)} %get-tuple-element.58), channel_id=1, source_target_pairs={{1,2},{2,1},{3,4},{4,3},{5,6},{6,5},{9,10},{10,9},{11,12},{12,11},... | collective-permute-start | bytes 786440 | tf_op jit(solution)/shard_map/ppermute | solution.py:313
  71.6 9.6 %collective-permute-start.6 = (bf16[16,16,256]{2,1,0:T(8,128)(2,1)S(1)}, bf16[16,16,256]{2,1,0:T(8,128)(2,1)S(1)}, u32[]{:S(2)}, u32[]{:S(2)}) collective-permute-start(bf16[16,16,256]{2,1,0:T(8,128)(2,1)S(1)} %get-tuple-element.59), channel_id=1, source_target_pairs={{1,10},{2,9},{3,12},{4,11},{5,14},{6,13},{9,18},{10,17},{11,20},{1... | collective-permute-start | bytes 393224 | tf_op jit(solution)/shard_map/ppermute | solution.py:313
  75.7 7.5 %collective-permute-start.7 = (bf16[16,16,256]{2,1,0:T(8,128)(2,1)S(1)}, bf16[16,16,256]{2,1,0:T(8,128)(2,1)S(1)}, u32[]{:S(2)}, u32[]{:S(2)}) collective-permute-start(bf16[16,16,256]{2,1,0:T(8,128)(2,1)S(1)} %get-tuple-element.60), channel_id=1, source_target_pairs={{9,2},{10,1},{11,4},{12,3},{13,6},{14,5},{17,10},{18,9},{19,12},{2... | collective-permute-start | bytes 393224 | tf_op jit(solution)/shard_map/ppermute | solution.py:313
  84.3 22.5 %collective-permute-start.8 = (bf16[16,48,256]{2,1,0:T(8,128)(2,1)S(1)}, bf16[16,48,256]{2,1,0:T(8,128)(2,1)S(1)}, u32[]{:S(2)}, u32[]{:S(2)}) collective-permute-start(bf16[16,48,256]{2,1,0:T(8,128)(2,1)S(1)} %get-tuple-element.63.low_ref.gl_ref), channel_id=1, source_target_pairs={{0,8},{1,9},{2,10},{3,11},{4,12},{5,13},{6,14},{7,15},{8,16},{9,17... | collective-permute-start | bytes 1179656 | tf_op jit(solution)/shard_map/ppermute | solution.py:313
  87.9 18.8 %collective-permute-start.9 = (bf16[16,48,256]{2,1,0:T(8,128)(2,1)S(1)}, bf16[16,48,256]{2,1,0:T(8,128)(2,1)S(1)}, u32[]{:S(2)}, u32[]{:S(2)}) collective-permute-start(bf16[16,48,256]{2,1,0:T(8,128)(2,1)S(1)} %get-tuple-element.62.top_ref.gt_ref), channel_id=1, source_target_pairs={{8,0},{9,1},{10,2},{11,3},{12,4},{13,5},{14,6},{15,7},{16,8},{17,9... | collective-permute-start | bytes 1179656 | tf_op jit(solution)/shard_map/ppermute | solution.py:313
  89.2 17.5 %collective-permute-start.12 = (bf16[32,16,256]{2,1,0:T(8,128)(2,1)S(1)}, bf16[32,16,256]{2,1,0:T(8,128)(2,1)S(1)}, u32[]{:S(2)}, u32[]{:S(2)}) collective-permute-start(bf16[32,16,256]{2,1,0:T(8,128)(2,1)S(1)} %get-tuple-element.68), channel_id=1, source_target_pairs={{1,2},{2,1},{3,4},{4,3},{5,6},{6,5},{9,10},{10,9},{11,12},{12,11},... | collective-permute-start | bytes 786440 | tf_op jit(solution)/shard_map/ppermute | solution.py:313
  91.4 7.2 %collective-permute-start.10 = (bf16[16,16,256]{2,1,0:T(8,128)(2,1)S(1)}, bf16[16,16,256]{2,1,0:T(8,128)(2,1)S(1)}, u32[]{:S(2)}, u32[]{:S(2)}) collective-permute-start(bf16[16,16,256]{2,1,0:T(8,128)(2,1)S(1)} %get-tuple-element.66), channel_id=1, source_target_pairs={{1,10},{2,9},{3,12},{4,11},{5,14},{6,13},{9,18},{10,17},{11,20},{1... | collective-permute-start | bytes 393224 | tf_op jit(solution)/shard_map/ppermute | solution.py:313
  96.7 10.0 %collective-permute-start.11 = (bf16[16,16,256]{2,1,0:T(8,128)(2,1)S(1)}, bf16[16,16,256]{2,1,0:T(8,128)(2,1)S(1)}, u32[]{:S(2)}, u32[]{:S(2)}) collective-permute-start(bf16[16,16,256]{2,1,0:T(8,128)(2,1)S(1)} %get-tuple-element.67), channel_id=1, source_target_pairs={{9,2},{10,1},{11,4},{12,3},{13,6},{14,5},{17,10},{18,9},{19,12},{2... | collective-permute-start | bytes 393224 | tf_op jit(solution)/shard_map/ppermute | solution.py:313
  98.6 9.9 %collective-permute-start.13 = (bf16[32,16,256]{2,1,0:T(8,128)(2,1)S(1)}, bf16[32,16,256]{2,1,0:T(8,128)(2,1)S(1)}, u32[]{:S(2)}, u32[]{:S(2)}) collective-permute-start(bf16[32,16,256]{2,1,0:T(8,128)(2,1)S(1)} %get-tuple-element.71), channel_id=1, source_target_pairs={{0,1},{1,0},{2,3},{3,2},{4,5},{5,4},{6,7},{7,6},{8,9},{9,8},{10,11... | collective-permute-start | bytes 786440 | tf_op jit(solution)/shard_map/ppermute | solution.py:313
  106.8 1.8 %collective-permute-start.14 = (bf16[32,16,256]{2,1,0:T(8,128)(2,1)S(1)}, bf16[32,16,256]{2,1,0:T(8,128)(2,1)S(1)}, u32[]{:S(2)}, u32[]{:S(2)}) collective-permute-start(bf16[32,16,256]{2,1,0:T(8,128)(2,1)S(1)} %edge.1), channel_id=1, source_target_pairs={{0,1},{1,0},{2,3},{3,2},{4,5},{5,4},{6,7},{7,6},{8,9},{9,8},{10,11... | collective-permute-start | bytes 786440 | tf_op jit(solution)/shard_map/ppermute | solution.py:313
  107.0 2.2 %copy-start.6 = (bf16[1024,1536]{1,0:T(8,128)(2,1)S(1)}, bf16[1024,1536]{1,0:T(8,128)(2,1)}, u32[]{:S(2)}) copy-start(bf16[1024,1536]{1,0:T(8,128)(2,1)} %copy-done.5) | copy-start | bytes 9437188
  113.3 4.4 %copy-start.13 = (bf16[64,80,256]{2,1,0:T(8,128)(2,1)}, bf16[64,80,256]{2,1,0:T(8,128)(2,1)S(1)}, u32[]{:S(2)}) copy-start(bf16[64,80,256]{2,1,0:T(8,128)(2,1)S(1)} %get-tuple-element.77.g_ref) | copy-start | bytes 7864324
  113.3 4.5 %collective-permute-start.15 = (bf16[32,152,128]{2,1,0:T(8,128)(2,1)S(1)}, bf16[32,152,128]{2,1,0:T(8,128)(2,1)S(1)}, u32[]{:S(2)}, u32[]{:S(2)}) collective-permute-start(bf16[32,152,128]{2,1,0:T(8,128)(2,1)S(1)} %get-tuple-element.79), channel_id=1, source_target_pairs={{0,1},{1,0},{2,3},{3,2},{4,5},{5,4},{6,7},{7,6},{8,9},{9,8},{10,11... | collective-permute-start | bytes 3735560 | tf_op jit(solution)/shard_map/ppermute | solution.py:313
  117.7 3.0 %collective-permute-start.16 = (bf16[32,152,128]{2,1,0:T(8,128)(2,1)S(1)}, bf16[32,152,128]{2,1,0:T(8,128)(2,1)S(1)}, u32[]{:S(2)}, u32[]{:S(2)}) collective-permute-start(bf16[32,152,128]{2,1,0:T(8,128)(2,1)S(1)} %get-tuple-element.81), channel_id=1, source_target_pairs={{0,1},{1,0},{2,3},{3,2},{4,5},{5,4},{6,7},{7,6},{8,9},{9,8},{10,11... | collective-permute-start | bytes 3735560 | tf_op jit(solution)/shard_map/ppermute | solution.py:313
  121.2 1.5 copy-start
  122.6 45.5 %all-to-all-start.1 = ((bf16[64,152,128]{2,1,0:T(8,128)(2,1)}), bf16[64,152,128]{2,1,0:T(8,128)(2,1)}, u32[]{:S(2)}, u32[]{:S(2)}) async-start(bf16[64,152,128]{2,1,0:T(8,128)(2,1)} %copy-done), calls=%async_computation.1 | async-start | bytes 4980736 | tf_op jit(solution)/shard_map/all_to_all | solution.py:423
  136.2 1.7 copy-start.10
  137.9 1.7 copy-start.14
  170.6 3.6 %collective-permute-start.17 = (f32[80,128]{1,0:T(8,128)S(1)}, f32[80,128]{1,0:T(8,128)S(1)}, u32[]{:S(2)}, u32[]{:S(2)}) collective-permute-start(f32[80,128]{1,0:T(8,128)S(1)} %get-tuple-element.83), channel_id=1, source_target_pairs={{0,1},{1,0},{2,3},{3,2},{4,5},{5,4},{6,7},{7,6},{8,9},{9,8},{10,11... | collective-permute-start | bytes 122888 | tf_op jit(solution)/shard_map/ppermute | solution.py:313

commit v4 on v3

--- a/solution.py
+++ b/solution.py
@@ -1,3 +1,5 @@
+import functools
+
 import jax
 import jax.numpy as jnp
 import numpy as np
@@ -26,8 +28,12 @@
     return pl.BlockSpec(memory_space=pltpu.VMEM)
 
 
-def params():
-    return pltpu.CompilerParams(vmem_limit_bytes=VMEM_LIMIT)
+def any_space():
+    return pl.BlockSpec(memory_space=pl.ANY)
+
+
+def params(limit):
+    return pltpu.CompilerParams(vmem_limit_bytes=limit)
 
 
 def cost(flops, size):
@@ -66,7 +72,7 @@
     give_ref[...] = acc[...].astype(BF)
 
 
-def spread_kernel(core_ref, keep_ref, got_ref, out_ref, acc):
+def spread_kernel(core_ref, keep_ref, got_ref, out_ref, acc, many, sems):
     first = core_ref[0] == 0
     keep, got = keep_ref[...].astype(F32), got_ref[...].astype(F32)
     even, odd = jnp.where(first, keep, got), jnp.where(first, got, keep)
@@ -77,10 +83,13 @@
     acc[148:150] = even[74:76]
     acc[150:152] = odd[74:76]
     chunk = acc[...].astype(BF)
-
-    @pl.loop(0, 64)
-    def _(k):
-        out_ref[k] = chunk
+    for k in range(8):
+        many[k] = chunk
+    copies = [pltpu.make_async_copy(many, out_ref.at[pl.ds(8 * k, 8)], sems.at[k]) for k in range(8)]
+    for copy in copies:
+        copy.start()
+    for copy in copies:
+        copy.wait()
 
 
 def flip_kernel(f_ref, ft_ref):
@@ -203,76 +212,85 @@
     edge_ref[16:32] = low_ref[:, cols, :]
 
 
-def wgrad_kernel(
-    core_ref, ft_ref, gt_ref, gl_ref, ht_ref, hl_ref, hi_ref, ho_ref, ct_ref, cl_ref, edge_ref, em_ref, eo_ref,
-    g_ref, mine_ref, other_ref,
-):
+def wgrad_taps(ft_ref, block, a, mine_ref, other_ref):
+    for b in range(3):
+        blocks = [block(i, 2 - b + j) for i in range(2) for j in range(3)]
+        res = dot(ft_ref[...], jnp.concatenate(blocks, axis=0)).astype(BF)
+        mine_ref[1024 * b : 1024 * b + 1024] = res[:, :128]
+        other_ref[1024 * b : 1024 * b + 1024] = res[:, 128:]
+
+
+def wgrad_mid_kernel(core_ref, ft_ref, gt_ref, gl_ref, hi_ref, ho_ref, g_ref, mine_ref, other_ref):
     core = core_ref[0]
     inner = pl.ds(pl.multiple_of(64 - 64 * core, 16), 16)
     outer = pl.ds(pl.multiple_of(64 * core, 16), 16)
-    g_ref[0:16, 16:64, :] = ht_ref[...]
-    g_ref[16:32, 16:64, :] = gt_ref[...]
-    g_ref[32:48, 16:64, :] = gl_ref[...]
-    g_ref[48:64, 16:64, :] = hl_ref[...]
-    g_ref[0:16, inner, :] = swap(edge_ref[0:16])
-    g_ref[16:48, inner, :] = swap(hi_ref[...])
-    g_ref[48:64, inner, :] = swap(edge_ref[16:32])
-    g_ref[0:16, outer, :] = swap(ct_ref[...])
-    g_ref[16:48, outer, :] = swap(ho_ref[...])
-    g_ref[48:64, outer, :] = swap(cl_ref[...])
-    wgrad_part(ft_ref, g_ref, em_ref, eo_ref, mine_ref, other_ref, 0)
-
-
-def wgrad_part(ft_ref, g_ref, em_ref, eo_ref, mine_ref, other_ref, chip0):
-    mine_ref[:, 144:152, :] = em_ref[chip0 : chip0 + 32]
-    other_ref[:, 144:152, :] = eo_ref[chip0 : chip0 + 32]
-    begin, end = 144 * chip0, 144 * chip0 + 4608
-    for t in range(9):
-        first, last = max(begin, 1024 * t), min(end, 1024 * t + 1024)
-        if first >= last:
-            continue
-        row, col = (2 - t // 3) * D, (2 - t % 3) * D
-        blocks = [
-            px(g_ref, row + 16 * i, row + 16 * i + 16, col + 16 * j, col + 16 * j + 16)
-            for i in range(2)
-            for j in range(3)
-        ]
-        res = dot(ft_ref[first - 1024 * t : last - 1024 * t], jnp.concatenate(blocks, axis=0)).astype(BF)
-        at = first
-        while at < last:
-            chip, r = divmod(at, 144)
-            size = min(144 - r, last - at)
-            mine_ref[chip - chip0, r : r + size, :] = res[at - first : at - first + size, :128]
-            other_ref[chip - chip0, r : r + size, :] = res[at - first : at - first + size, 128:]
+    g_ref[0:16, 16:64, :] = gt_ref[...]
+    g_ref[16:32, 16:64, :] = gl_ref[...]
+    g_ref[:, inner, :] = swap(hi_ref[...])
+    g_ref[:, outer, :] = swap(ho_ref[...])
+    wgrad_taps(
+        ft_ref, lambda i, j: px(g_ref, 16 * i, 16 * i + 16, 16 * j, 16 * j + 16), 1, mine_ref, other_ref
+    )
+
+
+def wgrad_row_kernel(a, core_ref, ft_ref, g_ref, h_ref, c_ref, edge_ref, e_ref, row_ref, mine_ref, other_ref):
+    core = core_ref[0]
+    row_ref[:, 16:64, :] = h_ref[...]
+    row_ref[:, pl.ds(pl.multiple_of(64 - 64 * core, 16), 16), :] = swap(edge_ref[8 * (2 - a) : 8 * (2 - a) + 16])
+    row_ref[:, pl.ds(pl.multiple_of(64 * core, 16), 16), :] = swap(c_ref[...])
+
+    def block(i, j):
+        if a == 0:
+            return px(g_ref, 16, 32, 16 * j, 16 * j + 16) if i == 0 else px(row_ref, 0, 16, 16 * j, 16 * j + 16)
+        return px(g_ref, 0, 16, 16 * j, 16 * j + 16) if i == 1 else px(row_ref, 0, 16, 16 * j, 16 * j + 16)
+
+    wgrad_taps(ft_ref, block, a, mine_ref, other_ref)
+    if a == 0:
+        other_ref[3072:3584] = e_ref[...].reshape(512, 128)
+
+
+def add_kernel(m_ref, r_ref, out_ref):
+    @pl.loop(0, 12)
+    def _(k):
+        rows = pl.ds(pl.multiple_of(256 * k, 256), 256)
+        out_ref[rows] = (m_ref[rows].astype(F32) + r_ref[rows].astype(F32)).astype(BF)
+
+
+def gather_kernel(t0_ref, t1_ref, m2_ref, r2_ref, e_ref, r0_ref, _, out_ref, near, sems):
+    copies = []
+    for k in range(64):
+        at = 144 * k
+        while at < 144 * (k + 1):
+            part, row = divmod(at, 3072)
+            size = min(144 * (k + 1) - at, 3072 - row)
+            if part < 2:
+                value = (t0_ref, t1_ref)[part][row : row + size]
+            else:
+                value = (m2_ref[row : row + size].astype(F32) + r2_ref[row : row + size].astype(F32)).astype(BF)
+            near[k, at - 144 * k : at - 144 * k + size] = value
             at += size
-
-
-def wgrad_rest_kernel(ft_ref, g_ref, em_ref, eo_ref, mine_ref, other_ref):
-    wgrad_part(ft_ref, g_ref, em_ref, eo_ref, mine_ref, other_ref, 32)
-
-
-def add_kernel(m_ref, r_ref, out_ref):
-    @pl.loop(0, 16)
-    def _(k):
-        pair = pl.ds(2 * k, 2)
-        out_ref[pair] = (m_ref[pair].astype(F32) + r_ref[pair].astype(F32)).astype(BF)
-
-
-def add_rest_kernel(first_ref, m_ref, r_ref, out_ref):
-    @pl.loop(0, 16)
-    def _(k):
-        pair = pl.ds(2 * k, 2)
-        out_ref[pair] = first_ref[pair]
-        out_ref[pl.ds(32 + 2 * k, 2)] = (m_ref[pair].astype(F32) + r_ref[pair].astype(F32)).astype(BF)
-
-
-def sum_kernel(core_ref, in_ref, keep_ref, give_ref, bias_ref, acc):
-    acc[...] = in_ref[0].astype(F32)
-
-    @pl.loop(1, 64)
-    def _(k):
-        acc[...] += in_ref[k].astype(F32)
-
+        ends = e_ref[k].astype(F32) + r0_ref[3072 + 8 * k : 3080 + 8 * k].astype(F32)
+        near[k, 144:152] = ends.astype(BF)
+        if k % 8 == 7:
+            part = pl.ds(k - 7, 8)
+            copy = pltpu.make_async_copy(near.at[part], out_ref.at[part], sems.at[k // 8])
+            copy.start()
+            copies.append(copy)
+    for copy in copies:
+        copy.wait()
+
+
+def sum_kernel(core_ref, far_ref, keep_ref, give_ref, bias_ref, acc, near, sems):
+    copies = [
+        pltpu.make_async_copy(far_ref.at[pl.ds(16 * k, 16)], near.at[pl.ds(16 * k, 16)], sems.at[k]) for k in range(4)
+    ]
+    for copy in copies:
+        copy.start()
+    total = jnp.zeros((152, 128), F32)
+    for k, copy in enumerate(copies):
+        copy.wait()
+        total = lax.fori_loop(16 * k, 16 * k + 16, lambda n, t: t + near[n].astype(F32), total, unroll=4)
+    acc[...] = total
     bias_ref[...] = acc[148:149]
     for out, c in ((keep_ref, core_ref[0]), (give_ref, 1 - core_ref[0])):
         out[0:72] = acc[pl.ds(pl.multiple_of(72 * c, 8), 72)]
@@ -287,16 +305,17 @@
     proj_ref[...] = both[72:74]
 
 
-def fgrad_kernel(g_ref, mine_ref, other_ref, out_ref):
-    @pl.loop(0, 4)
-    def _(k):
+def fgrad_kernel(top_ref, mid_ref, low_ref, mine_ref, other_ref, out_ref):
+    for k in range(4):
         acc = None
-        for t in range(9):
-            row, col = (2 - t // 3) * D, (2 - t % 3) * D
-            win = g_ref[pl.ds(row + 8 * k, 8), col : col + 48, :].reshape(384, 256)
-            term = dot(win, tap(mine_ref, other_ref, t // 3, t % 3), NT)
-            acc = term if acc is None else acc + term
-        out_ref[pl.ds(8 * k, 8)] = acc.astype(BF).reshape(8, 48, 1024)
+        for a in range(3):
+            row = 8 * k + (2 - a) * 16
+            ref, row = ((top_ref, row), (mid_ref, row - 16), (mid_ref, row - 16), (low_ref, row - 48))[row // 16]
+            for b in range(3):
+                win = px(ref, row, row + 8, (2 - b) * D, (2 - b) * D + 48)
+                term = dot(win, tap(mine_ref, other_ref, a, b), NT)
+                acc = term if acc is None else acc + term
+        out_ref[8 * k : 8 * k + 8] = acc.astype(BF).reshape(8, 48, 1024)
 
 
 def body(features, conv_weight, conv_bias, proj_weight, cotangent):
@@ -315,15 +334,16 @@
     def array(shape, dtype=BF):
         return jax.ShapeDtypeStruct(shape, dtype)
 
-    def call(kernel, name, outs, args, flops, size, scratch=()):
-        specs = [smem if a is core_s else vmem() for a in args]
+    def call(kernel, name, outs, args, flops, size, scratch=(), far=(), limit=VMEM_LIMIT, reuse=None):
+        specs = [smem if a is core_s else any_space() if any(a is f for f in far) else vmem() for a in args]
         return pl.pallas_call(
             kernel,
             out_shape=tuple(outs),
             in_specs=specs,
-            out_specs=(vmem(),) * len(outs),
+            out_specs=((vmem() if limit == VMEM_LIMIT and reuse is None else any_space()),) * len(outs),
             scratch_shapes=list(scratch),
-            compiler_params=params(),
+            input_output_aliases={} if reuse is None else {reuse: 0},
+            compiler_params=params(limit),
             cost_estimate=cost(int(flops), int(size)),
             name=name,
         )(*args)
@@ -342,7 +362,8 @@
         [core_s, keep, got],
         1e5,
         3e6,
-        [pltpu.VMEM((152, 128), F32)],
+        [pltpu.VMEM((152, 128), F32), pltpu.VMEM((8, 152, 128), BF), pltpu.SemaphoreType.DMA((8,))],
+        limit=40 * 1024 * 1024,
     )
     mine = lax.all_to_all(spread, CHIPS, 0, 0)
     (ft,) = call(flip_kernel, "flip", [array((1024, 1536))], [features], 1e6, 6e6)
@@ -403,26 +424,58 @@
         4e6,
         [pltpu.VMEM((256, 256), F32), pltpu.VMEM((64, 8, 128), F32)],
     )
-    h_top, h_low, c_top, c_low, h_outer = lax.optimization_barrier((h_top, h_low, c_top, c_low, h_outer))
+    part = array((3072, 128))
+    g_mid, m1, o1 = call(
+        wgrad_mid_kernel,
+        "wgrad1",
+        [array((32, 80, 256)), part, part],
+        [core_s, ft, g_top, g_low, h_inner, h_outer],
+        2.4e9,
+        6e6,
+    )
+    r1 = send(o1, 0, INNER)
+    h_top, h_low, c_top, c_low, e_mine, e_other, m1 = lax.optimization_barrier(
+        (h_top, h_low, c_top, c_low, e_mine, e_other, m1)
+    )
     (edge,) = call(edge_kernel, "edge", [array(side)], [core_s, h_top, h_low], 1e6, 1e6)
     edge = send(edge, 0, INNER)
-    half = array((32, 152, 128))
-    g, m1, o1 = call(
-        wgrad_kernel,
-        "wgrad",
-        [array((64, 80, 256)), half, half],
-        [core_s, ft, g_top, g_low, h_top, h_low, h_inner, h_outer, c_top, c_low, edge, e_mine, e_other],
-        3.6e9,
-        8e6,
-    )
-    r1 = send(o1, 0, INNER)
-    m2, o2 = call(wgrad_rest_kernel, "wgrad2", [half, half], [ft, g, e_mine, e_other], 3.6e9, 8e6)
+    row, long = array((16, 80, 256)), array((3584, 128))
+    g_bottom, m0, o0 = call(
+        functools.partial(wgrad_row_kernel, 0),
+        "wgrad0",
+        [row, part, long],
+        [core_s, ft, g_mid, h_low, c_low, edge, e_other],
+        2.4e9,
+        6e6,
+    )
+    r0 = send(o0, 0, INNER)
+    g_upper, m2, o2 = call(
+        functools.partial(wgrad_row_kernel, 2),
+        "wgrad2",
+        [row, part, part],
+        [core_s, ft, g_mid, h_top, c_top, edge, e_mine],
+        2.4e9,
+        6e6,
+    )
     r2 = send(o2, 0, INNER)
-    (t1,) = call(add_kernel, "add", [half], [m1, r1], 1e6, 4e6)
-    (total,) = call(add_rest_kernel, "add2", [array((64, 152, 128))], [t1, m2, r2], 1e6, 7e6)
+    (t1,) = call(add_kernel, "add1", [part], [m1, r1], 1e6, 4e6)
+    (t0,) = call(add_kernel, "add0", [part], [m0, r0], 1e6, 4e6)
+    (total,) = call(
+        gather_kernel,
+        "gather",
+        [array((64, 152, 128))],
+        [t0, t1, m2, r2, e_mine, r0, spread],
+        1e6,
+        7e6,
+        [pltpu.VMEM((64, 152, 128), BF), pltpu.SemaphoreType.DMA((8,))],
+        far=(spread,),
+        reuse=6,
+    )
     pieces = lax.all_to_all(total, CHIPS, 0, 0)
 
-    (features_grad,) = call(fgrad_kernel, "fgrad", [array((32, 48, 1024))], [g, mine, other], 7.2e9, 12e6)
+    (features_grad,) = call(
+        fgrad_kernel, "fgrad", [array((32, 48, 1024))], [g_upper, g_mid, g_bottom, mine, other], 7.2e9, 12e6
+    )
 
     pack = array((80, 128), F32)
     keep, give, bias_row = call(
@@ -432,7 +485,8 @@
         [core_s, pieces],
         1e6,
         3e6,
-        [pltpu.VMEM((152, 128), F32)],
+        [pltpu.VMEM((152, 128), F32), pltpu.VMEM((64, 152, 128), BF), pltpu.SemaphoreType.DMA((4,))],
+        far=(pieces,),
     )
     got = send(give, 0, INNER)
     conv_grad, proj_grad = call(

time: 176 us -> 170 us (0.966)
  waiting for transfers between devices: 66.7 us -> 62.8 us
  local copies, waits for them, and re-layouts: 14.5 us -> 11.8 us
    ppermute x18 -> x19, waiting for transfers between devices: 20.2 us -> 16 us  [send(): return lax.ppermute(x, ALL, perm)]
    unnamed x30, local copies, waits for them, and re-layouts: 13.9 us -> 11.2 us
    pallas_call x17 -> x19, Pallas kernels: 33.6 us -> 34.9 us  [call(): pl.pallas_call(kernel, out_shape=tuple(outs), in_specs=specs, out_specs=(...]
    ppermute x18 -> x19, starting transfers between devices: 34.2 us -> 34.5 us  [send(): return lax.ppermute(x, ALL, perm)]
  transfers between devices with their start and end apart: 20 -> 21, of which waited for: 10 -> 11; matrix products, arithmetic and copies ran while one was open for 0% -> 0% of each run, Pallas kernels for 12% -> 14%
where the time goes in v4:
time: 170 us; the launch traced here: 169 us
  waiting for transfers between devices  62.8 us (37%)
  starting transfers between devices  58.6 us (34%)
  Pallas kernels  34.9 us (21%)
  local copies, waits for them, and re-layouts  11.8 us (7%)
    pallas_call x19, Pallas kernels, call(): pl.pallas_call(kernel, out_shape=tuple(outs), in_specs=specs, out_specs=(...  34.9 us
    ppermute x19, starting transfers between devices, send(): return lax.ppermute(x, ALL, perm)  34.5 us
    all_to_all x1, waiting for transfers between devices, body(): mine = lax.all_to_all(spread, CHIPS, 0, 0)  27.9 us
    all_to_all x1, waiting for transfers between devices, body(): pieces = lax.all_to_all(total, CHIPS, 0, 0)  18.9 us
    ppermute x19, waiting for transfers between devices, send(): return lax.ppermute(x, ALL, perm)  16 us
    all_to_all x1, starting transfers between devices, body(): pieces = lax.all_to_all(total, CHIPS, 0, 0)  12.9 us
    all_to_all x1, starting transfers between devices, body(): mine = lax.all_to_all(spread, CHIPS, 0, 0)  11.2 us
    unnamed x30, local copies, waits for them, and re-layouts  11.2 us
  transfers between devices with their start and end apart: 21, of which 11 were waited for; matrix products, arithmetic and copies ran while one was open for 0% of the time, Pallas kernels for 14%

profile of v4, /device:TPU:1, one launch (start us, length us, event | category | flops | bytes accessed | tf_op | source)
XLA Modules:
  0.0 169.1 jit_solution(10275285883007632303)
XLA Ops:
  0.6 0.8 copy-done.5
  1.4 0.7 copy-done.6
  2.1 1.5 collective-permute-start
  3.6 0.8 collective-permute-done.got_ref
  4.4 1.5 spread.1._
  6.0 11.2 %all-to-all-start = ((bf16[64,152,128]{2,1,0:T(8,128)(2,1)}), bf16[64,152,128]{2,1,0:T(8,128)(2,1)S(1)}, u32[]{:S(2)}, u32[]{:S(2)}) async-start(bf16[64,152,128]{2,1,0:T(8,128)(2,1)} %spread.1._), calls=%async_computation | async-start | bytes 4980736 | tf_op jit(solution)/shard_map/all_to_all | solution.py:368
  17.2 1.9 %copy-done = bf16[32,48,1024]{2,1,0:T(8,128)(2,1)S(1)} copy-done((bf16[32,48,1024]{2,1,0:T(8,128)(2,1)S(1)}, bf16[32,48,1024]{2,1,0:T(8,128)(2,1)}, u32[]{:S(2)}) %copy-start) | copy-done | bytes 3145752
  19.1 0.9 flip.1.ft_ref
  20.0 1.7 copy-done.3
  21.7 27.9 %all-to-all-done.mine_ref = bf16[64,152,128]{2,1,0:T(8,128)(2,1)S(1)} async-done(((bf16[64,152,128]{2,1,0:T(8,128)(2,1)}), bf16[64,152,128]{2,1,0:T(8,128)(2,1)S(1)}, u32[]{:S(2)}, u32[]{:S(2)}) %all-to-all-start) | async-done | bytes 2490400 | tf_op jit(solution)/shard_map/all_to_all | solution.py:368
  49.5 2.3 %collective-permute-start.1 = (bf16[64,152,128]{2,1,0:T(8,128)(2,1)S(1)}, bf16[64,152,128]{2,1,0:T(8,128)(2,1)S(1)}, u32[]{:S(2)}, u32[]{:S(2)}) collective-permute-start(bf16[64,152,128]{2,1,0:T(8,128)(2,1)S(1)} %all-to-all-done.mine_ref), channel_id=1, source_target_pairs={{0,1},{1,0},{2,3},{3,2},{4,5},{5,4},{6,7},{7,6},{8,9},{9,8},{10,11... | collective-permute-start | bytes 7471112 | tf_op jit(solution)/shard_map/ppermute | solution.py:332
  51.9 4.3 %collective-permute-done.1.other_ref = bf16[64,152,128]{2,1,0:T(8,128)(2,1)S(1)} collective-permute-done((bf16[64,152,128]{2,1,0:T(8,128)(2,1)S(1)}, bf16[64,152,128]{2,1,0:T(8,128)(2,1)S(1)}, u32[]{:S(2)}, u32[]{:S(2)}) %collective-permute-start.1) | collective-permute-done | bytes 2490400 | tf_op jit(solution)/shard_map/ppermute | solution.py:332
  56.2 1.9 %copy-done.1 = bf16[32,48,1024]{2,1,0:T(8,128)(2,1)S(1)} copy-done((bf16[32,48,1024]{2,1,0:T(8,128)(2,1)S(1)}, bf16[32,48,1024]{2,1,0:T(8,128)(2,1)}, u32[]{:S(2)}) %copy-start.1) | copy-done | bytes 3145752
  58.1 3.8 %halo.1 = (bf16[16,48,256]{2,1,0:T(8,128)(2,1)S(1)}, bf16[16,48,256]{2,1,0:T(8,128)(2,1)S(1)}, bf16[64,16,256]{2,1,0:T(8,128)(2,1)S(1)}, bf16[32,16,256]{2,1,0:T...) custom-call(s32[1]{0:T(128)} %bitcast.core_ref, ...), custom_call_target="tpu_custom_call" | custom-call | flops 3500000000 | bytes 9000000 | tf_op jit(solution)/shard_map/halo/pallas_call | solution.py:339
  62.4 1.5 collective-permute-done.2.inner_ref
  64.0 2.5 %collective-permute-start.3 = (bf16[16,48,256]{2,1,0:T(8,128)(2,1)S(1)}, bf16[16,48,256]{2,1,0:T(8,128)(2,1)S(1)}, u32[]{:S(2)}, u32[]{:S(2)}) collective-permute-start(bf16[16,48,256]{2,1,0:T(8,128)(2,1)S(1)} %get-tuple-element.62), channel_id=1, source_target_pairs={{0,8},{1,9},{2,10},{3,11},{4,12},{5,13},{6,14},{7,15},{8,16},{9,17... | collective-permute-start | bytes 1179656 | tf_op jit(solution)/shard_map/ppermute | solution.py:332
  66.6 1.3 collective-permute-start.4
  67.9 5.6 %collective-permute-start.6 = (bf16[16,16,256]{2,1,0:T(8,128)(2,1)S(1)}, bf16[16,16,256]{2,1,0:T(8,128)(2,1)S(1)}, u32[]{:S(2)}, u32[]{:S(2)}) collective-permute-start(bf16[16,16,256]{2,1,0:T(8,128)(2,1)S(1)} %get-tuple-element.65), channel_id=1, source_target_pairs={{1,10},{2,9},{3,12},{4,11},{5,14},{6,13},{9,18},{10,17},{11,20},{1... | collective-permute-start | bytes 393224 | tf_op jit(solution)/shard_map/ppermute | solution.py:332
  73.5 1.3 collective-permute-start.7
  74.8 1.9 %collective-permute-start.5 = (bf16[32,16,256]{2,1,0:T(8,128)(2,1)S(1)}, bf16[32,16,256]{2,1,0:T(8,128)(2,1)S(1)}, u32[]{:S(2)}, u32[]{:S(2)}) collective-permute-start(bf16[32,16,256]{2,1,0:T(8,128)(2,1)S(1)} %get-tuple-element.64), channel_id=1, source_target_pairs={{1,2},{2,1},{3,4},{4,3},{5,6},{6,5},{9,10},{10,9},{11,12},{12,11},... | collective-permute-start | bytes 786440 | tf_op jit(solution)/shard_map/ppermute | solution.py:332
  76.7 4.3 %own.1 = (f32[32,48,256]{2,1,0:T(8,128)S(1)}, f32[32,48,256]{2,1,0:T(8,128)S(1)}) custom-call(s32[1]{0:T(128)} %bitcast.core_ref, bf16[32,48,1024]{2,1,0:T(8,128)(2,1)S(1)} %copy-done.2, bf16[64,152,128]{2,1,0:T(8,128)(2,1)S(1)} %all-to-all-done.mine_ref, bf16[64,152,128]{2,1,0:T(8,128)(2,1)S(1)} %collective-permute-done.1.other_ref, ...), custom_call_target="tpu_custom_call" | custom-call | flops 4000000000 | bytes 12000000 | tf_op jit(solution)/shard_map/own/pallas_call | solution.py:339
  81.0 2.0 %collective-permute-done.7.cs_ref = bf16[16,16,256]{2,1,0:T(8,128)(2,1)S(1)} collective-permute-done((bf16[16,16,256]{2,1,0:T(8,128)(2,1)S(1)}, bf16[16,16,256]{2,1,0:T(8,128)(2,1)S(1)}, u32[]{:S(2)}, u32[]{:S(2)}) %collective-permute-start.7) | collective-permute-done | bytes 131104 | tf_op jit(solution)/shard_map/ppermute | solution.py:332
  83.0 0.9 collective-permute-done.5.outer_ref
  83.9 1.1 point.1
  85.1 1.9 %collective-permute-start.9 = (bf16[32,16,256]{2,1,0:T(8,128)(2,1)S(1)}, bf16[32,16,256]{2,1,0:T(8,128)(2,1)S(1)}, u32[]{:S(2)}, u32[]{:S(2)}) collective-permute-start(bf16[32,16,256]{2,1,0:T(8,128)(2,1)S(1)} %get-tuple-element.73), channel_id=1, source_target_pairs={{1,2},{2,1},{3,4},{4,3},{5,6},{6,5},{9,10},{10,9},{11,12},{12,11},... | collective-permute-start | bytes 786440 | tf_op jit(solution)/shard_map/ppermute | solution.py:332
  87.0 1.3 collective-permute-start.11
  88.3 4.9 %collective-permute-start.10 = (bf16[16,48,256]{2,1,0:T(8,128)(2,1)S(1)}, bf16[16,48,256]{2,1,0:T(8,128)(2,1)S(1)}, u32[]{:S(2)}, u32[]{:S(2)}) collective-permute-start(bf16[16,48,256]{2,1,0:T(8,128)(2,1)S(1)} %get-tuple-element.69.low_ref.gl_ref), channel_id=1, source_target_pairs={{0,8},{1,9},{2,10},{3,11},{4,12},{5,13},{6,14},{7,15},{8,16},{9,17... | collective-permute-start | bytes 1179656 | tf_op jit(solution)/shard_map/ppermute | solution.py:332
  93.2 1.5 proj.1
  94.7 4.5 %collective-permute-start.12 = (bf16[16,16,256]{2,1,0:T(8,128)(2,1)S(1)}, bf16[16,16,256]{2,1,0:T(8,128)(2,1)S(1)}, u32[]{:S(2)}, u32[]{:S(2)}) collective-permute-start(bf16[16,16,256]{2,1,0:T(8,128)(2,1)S(1)} %get-tuple-element.75), channel_id=1, source_target_pairs={{1,10},{2,9},{3,12},{4,11},{5,14},{6,13},{9,18},{10,17},{11,20},{1... | collective-permute-start | bytes 393224 | tf_op jit(solution)/shard_map/ppermute | solution.py:332
  99.2 1.5 collective-permute-start.13
  100.7 2.7 %wgrad1.1 = (bf16[32,80,256]{2,1,0:T(8,128)(2,1)S(1)}, bf16[3072,128]{1,0:T(8,128)(2,1)S(1)}, bf16[3072,128]{1,0:T(8,128)(2,1)S(1)}) custom-call(s32[1]{0:T(128)} %bitcast.core_ref, bf16[1024,1536]{1,0:T(8,128)(2,1)S(1)} %copy-done.4, bf16[16,48,256]{2,1,0:T(8,128)(2,1)S(1)} %get-tuple-element.68.top_ref.gt_ref, ...), custom_call_target="tpu_custom_call" | custom-call | flops 2400000000 | bytes 6000000 | tf_op jit(solution)/shard_map/wgrad1/pallas_call | solution.py:339
  103.5 3.9 %collective-permute-done.13.c_ref = bf16[16,16,256]{2,1,0:T(8,128)(2,1)S(1)} collective-permute-done((bf16[16,16,256]{2,1,0:T(8,128)(2,1)S(1)}, bf16[16,16,256]{2,1,0:T(8,128)(2,1)S(1)}, u32[]{:S(2)}, u32[]{:S(2)}) %collective-permute-start.13) | collective-permute-done | bytes 131104 | tf_op jit(solution)/shard_map/ppermute | solution.py:332
  107.5 0.5 collective-permute-start.16
  108.0 1.0 collective-permute-done.14.edge_ref
  109.0 2.6 %wgrad0.1 = (bf16[16,80,256]{2,1,0:T(8,128)(2,1)S(1)}, bf16[3072,128]{1,0:T(8,128)(2,1)S(1)}, bf16[3584,128]{1,0:T(8,128)(2,1)S(1)}) custom-call(s32[1]{0:T(128)} %bitcast.core_ref, bf16[1024,1536]{1,0:T(8,128)(2,1)S(1)} %copy-done.4, bf16[32,80,256]{2,1,0:T(8,128)(2,1)S(1)} %get-tuple-element.74.g_ref.mid_ref, ...), custom_call_target="tpu_custom_call" | custom-call | flops 2400000000 | bytes 6000000 | tf_op jit(solution)/shard_map/wgrad0/pallas_call | solution.py:339
  111.9 2.6 %wgrad2.1 = (bf16[16,80,256]{2,1,0:T(8,128)(2,1)S(1)}, bf16[3072,128]{1,0:T(8,128)(2,1)S(1)}, bf16[3072,128]{1,0:T(8,128)(2,1)S(1)}) custom-call(s32[1]{0:T(128)} %bitcast.core_ref, bf16[1024,1536]{1,0:T(8,128)(2,1)S(1)} %copy-done.4, bf16[32,80,256]{2,1,0:T(8,128)(2,1)S(1)} %get-tuple-element.74.g_ref.mid_ref, ...), custom_call_target="tpu_custom_call" | custom-call | flops 2400000000 | bytes 6000000 | tf_op jit(solution)/shard_map/wgrad2/pallas_call | solution.py:339
  115.7 1.2 collective-permute-done.17.r2_ref
  116.9 1.5 gather.1
  118.5 12.9 %all-to-all-start.1 = ((bf16[64,152,128]{2,1,0:T(8,128)(2,1)}), bf16[64,152,128]{2,1,0:T(8,128)(2,1)}, u32[]{:S(2)}, u32[]{:S(2)}) async-start(bf16[64,152,128]{2,1,0:T(8,128)(2,1)} %gather.1), calls=%async_computation.1 | async-start | bytes 4980736 | tf_op jit(solution)/shard_map/all_to_all | solution.py:474
  131.4 1.7 %copy-done.8 = bf16[64,152,128]{2,1,0:T(8,128)(2,1)S(1)} copy-done((bf16[64,152,128]{2,1,0:T(8,128)(2,1)S(1)}, bf16[64,152,128]{2,1,0:T(8,128)(2,1)}, u32[]{:S(2)}) %copy-start.8) | copy-done | bytes 2490392
  133.1 1.3 copy-done.12
  134.4 1.1 copy-done.14
  135.5 9.2 %fgrad.1 = bf16[32,48,1024]{2,1,0:T(8,128)(2,1)} custom-call(bf16[16,80,256]{2,1,0:T(8,128)(2,1)S(1)} %copy-done.14, bf16[32,80,256]{2,1,0:T(8,128)(2,1)S(1)} %copy-done.12, bf16[16,80,256]{2,1,0:T(8,128)(2,1)S(1)} %get-tuple-element.87.low_ref, bf16[64,152,128]{2,1,0:T(8,128)(2,1)S(1)} %all-to-all-done.mine_ref, bf16[64,152,128]{2,1,0:T(8,128)(2,1)S(1)} %copy-done.8), custom_call_target="tpu_custom_call" | custom-call | flops 7200000000 | bytes 12000000 | tf_op jit(solution)/shard_map/fgrad/pallas_call | solution.py:339
  144.7 18.9 %all-to-all-done.1.far_ref = bf16[64,152,128]{2,1,0:T(8,128)(2,1)} async-done(((bf16[64,152,128]{2,1,0:T(8,128)(2,1)}), bf16[64,152,128]{2,1,0:T(8,128)(2,1)}, u32[]{:S(2)}, u32[]{:S(2)}) %all-to-all-start.1) | async-done | bytes 2490400 | tf_op jit(solution)/shard_map/all_to_all | solution.py:474
  163.5 1.8 %sum.1 = (f32[80,128]{1,0:T(8,128)S(1)}, f32[80,128]{1,0:T(8,128)S(1)}, f32[1,128]{1,0:T(1,128)S(1)}) custom-call(s32[1]{0:T(128)} %bitcast.core_ref, bf16[64,152,128]{2,1,0:T(8,128)(2,1)} %all-to-all-done.1.far_ref), custom_call_target="tpu_custom_call" | custom-call | flops 1000000 | bytes 3000000 | tf_op jit(solution)/shard_map/sum/pallas_call | solution.py:339
  165.3 2.2 %collective-permute-start.18 = (f32[80,128]{1,0:T(8,128)S(1)}, f32[80,128]{1,0:T(8,128)S(1)}, u32[]{:S(2)}, u32[]{:S(2)}) collective-permute-start(f32[80,128]{1,0:T(8,128)S(1)} %get-tuple-element.95), channel_id=1, source_target_pairs={{0,1},{1,0},{2,3},{3,2},{4,5},{5,4},{6,7},{7,6},{8,9},{9,8},{10,11... | collective-permute-start | bytes 122888 | tf_op jit(solution)/shard_map/ppermute | solution.py:332
  167.5 0.6 dynamic-slice_bitcast_fusion
  168.4 0.6 join.1
  (44 shorter events, 2.5 us)
Async XLA Ops:
  0.6 0.8 copy-start.5
  1.4 0.7 copy-start.6
  2.1 2.3 %collective-permute-start = (bf16[80,128]{1,0:T(8,128)(2,1)S(1)}, bf16[80,128]{1,0:T(8,128)(2,1)S(1)}, u32[]{:S(2)}, u32[]{:S(2)}) collective-permute-start(bf16[80,128]{1,0:T(8,128)(2,1)S(1)} %get-tuple-element.53), channel_id=1, source_target_pairs={{0,1},{1,0},{2,3},{3,2},{4,5},{5,4},{6,7},{7,6},{8,9},{9,8},{10,11... | collective-permute-start | bytes 61448 | tf_op jit(solution)/shard_map/ppermute | solution.py:332
  6.0 43.5 %all-to-all-start = ((bf16[64,152,128]{2,1,0:T(8,128)(2,1)}), bf16[64,152,128]{2,1,0:T(8,128)(2,1)S(1)}, u32[]{:S(2)}, u32[]{:S(2)}) async-start(bf16[64,152,128]{2,1,0:T(8,128)(2,1)} %spread.1._), calls=%async_computation | async-start | bytes 4980736 | tf_op jit(solution)/shard_map/all_to_all | solution.py:368
  17.2 1.9 %copy-start = (bf16[32,48,1024]{2,1,0:T(8,128)(2,1)S(1)}, bf16[32,48,1024]{2,1,0:T(8,128)(2,1)}, u32[]{:S(2)}) copy-start(bf16[32,48,1024]{2,1,0:T(8,128)(2,1)} %f_ref.5) | copy-start | bytes 9437188
  20.0 1.7 copy-start.3
  49.5 6.7 %collective-permute-start.1 = (bf16[64,152,128]{2,1,0:T(8,128)(2,1)S(1)}, bf16[64,152,128]{2,1,0:T(8,128)(2,1)S(1)}, u32[]{:S(2)}, u32[]{:S(2)}) collective-permute-start(bf16[64,152,128]{2,1,0:T(8,128)(2,1)S(1)} %all-to-all-done.mine_ref), channel_id=1, source_target_pairs={{0,1},{1,0},{2,3},{3,2},{4,5},{5,4},{6,7},{7,6},{8,9},{9,8},{10,11... | collective-permute-start | bytes 7471112 | tf_op jit(solution)/shard_map/ppermute | solution.py:332
  56.2 1.9 %copy-start.1 = (bf16[32,48,1024]{2,1,0:T(8,128)(2,1)S(1)}, bf16[32,48,1024]{2,1,0:T(8,128)(2,1)}, u32[]{:S(2)}) copy-start(bf16[32,48,1024]{2,1,0:T(8,128)(2,1)} %f_ref.5) | copy-start | bytes 9437188
  58.1 18.6 %copy-start.7 = (bf16[64,152,128]{2,1,0:T(8,128)(2,1)}, bf16[64,152,128]{2,1,0:T(8,128)(2,1)S(1)}, u32[]{:S(2)}) copy-start(bf16[64,152,128]{2,1,0:T(8,128)(2,1)S(1)} %collective-permute-done.1.other_ref) | copy-start | bytes 7471108
  58.1 18.6 %copy-start.2 = (bf16[32,48,1024]{2,1,0:T(8,128)(2,1)S(1)}, bf16[32,48,1024]{2,1,0:T(8,128)(2,1)}, u32[]{:S(2)}) copy-start(bf16[32,48,1024]{2,1,0:T(8,128)(2,1)} %f_ref.5) | copy-start | bytes 9437188
  58.1 18.6 %copy-start.9 = (bf16[32,48,256]{2,1,0:T(8,128)(2,1)S(1)}, bf16[32,48,256]{2,1,0:T(8,128)(2,1)}, u32[]{:S(2)}) copy-start(bf16[32,48,256]{2,1,0:T(8,128)(2,1)} %cot_ref.3) | copy-start | bytes 2359300
  58.1 18.6 %copy-start.10 = (f32[256]{0:T(256)S(1)}, f32[256]{0:T(256)}, u32[]{:S(2)}) copy-start(f32[256]{0:T(256)} %param.7) | copy-start | bytes 3076
  61.9 2.0 %collective-permute-start.2 = (bf16[64,16,256]{2,1,0:T(8,128)(2,1)S(1)}, bf16[64,16,256]{2,1,0:T(8,128)(2,1)S(1)}, u32[]{:S(2)}, u32[]{:S(2)}) collective-permute-start(bf16[64,16,256]{2,1,0:T(8,128)(2,1)S(1)} %get-tuple-element.61), channel_id=1, source_target_pairs={{0,1},{1,0},{2,3},{3,2},{4,5},{5,4},{6,7},{7,6},{8,9},{9,8},{10,11... | collective-permute-start | bytes 1572872 | tf_op jit(solution)/shard_map/ppermute | solution.py:332
  64.0 19.8 %collective-permute-start.3 = (bf16[16,48,256]{2,1,0:T(8,128)(2,1)S(1)}, bf16[16,48,256]{2,1,0:T(8,128)(2,1)S(1)}, u32[]{:S(2)}, u32[]{:S(2)}) collective-permute-start(bf16[16,48,256]{2,1,0:T(8,128)(2,1)S(1)} %get-tuple-element.62), channel_id=1, source_target_pairs={{0,8},{1,9},{2,10},{3,11},{4,12},{5,13},{6,14},{7,15},{8,16},{9,17... | collective-permute-start | bytes 1179656 | tf_op jit(solution)/shard_map/ppermute | solution.py:332
  66.6 17.3 %collective-permute-start.4 = (bf16[16,48,256]{2,1,0:T(8,128)(2,1)S(1)}, bf16[16,48,256]{2,1,0:T(8,128)(2,1)S(1)}, u32[]{:S(2)}, u32[]{:S(2)}) collective-permute-start(bf16[16,48,256]{2,1,0:T(8,128)(2,1)S(1)} %get-tuple-element.63), channel_id=1, source_target_pairs={{8,0},{9,1},{10,2},{11,3},{12,4},{13,5},{14,6},{15,7},{16,8},{17,9... | collective-permute-start | bytes 1179656 | tf_op jit(solution)/shard_map/ppermute | solution.py:332
  67.9 13.2 %collective-permute-start.6 = (bf16[16,16,256]{2,1,0:T(8,128)(2,1)S(1)}, bf16[16,16,256]{2,1,0:T(8,128)(2,1)S(1)}, u32[]{:S(2)}, u32[]{:S(2)}) collective-permute-start(bf16[16,16,256]{2,1,0:T(8,128)(2,1)S(1)} %get-tuple-element.65), channel_id=1, source_target_pairs={{1,10},{2,9},{3,12},{4,11},{5,14},{6,13},{9,18},{10,17},{11,20},{1... | collective-permute-start | bytes 393224 | tf_op jit(solution)/shard_map/ppermute | solution.py:332
  73.5 9.5 %collective-permute-start.7 = (bf16[16,16,256]{2,1,0:T(8,128)(2,1)S(1)}, bf16[16,16,256]{2,1,0:T(8,128)(2,1)S(1)}, u32[]{:S(2)}, u32[]{:S(2)}) collective-permute-start(bf16[16,16,256]{2,1,0:T(8,128)(2,1)S(1)} %get-tuple-element.66), channel_id=1, source_target_pairs={{9,2},{10,1},{11,4},{12,3},{13,6},{14,5},{17,10},{18,9},{19,12},{2... | collective-permute-start | bytes 393224 | tf_op jit(solution)/shard_map/ppermute | solution.py:332
  74.8 9.1 %collective-permute-start.5 = (bf16[32,16,256]{2,1,0:T(8,128)(2,1)S(1)}, bf16[32,16,256]{2,1,0:T(8,128)(2,1)S(1)}, u32[]{:S(2)}, u32[]{:S(2)}) collective-permute-start(bf16[32,16,256]{2,1,0:T(8,128)(2,1)S(1)} %get-tuple-element.64), channel_id=1, source_target_pairs={{1,2},{2,1},{3,4},{4,3},{5,6},{6,5},{9,10},{10,9},{11,12},{12,11},... | collective-permute-start | bytes 786440 | tf_op jit(solution)/shard_map/ppermute | solution.py:332
  85.0 14.3 %collective-permute-start.8 = (bf16[32,16,256]{2,1,0:T(8,128)(2,1)S(1)}, bf16[32,16,256]{2,1,0:T(8,128)(2,1)S(1)}, u32[]{:S(2)}, u32[]{:S(2)}) collective-permute-start(bf16[32,16,256]{2,1,0:T(8,128)(2,1)S(1)} %get-tuple-element.72), channel_id=1, source_target_pairs={{0,1},{1,0},{2,3},{3,2},{4,5},{5,4},{6,7},{7,6},{8,9},{9,8},{10,11... | collective-permute-start | bytes 786440 | tf_op jit(solution)/shard_map/ppermute | solution.py:332
  85.1 15.7 %collective-permute-start.9 = (bf16[32,16,256]{2,1,0:T(8,128)(2,1)S(1)}, bf16[32,16,256]{2,1,0:T(8,128)(2,1)S(1)}, u32[]{:S(2)}, u32[]{:S(2)}) collective-permute-start(bf16[32,16,256]{2,1,0:T(8,128)(2,1)S(1)} %get-tuple-element.73), channel_id=1, source_target_pairs={{1,2},{2,1},{3,4},{4,3},{5,6},{6,5},{9,10},{10,9},{11,12},{12,11},... | collective-permute-start | bytes 786440 | tf_op jit(solution)/shard_map/ppermute | solution.py:332
  87.0 20.4 %collective-permute-start.11 = (bf16[16,48,256]{2,1,0:T(8,128)(2,1)S(1)}, bf16[16,48,256]{2,1,0:T(8,128)(2,1)S(1)}, u32[]{:S(2)}, u32[]{:S(2)}) collective-permute-start(bf16[16,48,256]{2,1,0:T(8,128)(2,1)S(1)} %get-tuple-element.68.top_ref.gt_ref), channel_id=1, source_target_pairs={{8,0},{9,1},{10,2},{11,3},{12,4},{13,5},{14,6},{15,7},{16,8},{17,9... | collective-permute-start | bytes 1179656 | tf_op jit(solution)/shard_map/ppermute | solution.py:332
  88.3 19.1 %collective-permute-start.10 = (bf16[16,48,256]{2,1,0:T(8,128)(2,1)S(1)}, bf16[16,48,256]{2,1,0:T(8,128)(2,1)S(1)}, u32[]{:S(2)}, u32[]{:S(2)}) collective-permute-start(bf16[16,48,256]{2,1,0:T(8,128)(2,1)S(1)} %get-tuple-element.69.low_ref.gl_ref), channel_id=1, source_target_pairs={{0,8},{1,9},{2,10},{3,11},{4,12},{5,13},{6,14},{7,15},{8,16},{9,17... | collective-permute-start | bytes 1179656 | tf_op jit(solution)/shard_map/ppermute | solution.py:332
  93.2 7.5 %copy-start.4 = (bf16[1024,1536]{1,0:T(8,128)(2,1)S(1)}, bf16[1024,1536]{1,0:T(8,128)(2,1)}, u32[]{:S(2)}) copy-start(bf16[1024,1536]{1,0:T(8,128)(2,1)} %copy-done.3) | copy-start | bytes 9437188
  94.7 8.8 %collective-permute-start.12 = (bf16[16,16,256]{2,1,0:T(8,128)(2,1)S(1)}, bf16[16,16,256]{2,1,0:T(8,128)(2,1)S(1)}, u32[]{:S(2)}, u32[]{:S(2)}) collective-permute-start(bf16[16,16,256]{2,1,0:T(8,128)(2,1)S(1)} %get-tuple-element.75), channel_id=1, source_target_pairs={{1,10},{2,9},{3,12},{4,11},{5,14},{6,13},{9,18},{10,17},{11,20},{1... | collective-permute-start | bytes 393224 | tf_op jit(solution)/shard_map/ppermute | solution.py:332
  99.2 8.2 %collective-permute-start.13 = (bf16[16,16,256]{2,1,0:T(8,128)(2,1)S(1)}, bf16[16,16,256]{2,1,0:T(8,128)(2,1)S(1)}, u32[]{:S(2)}, u32[]{:S(2)}) collective-permute-start(bf16[16,16,256]{2,1,0:T(8,128)(2,1)S(1)} %get-tuple-element.76), channel_id=1, source_target_pairs={{9,2},{10,1},{11,4},{12,3},{13,6},{14,5},{17,10},{18,9},{19,12},{2... | collective-permute-start | bytes 393224 | tf_op jit(solution)/shard_map/ppermute | solution.py:332
  103.4 8.5 %copy-start.11 = (bf16[32,80,256]{2,1,0:T(8,128)(2,1)}, bf16[32,80,256]{2,1,0:T(8,128)(2,1)S(1)}, u32[]{:S(2)}) copy-start(bf16[32,80,256]{2,1,0:T(8,128)(2,1)S(1)} %get-tuple-element.74.g_ref.mid_ref) | copy-start | bytes 3932164
  107.4 1.6 collective-permute-start.14
  107.5 7.5 %collective-permute-start.16 = (bf16[3072,128]{1,0:T(8,128)(2,1)S(1)}, bf16[3072,128]{1,0:T(8,128)(2,1)S(1)}, u32[]{:S(2)}, u32[]{:S(2)}) collective-permute-start(bf16[3072,128]{1,0:T(8,128)(2,1)S(1)} %get-tuple-element.91), channel_id=1, source_target_pairs={{0,1},{1,0},{2,3},{3,2},{4,5},{5,4},{6,7},{7,6},{8,9},{9,8},{10,11... | collective-permute-start | bytes 2359304 | tf_op jit(solution)/shard_map/ppermute | solution.py:332
  111.7 3.6 %collective-permute-start.15 = (bf16[3584,128]{1,0:T(8,128)(2,1)S(1)}, bf16[3584,128]{1,0:T(8,128)(2,1)S(1)}, u32[]{:S(2)}, u32[]{:S(2)}) collective-permute-start(bf16[3584,128]{1,0:T(8,128)(2,1)S(1)} %get-tuple-element.89), channel_id=1, source_target_pairs={{0,1},{1,0},{2,3},{3,2},{4,5},{5,4},{6,7},{7,6},{8,9},{9,8},{10,11... | collective-permute-start | bytes 2752520 | tf_op jit(solution)/shard_map/ppermute | solution.py:332
  114.6 0.9 copy-start.13
  114.6 2.4 %collective-permute-start.17 = (bf16[3072,128]{1,0:T(8,128)(2,1)S(1)}, bf16[3072,128]{1,0:T(8,128)(2,1)S(1)}, u32[]{:S(2)}, u32[]{:S(2)}) collective-permute-start(bf16[3072,128]{1,0:T(8,128)(2,1)S(1)} %get-tuple-element.93), channel_id=1, source_target_pairs={{0,1},{1,0},{2,3},{3,2},{4,5},{5,4},{6,7},{7,6},{8,9},{9,8},{10,11... | collective-permute-start | bytes 2359304 | tf_op jit(solution)/shard_map/ppermute | solution.py:332
  118.5 45.1 %all-to-all-start.1 = ((bf16[64,152,128]{2,1,0:T(8,128)(2,1)}), bf16[64,152,128]{2,1,0:T(8,128)(2,1)}, u32[]{:S(2)}, u32[]{:S(2)}) async-start(bf16[64,152,128]{2,1,0:T(8,128)(2,1)} %gather.1), calls=%async_computation.1 | async-start | bytes 4980736 | tf_op jit(solution)/shard_map/all_to_all | solution.py:474
  131.4 1.7 %copy-start.8 = (bf16[64,152,128]{2,1,0:T(8,128)(2,1)S(1)}, bf16[64,152,128]{2,1,0:T(8,128)(2,1)}, u32[]{:S(2)}) copy-start(bf16[64,152,128]{2,1,0:T(8,128)(2,1)} %copy-done.7) | copy-start | bytes 7471108
  133.1 1.3 copy-start.12
  134.4 1.1 copy-start.14
  165.3 3.1 %collective-permute-start.18 = (f32[80,128]{1,0:T(8,128)S(1)}, f32[80,128]{1,0:T(8,128)S(1)}, u32[]{:S(2)}, u32[]{:S(2)}) collective-permute-start(f32[80,128]{1,0:T(8,128)S(1)} %get-tuple-element.95), channel_id=1, source_target_pairs={{0,1},{1,0},{2,3},{3,2},{4,5},{5,4},{6,7},{7,6},{8,9},{9,8},{10,11... | collective-permute-start | bytes 122888 | tf_op jit(solution)/shard_map/ppermute | solution.py:332

commit v5 on v4

--- a/solution.py
+++ b/solution.py
@@ -109,9 +109,9 @@
     proj_ref[128:256] = acc[pl.ds(128 - start, 128), :].astype(BF)
 
 
-def halo_kernel(core_ref, f_ref, mine_ref, other_ref, n_ref, s_ref, inner_ref, outer_ref, cn_ref, cs_ref, sides, acc):
+def rows_out_kernel(core_ref, f_ref, mine_ref, other_ref, n_ref, s_ref, inner_ref, cn_ref, cs_ref, sides, acc):
     core = core_ref[0]
-    for out, a, r0, block in ((n_ref, 2, 0, 0), (s_ref, 0, 16, 3)):
+    for out, a, r0, block in ((n_ref, 2, 0, 0), (s_ref, 0, 16, 1)):
         acc[...] = jnp.zeros_like(acc)
         for b in range(3):
             c = (2 - b) * D
@@ -121,21 +121,26 @@
         sides[0, 16 * block : 16 * block + 16] = acc[:, 0:16, :].astype(BF)
         out[...] = acc[:, 16:64, :].astype(BF)
         sides[1, 16 * block : 16 * block + 16] = acc[:, 64:80, :].astype(BF)
+    inner_ref[...] = sides[1 - core]
+    cn_ref[...] = sides[core, 0:16]
+    cs_ref[...] = sides[core, 16:32]
+
+
+def sides_out_kernel(core_ref, f_ref, mine_ref, other_ref, inner_ref, outer_ref, sides):
+    core = core_ref[0]
     for side, b, c0 in ((0, 2, 0), (1, 0, 32)):
         mid = dot(px(f_ref, 0, 32, c0, c0 + 16), tap(mine_ref, other_ref, 1, b))
         top = mid[:256] + dot(px(f_ref, 16, 32, c0, c0 + 16), tap(mine_ref, other_ref, 2, b))
         low = mid[256:] + dot(px(f_ref, 0, 16, c0, c0 + 16), tap(mine_ref, other_ref, 0, b))
-        sides[side, 16:32] = top.reshape(16, 16, 256).astype(BF)
-        sides[side, 32:48] = low.reshape(16, 16, 256).astype(BF)
+        sides[side, 0:16] = top.reshape(16, 16, 256).astype(BF)
+        sides[side, 16:32] = low.reshape(16, 16, 256).astype(BF)
     inner_ref[...] = sides[1 - core]
-    outer_ref[...] = sides[core, 16:48]
-    cn_ref[...] = sides[core, 0:16]
-    cs_ref[...] = sides[core, 48:64]
+    outer_ref[...] = sides[core]
 
 
 def merge_kernel(core_ref, n_ref, s_ref, inner_ref, no_ref, so_ref):
     cols = pl.ds(pl.multiple_of(32 - 32 * core_ref[0], 16), 16)
-    for src, dst, r in ((n_ref, no_ref, 0), (s_ref, so_ref, 48)):
+    for src, dst, r in ((n_ref, no_ref, 0), (s_ref, so_ref, 16)):
         dst[...] = src[...]
         dst[:, cols, :] = (src[:, cols, :].astype(F32) + swap(inner_ref[r : r + 16]).astype(F32)).astype(BF)
 
@@ -165,7 +170,7 @@
     outer = pl.ds(pl.multiple_of(32 * core, 16), 16)
     pre_ref[0:16] = own_ref[0:16] + n_ref[...].astype(F32)
     pre_ref[16:32] = own_ref[16:32] + s_ref[...].astype(F32)
-    pre_ref[:, inner, :] += swap(inner_ref[16:48]).astype(F32)
+    pre_ref[:, inner, :] += swap(inner_ref[...]).astype(F32)
     pre_ref[:, outer, :] += swap(outer_ref[...]).astype(F32)
     pre_ref[0:16, outer, :] += swap(cn_ref[...]).astype(F32)
     pre_ref[16:32, outer, :] += swap(cs_ref[...]).astype(F32)
@@ -256,7 +261,7 @@
         out_ref[rows] = (m_ref[rows].astype(F32) + r_ref[rows].astype(F32)).astype(BF)
 
 
-def gather_kernel(t0_ref, t1_ref, m2_ref, r2_ref, e_ref, r0_ref, _, out_ref, near, sems):
+def gather_kernel(t0_ref, t1_ref, m2_ref, r2_ref, e_ref, r0_ref, out_ref, near, sems):
     copies = []
     for k in range(64):
         at = 144 * k
@@ -366,23 +371,35 @@
         limit=40 * 1024 * 1024,
     )
     mine = lax.all_to_all(spread, CHIPS, 0, 0)
-    (ft,) = call(flip_kernel, "flip", [array((1024, 1536))], [features], 1e6, 6e6)
-    mine, ft = lax.optimization_barrier((mine, ft))
+    mine, features = lax.optimization_barrier((mine, features))
+    (ft,) = call(flip_kernel, "flip", [array((1024, 1536))], [features], 1e9, 6e6)
     other = send(mine, 0, INNER)
     (proj,) = call(rows_kernel, "rows", [array((256, 256))], [core_s, mine], 1e6, 1e6, [pltpu.VMEM((256, 256), F32)])
-    other, proj = lax.optimization_barrier((other, proj))
+    other, proj, ft = lax.optimization_barrier((other, proj, ft))
     tile, strip, small, side = (32, 48, 256), (16, 48, 256), (16, 16, 256), (32, 16, 256)
-    n, s, inner, outer, cn, cs = call(
-        halo_kernel,
-        "halo",
-        [array(strip), array(strip), array((64, 16, 256)), array(side), array(small), array(small)],
+    n, s, corners, cn, cs = call(
+        rows_out_kernel,
+        "rows_out",
+        [array(strip), array(strip), array(side), array(small), array(small)],
         [core_s, features, mine, other],
-        3.5e9,
+        1.7e9,
         9e6,
-        [pltpu.VMEM((2, 64, 16, 256), BF), pltpu.VMEM((16, 80, 256), F32)],
-    )
+        [pltpu.VMEM((2, 32, 16, 256), BF), pltpu.VMEM((16, 80, 256), F32)],
+    )
+    corners, features = lax.optimization_barrier((corners, features))
+    corners = send(corners, 0, INNER)
+    inner, outer = call(
+        sides_out_kernel,
+        "sides_out",
+        [array(side), array(side)],
+        [core_s, features, mine, other],
+        1.9e9,
+        9e6,
+        [pltpu.VMEM((2, 32, 16, 256), BF)],
+    )
+    n, inner = lax.optimization_barrier((n, inner))
+    n, s = call(merge_kernel, "merge", [array(strip), array(strip)], [core_s, n, s, corners], 1e6, 2e6)
     inner = send(inner, 0, INNER)
-    n, s = call(merge_kernel, "merge", [array(strip), array(strip)], [core_s, n, s, inner], 1e6, 2e6)
     from_s = send(n, -1, SAME)
     from_n = send(s, 1, SAME)
     outer = send(outer, 0, OUTER)
@@ -414,26 +431,27 @@
     c_low = send(ct, -1, OUTER)
     h_inner = send(gi, 0, INNER)
 
+    part = array((3072, 128))
+    g_mid, m1, o1 = call(
+        wgrad_mid_kernel,
+        "wgrad1",
+        [array((32, 80, 256)), part, part],
+        [core_s, ft, g_top, g_low, h_inner, h_outer],
+        1e8,
+        6e6,
+    )
+    r1 = send(o1, 0, INNER)
+    hidden, m1 = lax.optimization_barrier((hidden, m1))
     ends = array((64, 8, 128))
     projected, e_mine, e_other = call(
         proj_kernel,
         "proj",
         [array(tile), ends, ends],
         [core_s, hidden, cotangent, proj, g_top, g_low],
-        4e9,
+        1e8,
         4e6,
         [pltpu.VMEM((256, 256), F32), pltpu.VMEM((64, 8, 128), F32)],
     )
-    part = array((3072, 128))
-    g_mid, m1, o1 = call(
-        wgrad_mid_kernel,
-        "wgrad1",
-        [array((32, 80, 256)), part, part],
-        [core_s, ft, g_top, g_low, h_inner, h_outer],
-        2.4e9,
-        6e6,
-    )
-    r1 = send(o1, 0, INNER)
     h_top, h_low, c_top, c_low, e_mine, e_other, m1 = lax.optimization_barrier(
         (h_top, h_low, c_top, c_low, e_mine, e_other, m1)
     )
@@ -464,12 +482,11 @@
         gather_kernel,
         "gather",
         [array((64, 152, 128))],
-        [t0, t1, m2, r2, e_mine, r0, spread],
+        [t0, t1, m2, r2, e_mine, r0],
         1e6,
         7e6,
         [pltpu.VMEM((64, 152, 128), BF), pltpu.SemaphoreType.DMA((8,))],
-        far=(spread,),
-        reuse=6,
+        limit=49 * 1024 * 1024,
     )
     pieces = lax.all_to_all(total, CHIPS, 0, 0)
 

time: 170 us -> 164 us (0.965)
  blocking collectives: 0 us -> 44.7 us
  waiting for transfers between devices: 62.8 us -> 34.4 us
  starting transfers between devices: 58.6 us -> 42.7 us
  local copies, waits for them, and re-layouts: 11.8 us -> 6.15 us
    all_to_all x0 -> x1, blocking collectives: none -> 44.7 us  [body(): mine = lax.all_to_all(spread, CHIPS, 0, 0)]
    all_to_all x1 -> x0, waiting for transfers between devices: 27.9 us -> none  [body(): mine = lax.all_to_all(spread, CHIPS, 0, 0)]
    all_to_all x1 -> x0, starting transfers between devices: 11.2 us -> none  [body(): mine = lax.all_to_all(spread, CHIPS, 0, 0)]
    unnamed x30 -> x22, local copies, waits for them, and re-layouts: 11.2 us -> 5.57 us
    ppermute x19 -> x20, starting transfers between devices: 34.5 us -> 31.4 us  [send(): return lax.ppermute(x, ALL, perm)]
    ppermute x19 -> x20, waiting for transfers between devices: 16 us -> 15.5 us  [send(): return lax.ppermute(x, ALL, perm)]
    pallas_call x19 -> x20, Pallas kernels: 34.9 us -> 34.4 us  [call(): pl.pallas_call(kernel, out_shape=tuple(outs), in_specs=specs, out_specs=(...]
  transfers between devices with their start and end apart: 21 -> 21, of which waited for: 11 -> 9; matrix products, arithmetic and copies ran while one was open for 0% -> 0% of each run, Pallas kernels for 14% -> 16%
where the time goes in v5:
time: 164 us; the launch traced here: 163 us
  blocking collectives  44.7 us (27%)
  starting transfers between devices  42.7 us (26%)
  Pallas kernels  34.4 us (21%)
  waiting for transfers between devices  34.4 us (21%)
  local copies, waits for them, and re-layouts  6.15 us (4%)
    all_to_all x1, blocking collectives, body(): mine = lax.all_to_all(spread, CHIPS, 0, 0)  44.7 us
    pallas_call x20, Pallas kernels, call(): pl.pallas_call(kernel, out_shape=tuple(outs), in_specs=specs, out_specs=(...  34.4 us
    ppermute x20, starting transfers between devices, send(): return lax.ppermute(x, ALL, perm)  31.4 us
    all_to_all x1, waiting for transfers between devices, body(): pieces = lax.all_to_all(total, CHIPS, 0, 0)  18.9 us
    ppermute x20, waiting for transfers between devices, send(): return lax.ppermute(x, ALL, perm)  15.5 us
    all_to_all x1, starting transfers between devices, body(): pieces = lax.all_to_all(total, CHIPS, 0, 0)  11.3 us
    unnamed x22, local copies, waits for them, and re-layouts  5.57 us
  transfers between devices with their start and end apart: 21, of which 9 were waited for; matrix products, arithmetic and copies ran while one was open for 0% of the time, Pallas kernels for 16%

profile of v5, /device:TPU:1, one launch (start us, length us, event | category | flops | bytes accessed | tf_op | source)
XLA Modules:
  0.0 163.3 jit_solution(15728561221576644073)
XLA Ops:
  0.6 0.8 copy-done.4
  1.4 0.7 copy-done.5
  2.1 1.5 collective-permute-start
  3.6 0.8 collective-permute-done.got_ref
  4.4 0.8 spread.1
  5.2 44.7 %all_to_all.10.mine_ref = bf16[64,152,128]{2,1,0:T(8,128)(2,1)S(1)} all-to-all(bf16[64,152,128]{2,1,0:T(8,128)(2,1)S(1)} %spread.1), channel_id=1, replica_groups=mesh['y'=4,'x'=4,'z'=4,'core'=2] {'y','x','z'}, dimensions={0} | all-to-all | bytes 4980736 | tf_op jit(solution)/shard_map/all_to_all | solution.py:373
  49.9 1.9 %collective-permute-start.1 = (bf16[64,152,128]{2,1,0:T(8,128)(2,1)S(1)}, bf16[64,152,128]{2,1,0:T(8,128)(2,1)S(1)}, u32[]{:S(2)}, u32[]{:S(2)}) collective-permute-start(bf16[64,152,128]{2,1,0:T(8,128)(2,1)S(1)} %all_to_all.10.mine_ref), channel_id=1, source_target_pairs={{0,1},{1,0},{2,3},{3,2},{4,5},{5,4},{6,7},{7,6},{8,9},{9,8},{10,11... | collective-permute-start | bytes 7471112 | tf_op jit(solution)/shard_map/ppermute | solution.py:337
  51.9 0.9 flip.1.ft_ref
  52.8 3.4 %collective-permute-done.1.other_ref = bf16[64,152,128]{2,1,0:T(8,128)(2,1)S(1)} collective-permute-done((bf16[64,152,128]{2,1,0:T(8,128)(2,1)S(1)}, bf16[64,152,128]{2,1,0:T(8,128)(2,1)S(1)}, u32[]{:S(2)}, u32[]{:S(2)}) %collective-permute-start.1) | collective-permute-done | bytes 2490400 | tf_op jit(solution)/shard_map/ppermute | solution.py:337
  56.2 2.7 %rows_out.1 = (bf16[16,48,256]{2,1,0:T(8,128)(2,1)S(1)}, bf16[16,48,256]{2,1,0:T(8,128)(2,1)S(1)}, bf16[32,16,256]{2,1,0:T(8,128)(2,1)S(1)}, bf16[16,16,256]{2,1,0:T(8,128)(2,1)S(1)}, bf16[16,16,256]{2,1,0:T(8,128)(2,1)S(1)}) custom-call(s32[1]{0:T(128)} %bitcast.core_ref, bf16[32,48,1024]{2,1,0:T(8,128)(2,1)S(1)} %copy-done, ...), custom_call_target="tpu_custom_call" | custom-call | flops 1700000000 | bytes 9000000 | tf_op jit(solution)/shard_map/rows_out/pallas_call | solution.py:344
  58.9 0.5 collective-permute-start.2
  59.3 2.7 %collective-permute-start.7 = (bf16[16,16,256]{2,1,0:T(8,128)(2,1)S(1)}, bf16[16,16,256]{2,1,0:T(8,128)(2,1)S(1)}, u32[]{:S(2)}, u32[]{:S(2)}) collective-permute-start(bf16[16,16,256]{2,1,0:T(8,128)(2,1)S(1)} %get-tuple-element.79), channel_id=1, source_target_pairs={{1,10},{2,9},{3,12},{4,11},{5,14},{6,13},{9,18},{10,17},{11,20},{1... | collective-permute-start | bytes 393224 | tf_op jit(solution)/shard_map/ppermute | solution.py:337
  62.1 1.3 sides_out.1
  63.6 1.7 %collective-permute-start.3 = (bf16[16,48,256]{2,1,0:T(8,128)(2,1)S(1)}, bf16[16,48,256]{2,1,0:T(8,128)(2,1)S(1)}, u32[]{:S(2)}, u32[]{:S(2)}) collective-permute-start(bf16[16,48,256]{2,1,0:T(8,128)(2,1)S(1)} %get-tuple-element.75), channel_id=1, source_target_pairs={{0,8},{1,9},{2,10},{3,11},{4,12},{5,13},{6,14},{7,15},{8,16},{9,17... | collective-permute-start | bytes 1179656 | tf_op jit(solution)/shard_map/ppermute | solution.py:337
  65.2 1.3 collective-permute-start.4
  66.5 1.3 collective-permute-start.8
  67.9 3.6 %collective-permute-start.6 = (bf16[32,16,256]{2,1,0:T(8,128)(2,1)S(1)}, bf16[32,16,256]{2,1,0:T(8,128)(2,1)S(1)}, u32[]{:S(2)}, u32[]{:S(2)}) collective-permute-start(bf16[32,16,256]{2,1,0:T(8,128)(2,1)S(1)} %get-tuple-element.78), channel_id=1, source_target_pairs={{1,2},{2,1},{3,4},{4,3},{5,6},{6,5},{9,10},{10,9},{11,12},{12,11},... | collective-permute-start | bytes 786440 | tf_op jit(solution)/shard_map/ppermute | solution.py:337
  71.5 4.3 %own.1 = (f32[32,48,256]{2,1,0:T(8,128)S(1)}, f32[32,48,256]{2,1,0:T(8,128)S(1)}) custom-call(s32[1]{0:T(128)} %bitcast.core_ref, bf16[32,48,1024]{2,1,0:T(8,128)(2,1)S(1)} %copy-done, bf16[64,152,128]{2,1,0:T(8,128)(2,1)S(1)} %all_to_all.10.mine_ref, bf16[64,152,128]{2,1,0:T(8,128)(2,1)S(1)} %collective-permute-done.1.other_ref, ...), custom_call_target="tpu_custom_call" | custom-call | flops 4000000000 | bytes 12000000 | tf_op jit(solution)/shard_map/own/pallas_call | solution.py:344
  75.8 5.2 %collective-permute-done.8.cs_ref = bf16[16,16,256]{2,1,0:T(8,128)(2,1)S(1)} collective-permute-done((bf16[16,16,256]{2,1,0:T(8,128)(2,1)S(1)}, bf16[16,16,256]{2,1,0:T(8,128)(2,1)S(1)}, u32[]{:S(2)}, u32[]{:S(2)}) %collective-permute-start.8) | collective-permute-done | bytes 131104 | tf_op jit(solution)/shard_map/ppermute | solution.py:337
  81.1 1.1 point.1
  82.3 1.3 collective-permute-start.12
  83.6 4.0 %collective-permute-start.11 = (bf16[16,48,256]{2,1,0:T(8,128)(2,1)S(1)}, bf16[16,48,256]{2,1,0:T(8,128)(2,1)S(1)}, u32[]{:S(2)}, u32[]{:S(2)}) collective-permute-start(bf16[16,48,256]{2,1,0:T(8,128)(2,1)S(1)} %get-tuple-element.84.gl_ref.low_ref), channel_id=1, source_target_pairs={{0,8},{1,9},{2,10},{3,11},{4,12},{5,13},{6,14},{7,15},{8,16},{9,17... | collective-permute-start | bytes 1179656 | tf_op jit(solution)/shard_map/ppermute | solution.py:337
  87.6 4.5 %collective-permute-start.10 = (bf16[32,16,256]{2,1,0:T(8,128)(2,1)S(1)}, bf16[32,16,256]{2,1,0:T(8,128)(2,1)S(1)}, u32[]{:S(2)}, u32[]{:S(2)}) collective-permute-start(bf16[32,16,256]{2,1,0:T(8,128)(2,1)S(1)} %get-tuple-element.86), channel_id=1, source_target_pairs={{1,2},{2,1},{3,4},{4,3},{5,6},{6,5},{9,10},{10,9},{11,12},{12,11},... | collective-permute-start | bytes 786440 | tf_op jit(solution)/shard_map/ppermute | solution.py:337
  92.1 2.0 %collective-permute-start.13 = (bf16[16,16,256]{2,1,0:T(8,128)(2,1)S(1)}, bf16[16,16,256]{2,1,0:T(8,128)(2,1)S(1)}, u32[]{:S(2)}, u32[]{:S(2)}) collective-permute-start(bf16[16,16,256]{2,1,0:T(8,128)(2,1)S(1)} %get-tuple-element.91), channel_id=1, source_target_pairs={{1,10},{2,9},{3,12},{4,11},{5,14},{6,13},{9,18},{10,17},{11,20},{1... | collective-permute-start | bytes 393224 | tf_op jit(solution)/shard_map/ppermute | solution.py:337
  94.2 1.5 collective-permute-start.14
  95.7 0.5 collective-permute-done.10.ho_ref
  96.2 2.7 %wgrad1.1 = (bf16[32,80,256]{2,1,0:T(8,128)(2,1)S(1)}, bf16[3072,128]{1,0:T(8,128)(2,1)S(1)}, bf16[3072,128]{1,0:T(8,128)(2,1)S(1)}) custom-call(s32[1]{0:T(128)} %bitcast.core_ref, bf16[1024,1536]{1,0:T(8,128)(2,1)S(1)} %flip.1.ft_ref, bf16[16,48,256]{2,1,0:T(8,128)(2,1)S(1)} %get-tuple-element.83.gt_ref.top_ref, ...), custom_call_target="tpu_custom_call" | custom-call | flops 100000000 | bytes 6000000 | tf_op jit(solution)/shard_map/wgrad1/pallas_call | solution.py:344
  98.9 1.5 proj.1
  100.4 2.7 %collective-permute-done.14.c_ref = bf16[16,16,256]{2,1,0:T(8,128)(2,1)S(1)} collective-permute-done((bf16[16,16,256]{2,1,0:T(8,128)(2,1)S(1)}, bf16[16,16,256]{2,1,0:T(8,128)(2,1)S(1)}, u32[]{:S(2)}, u32[]{:S(2)}) %collective-permute-start.14) | collective-permute-done | bytes 131104 | tf_op jit(solution)/shard_map/ppermute | solution.py:337
  103.2 0.5 collective-permute-start.17
  103.7 1.0 collective-permute-done.15.edge_ref
  104.8 2.6 %wgrad0.1 = (bf16[16,80,256]{2,1,0:T(8,128)(2,1)S(1)}, bf16[3072,128]{1,0:T(8,128)(2,1)S(1)}, bf16[3584,128]{1,0:T(8,128)(2,1)S(1)}) custom-call(s32[1]{0:T(128)} %bitcast.core_ref, bf16[1024,1536]{1,0:T(8,128)(2,1)S(1)} %flip.1.ft_ref, bf16[32,80,256]{2,1,0:T(8,128)(2,1)S(1)} %get-tuple-element.90.g_ref.mid_ref, ...), custom_call_target="tpu_custom_call" | custom-call | flops 2400000000 | bytes 6000000 | tf_op jit(solution)/shard_map/wgrad0/pallas_call | solution.py:344
  107.6 2.6 %wgrad2.1 = (bf16[16,80,256]{2,1,0:T(8,128)(2,1)S(1)}, bf16[3072,128]{1,0:T(8,128)(2,1)S(1)}, bf16[3072,128]{1,0:T(8,128)(2,1)S(1)}) custom-call(s32[1]{0:T(128)} %bitcast.core_ref, bf16[1024,1536]{1,0:T(8,128)(2,1)S(1)} %flip.1.ft_ref, bf16[32,80,256]{2,1,0:T(8,128)(2,1)S(1)} %get-tuple-element.90.g_ref.mid_ref, ...), custom_call_target="tpu_custom_call" | custom-call | flops 2400000000 | bytes 6000000 | tf_op jit(solution)/shard_map/wgrad2/pallas_call | solution.py:344
  110.3 0.5 collective-permute-start.18
  111.0 0.2 add0.1.t0_ref
  111.3 1.4 collective-permute-done.18.r2_ref
  112.7 1.6 gather.1
  114.3 11.3 %all-to-all-start.1 = ((bf16[64,152,128]{2,1,0:T(8,128)(2,1)}), bf16[64,152,128]{2,1,0:T(8,128)(2,1)}, u32[]{:S(2)}, u32[]{:S(2)}) async-start(bf16[64,152,128]{2,1,0:T(8,128)(2,1)} %gather.1), calls=%async_computation.1 | async-start | bytes 4980736 | tf_op jit(solution)/shard_map/all_to_all | solution.py:491
  125.6 1.7 %copy-done.2 = bf16[64,152,128]{2,1,0:T(8,128)(2,1)S(1)} copy-done((bf16[64,152,128]{2,1,0:T(8,128)(2,1)S(1)}, bf16[64,152,128]{2,1,0:T(8,128)(2,1)}, u32[]{:S(2)}) %copy-start.2) | copy-done | bytes 2490392
  127.3 1.3 copy-done.7
  128.6 1.1 copy-done.10
  129.7 9.2 %fgrad.1 = bf16[32,48,1024]{2,1,0:T(8,128)(2,1)} custom-call(bf16[16,80,256]{2,1,0:T(8,128)(2,1)S(1)} %copy-done.10, bf16[32,80,256]{2,1,0:T(8,128)(2,1)S(1)} %copy-done.7, bf16[16,80,256]{2,1,0:T(8,128)(2,1)S(1)} %get-tuple-element.103.low_ref, bf16[64,152,128]{2,1,0:T(8,128)(2,1)S(1)} %all_to_all.10.mine_ref, bf16[64,152,128]{2,1,0:T(8,128)(2,1)S(1)} %copy-done.2), custom_call_target="tpu_custom_call" | custom-call | flops 7200000000 | bytes 12000000 | tf_op jit(solution)/shard_map/fgrad/pallas_call | solution.py:344
  138.9 18.9 %all-to-all-done.1.far_ref = bf16[64,152,128]{2,1,0:T(8,128)(2,1)} async-done(((bf16[64,152,128]{2,1,0:T(8,128)(2,1)}), bf16[64,152,128]{2,1,0:T(8,128)(2,1)}, u32[]{:S(2)}, u32[]{:S(2)}) %all-to-all-start.1) | async-done | bytes 2490400 | tf_op jit(solution)/shard_map/all_to_all | solution.py:491
  157.8 1.8 %sum.1 = (f32[80,128]{1,0:T(8,128)S(1)}, f32[80,128]{1,0:T(8,128)S(1)}, f32[1,128]{1,0:T(1,128)S(1)}) custom-call(s32[1]{0:T(128)} %bitcast.core_ref, bf16[64,152,128]{2,1,0:T(8,128)(2,1)} %all-to-all-done.1.far_ref), custom_call_target="tpu_custom_call" | custom-call | flops 1000000 | bytes 3000000 | tf_op jit(solution)/shard_map/sum/pallas_call | solution.py:344
  159.6 2.2 %collective-permute-start.19 = (f32[80,128]{1,0:T(8,128)S(1)}, f32[80,128]{1,0:T(8,128)S(1)}, u32[]{:S(2)}, u32[]{:S(2)}) collective-permute-start(f32[80,128]{1,0:T(8,128)S(1)} %get-tuple-element.111), channel_id=1, source_target_pairs={{0,1},{1,0},{2,3},{3,2},{4,5},{5,4},{6,7},{7,6},{8,9},{9,8},{10,11... | collective-permute-start | bytes 122888 | tf_op jit(solution)/shard_map/ppermute | solution.py:337
  161.8 0.6 dynamic-slice_bitcast_fusion
  162.3 0.3 collective-permute-done.19.got_ref
  162.6 0.6 join.1
  (38 shorter events, 1.0 us)
Async XLA Ops:
  0.6 0.8 copy-start.4
  1.4 0.7 copy-start.5
  2.1 2.3 %collective-permute-start = (bf16[80,128]{1,0:T(8,128)(2,1)S(1)}, bf16[80,128]{1,0:T(8,128)(2,1)S(1)}, u32[]{:S(2)}, u32[]{:S(2)}) collective-permute-start(bf16[80,128]{1,0:T(8,128)(2,1)S(1)} %get-tuple-element.61), channel_id=1, source_target_pairs={{0,1},{1,0},{2,3},{3,2},{4,5},{5,4},{6,7},{7,6},{8,9},{9,8},{10,11... | collective-permute-start | bytes 61448 | tf_op jit(solution)/shard_map/ppermute | solution.py:337
  5.2 46.7 %copy-start = (bf16[32,48,1024]{2,1,0:T(8,128)(2,1)S(1)}, bf16[32,48,1024]{2,1,0:T(8,128)(2,1)}, u32[]{:S(2)}) copy-start(bf16[32,48,1024]{2,1,0:T(8,128)(2,1)} %f_ref.3) | copy-start | bytes 9437188
  49.9 6.3 %collective-permute-start.1 = (bf16[64,152,128]{2,1,0:T(8,128)(2,1)S(1)}, bf16[64,152,128]{2,1,0:T(8,128)(2,1)S(1)}, u32[]{:S(2)}, u32[]{:S(2)}) collective-permute-start(bf16[64,152,128]{2,1,0:T(8,128)(2,1)S(1)} %all_to_all.10.mine_ref), channel_id=1, source_target_pairs={{0,1},{1,0},{2,3},{3,2},{4,5},{5,4},{6,7},{7,6},{8,9},{9,8},{10,11... | collective-permute-start | bytes 7471112 | tf_op jit(solution)/shard_map/ppermute | solution.py:337
  56.2 15.3 %copy-start.1 = (bf16[64,152,128]{2,1,0:T(8,128)(2,1)}, bf16[64,152,128]{2,1,0:T(8,128)(2,1)S(1)}, u32[]{:S(2)}) copy-start(bf16[64,152,128]{2,1,0:T(8,128)(2,1)S(1)} %collective-permute-done.1.other_ref) | copy-start | bytes 7471108
  58.9 4.6 %collective-permute-start.2 = (bf16[32,16,256]{2,1,0:T(8,128)(2,1)S(1)}, bf16[32,16,256]{2,1,0:T(8,128)(2,1)S(1)}, u32[]{:S(2)}, u32[]{:S(2)}) collective-permute-start(bf16[32,16,256]{2,1,0:T(8,128)(2,1)S(1)} %get-tuple-element.74), channel_id=1, source_target_pairs={{0,1},{1,0},{2,3},{3,2},{4,5},{5,4},{6,7},{7,6},{8,9},{9,8},{10,11... | collective-permute-start | bytes 786440 | tf_op jit(solution)/shard_map/ppermute | solution.py:337
  59.3 12.2 %copy-start.3 = (bf16[32,48,256]{2,1,0:T(8,128)(2,1)S(1)}, bf16[32,48,256]{2,1,0:T(8,128)(2,1)}, u32[]{:S(2)}) copy-start(bf16[32,48,256]{2,1,0:T(8,128)(2,1)} %cot_ref.3) | copy-start | bytes 2359300
  59.3 12.2 %copy-start.8 = (f32[256]{0:T(256)S(1)}, f32[256]{0:T(256)}, u32[]{:S(2)}) copy-start(f32[256]{0:T(256)} %param.7) | copy-start | bytes 3076
  59.3 8.6 %collective-permute-start.7 = (bf16[16,16,256]{2,1,0:T(8,128)(2,1)S(1)}, bf16[16,16,256]{2,1,0:T(8,128)(2,1)S(1)}, u32[]{:S(2)}, u32[]{:S(2)}) collective-permute-start(bf16[16,16,256]{2,1,0:T(8,128)(2,1)S(1)} %get-tuple-element.79), channel_id=1, source_target_pairs={{1,10},{2,9},{3,12},{4,11},{5,14},{6,13},{9,18},{10,17},{11,20},{1... | collective-permute-start | bytes 393224 | tf_op jit(solution)/shard_map/ppermute | solution.py:337
  63.6 17.5 %collective-permute-start.3 = (bf16[16,48,256]{2,1,0:T(8,128)(2,1)S(1)}, bf16[16,48,256]{2,1,0:T(8,128)(2,1)S(1)}, u32[]{:S(2)}, u32[]{:S(2)}) collective-permute-start(bf16[16,48,256]{2,1,0:T(8,128)(2,1)S(1)} %get-tuple-element.75), channel_id=1, source_target_pairs={{0,8},{1,9},{2,10},{3,11},{4,12},{5,13},{6,14},{7,15},{8,16},{9,17... | collective-permute-start | bytes 1179656 | tf_op jit(solution)/shard_map/ppermute | solution.py:337
  65.2 15.8 %collective-permute-start.4 = (bf16[16,48,256]{2,1,0:T(8,128)(2,1)S(1)}, bf16[16,48,256]{2,1,0:T(8,128)(2,1)S(1)}, u32[]{:S(2)}, u32[]{:S(2)}) collective-permute-start(bf16[16,48,256]{2,1,0:T(8,128)(2,1)S(1)} %get-tuple-element.76), channel_id=1, source_target_pairs={{8,0},{9,1},{10,2},{11,3},{12,4},{13,5},{14,6},{15,7},{16,8},{17,9... | collective-permute-start | bytes 1179656 | tf_op jit(solution)/shard_map/ppermute | solution.py:337
  66.5 14.5 %collective-permute-start.8 = (bf16[16,16,256]{2,1,0:T(8,128)(2,1)S(1)}, bf16[16,16,256]{2,1,0:T(8,128)(2,1)S(1)}, u32[]{:S(2)}, u32[]{:S(2)}) collective-permute-start(bf16[16,16,256]{2,1,0:T(8,128)(2,1)S(1)} %get-tuple-element.80), channel_id=1, source_target_pairs={{9,2},{10,1},{11,4},{12,3},{13,6},{14,5},{17,10},{18,9},{19,12},{2... | collective-permute-start | bytes 393224 | tf_op jit(solution)/shard_map/ppermute | solution.py:337
  67.8 13.2 %collective-permute-start.5 = (bf16[32,16,256]{2,1,0:T(8,128)(2,1)S(1)}, bf16[32,16,256]{2,1,0:T(8,128)(2,1)S(1)}, u32[]{:S(2)}, u32[]{:S(2)}) collective-permute-start(bf16[32,16,256]{2,1,0:T(8,128)(2,1)S(1)} %get-tuple-element.77), channel_id=1, source_target_pairs={{0,1},{1,0},{2,3},{3,2},{4,5},{5,4},{6,7},{7,6},{8,9},{9,8},{10,11... | collective-permute-start | bytes 786440 | tf_op jit(solution)/shard_map/ppermute | solution.py:337
  67.9 13.1 %collective-permute-start.6 = (bf16[32,16,256]{2,1,0:T(8,128)(2,1)S(1)}, bf16[32,16,256]{2,1,0:T(8,128)(2,1)S(1)}, u32[]{:S(2)}, u32[]{:S(2)}) collective-permute-start(bf16[32,16,256]{2,1,0:T(8,128)(2,1)S(1)} %get-tuple-element.78), channel_id=1, source_target_pairs={{1,2},{2,1},{3,4},{4,3},{5,6},{6,5},{9,10},{10,9},{11,12},{12,11},... | collective-permute-start | bytes 786440 | tf_op jit(solution)/shard_map/ppermute | solution.py:337
  82.2 12.0 %collective-permute-start.9 = (bf16[32,16,256]{2,1,0:T(8,128)(2,1)S(1)}, bf16[32,16,256]{2,1,0:T(8,128)(2,1)S(1)}, u32[]{:S(2)}, u32[]{:S(2)}) collective-permute-start(bf16[32,16,256]{2,1,0:T(8,128)(2,1)S(1)} %get-tuple-element.85), channel_id=1, source_target_pairs={{0,1},{1,0},{2,3},{3,2},{4,5},{5,4},{6,7},{7,6},{8,9},{9,8},{10,11... | collective-permute-start | bytes 786440 | tf_op jit(solution)/shard_map/ppermute | solution.py:337
  82.3 20.8 %collective-permute-start.12 = (bf16[16,48,256]{2,1,0:T(8,128)(2,1)S(1)}, bf16[16,48,256]{2,1,0:T(8,128)(2,1)S(1)}, u32[]{:S(2)}, u32[]{:S(2)}) collective-permute-start(bf16[16,48,256]{2,1,0:T(8,128)(2,1)S(1)} %get-tuple-element.83.gt_ref.top_ref), channel_id=1, source_target_pairs={{8,0},{9,1},{10,2},{11,3},{12,4},{13,5},{14,6},{15,7},{16,8},{17,9... | collective-permute-start | bytes 1179656 | tf_op jit(solution)/shard_map/ppermute | solution.py:337
  83.6 19.6 %collective-permute-start.11 = (bf16[16,48,256]{2,1,0:T(8,128)(2,1)S(1)}, bf16[16,48,256]{2,1,0:T(8,128)(2,1)S(1)}, u32[]{:S(2)}, u32[]{:S(2)}) collective-permute-start(bf16[16,48,256]{2,1,0:T(8,128)(2,1)S(1)} %get-tuple-element.84.gl_ref.low_ref), channel_id=1, source_target_pairs={{0,8},{1,9},{2,10},{3,11},{4,12},{5,13},{6,14},{7,15},{8,16},{9,17... | collective-permute-start | bytes 1179656 | tf_op jit(solution)/shard_map/ppermute | solution.py:337
  87.6 8.6 %collective-permute-start.10 = (bf16[32,16,256]{2,1,0:T(8,128)(2,1)S(1)}, bf16[32,16,256]{2,1,0:T(8,128)(2,1)S(1)}, u32[]{:S(2)}, u32[]{:S(2)}) collective-permute-start(bf16[32,16,256]{2,1,0:T(8,128)(2,1)S(1)} %get-tuple-element.86), channel_id=1, source_target_pairs={{1,2},{2,1},{3,4},{4,3},{5,6},{6,5},{9,10},{10,9},{11,12},{12,11},... | collective-permute-start | bytes 786440 | tf_op jit(solution)/shard_map/ppermute | solution.py:337
  92.1 8.2 %collective-permute-start.13 = (bf16[16,16,256]{2,1,0:T(8,128)(2,1)S(1)}, bf16[16,16,256]{2,1,0:T(8,128)(2,1)S(1)}, u32[]{:S(2)}, u32[]{:S(2)}) collective-permute-start(bf16[16,16,256]{2,1,0:T(8,128)(2,1)S(1)} %get-tuple-element.91), channel_id=1, source_target_pairs={{1,10},{2,9},{3,12},{4,11},{5,14},{6,13},{9,18},{10,17},{11,20},{1... | collective-permute-start | bytes 393224 | tf_op jit(solution)/shard_map/ppermute | solution.py:337
  94.2 8.9 %collective-permute-start.14 = (bf16[16,16,256]{2,1,0:T(8,128)(2,1)S(1)}, bf16[16,16,256]{2,1,0:T(8,128)(2,1)S(1)}, u32[]{:S(2)}, u32[]{:S(2)}) collective-permute-start(bf16[16,16,256]{2,1,0:T(8,128)(2,1)S(1)} %get-tuple-element.92), channel_id=1, source_target_pairs={{9,2},{10,1},{11,4},{12,3},{13,6},{14,5},{17,10},{18,9},{19,12},{2... | collective-permute-start | bytes 393224 | tf_op jit(solution)/shard_map/ppermute | solution.py:337
  98.9 8.8 %copy-start.6 = (bf16[32,80,256]{2,1,0:T(8,128)(2,1)}, bf16[32,80,256]{2,1,0:T(8,128)(2,1)S(1)}, u32[]{:S(2)}) copy-start(bf16[32,80,256]{2,1,0:T(8,128)(2,1)S(1)} %get-tuple-element.90.g_ref.mid_ref) | copy-start | bytes 3932164
  103.1 1.6 collective-permute-start.15
  103.2 7.5 %collective-permute-start.17 = (bf16[3072,128]{1,0:T(8,128)(2,1)S(1)}, bf16[3072,128]{1,0:T(8,128)(2,1)S(1)}, u32[]{:S(2)}, u32[]{:S(2)}) collective-permute-start(bf16[3072,128]{1,0:T(8,128)(2,1)S(1)} %get-tuple-element.107), channel_id=1, source_target_pairs={{0,1},{1,0},{2,3},{3,2},{4,5},{5,4},{6,7},{7,6},{8,9},{9,8},{10,11... | collective-permute-start | bytes 2359304 | tf_op jit(solution)/shard_map/ppermute | solution.py:337
  107.4 3.6 %collective-permute-start.16 = (bf16[3584,128]{1,0:T(8,128)(2,1)S(1)}, bf16[3584,128]{1,0:T(8,128)(2,1)S(1)}, u32[]{:S(2)}, u32[]{:S(2)}) collective-permute-start(bf16[3584,128]{1,0:T(8,128)(2,1)S(1)} %get-tuple-element.105), channel_id=1, source_target_pairs={{0,1},{1,0},{2,3},{3,2},{4,5},{5,4},{6,7},{7,6},{8,9},{9,8},{10,11... | collective-permute-start | bytes 2752520 | tf_op jit(solution)/shard_map/ppermute | solution.py:337
  110.3 2.4 %copy-start.9 = (bf16[16,80,256]{2,1,0:T(8,128)(2,1)}, bf16[16,80,256]{2,1,0:T(8,128)(2,1)S(1)}, u32[]{:S(2)}) copy-start(bf16[16,80,256]{2,1,0:T(8,128)(2,1)S(1)} %get-tuple-element.100.top_ref) | copy-start | bytes 1966084
  110.3 2.4 %collective-permute-start.18 = (bf16[3072,128]{1,0:T(8,128)(2,1)S(1)}, bf16[3072,128]{1,0:T(8,128)(2,1)S(1)}, u32[]{:S(2)}, u32[]{:S(2)}) collective-permute-start(bf16[3072,128]{1,0:T(8,128)(2,1)S(1)} %get-tuple-element.109), channel_id=1, source_target_pairs={{0,1},{1,0},{2,3},{3,2},{4,5},{5,4},{6,7},{7,6},{8,9},{9,8},{10,11... | collective-permute-start | bytes 2359304 | tf_op jit(solution)/shard_map/ppermute | solution.py:337
  114.3 43.5 %all-to-all-start.1 = ((bf16[64,152,128]{2,1,0:T(8,128)(2,1)}), bf16[64,152,128]{2,1,0:T(8,128)(2,1)}, u32[]{:S(2)}, u32[]{:S(2)}) async-start(bf16[64,152,128]{2,1,0:T(8,128)(2,1)} %gather.1), calls=%async_computation.1 | async-start | bytes 4980736 | tf_op jit(solution)/shard_map/all_to_all | solution.py:491
  125.6 1.7 %copy-start.2 = (bf16[64,152,128]{2,1,0:T(8,128)(2,1)S(1)}, bf16[64,152,128]{2,1,0:T(8,128)(2,1)}, u32[]{:S(2)}) copy-start(bf16[64,152,128]{2,1,0:T(8,128)(2,1)} %copy-done.1) | copy-start | bytes 7471108
  127.3 1.3 copy-start.7
  128.6 1.1 copy-start.10
  159.6 3.1 %collective-permute-start.19 = (f32[80,128]{1,0:T(8,128)S(1)}, f32[80,128]{1,0:T(8,128)S(1)}, u32[]{:S(2)}, u32[]{:S(2)}) collective-permute-start(f32[80,128]{1,0:T(8,128)S(1)} %get-tuple-element.111), channel_id=1, source_target_pairs={{0,1},{1,0},{2,3},{3,2},{4,5},{5,4},{6,7},{7,6},{8,9},{9,8},{10,11... | collective-permute-start | bytes 122888 | tf_op jit(solution)/shard_map/ppermute | solution.py:337

commit v6 on v5

--- a/solution.py
+++ b/solution.py
@@ -399,6 +399,7 @@
     )
     n, inner = lax.optimization_barrier((n, inner))
     n, s = call(merge_kernel, "merge", [array(strip), array(strip)], [core_s, n, s, corners], 1e6, 2e6)
+    n, s, cn, cs, outer, inner = lax.optimization_barrier((n, s, cn, cs, outer, inner))
     inner = send(inner, 0, INNER)
     from_s = send(n, -1, SAME)
     from_n = send(s, 1, SAME)
@@ -411,7 +412,7 @@
         "own",
         [array(tile, F32), array(tile, F32)],
         [core_s, features, mine, other, cotangent, proj, conv_bias.reshape(1, 256)],
-        4e9,
+        1e8,
         12e6,
     )
     hidden, g_top, g_low, gi, go, ct, cl = call(

time: 164 us -> 167 us (1.018)
  starting transfers between devices: 42.7 us -> 47.3 us
    ppermute x20, starting transfers between devices: 31.4 us -> 34.8 us  [send(): return lax.ppermute(x, ALL, perm)]
  transfers between devices with their start and end apart: 21 -> 21, of which waited for: 9 -> 9; matrix products, arithmetic and copies ran while one was open for 0% -> 0% of each run, Pallas kernels for 16% -> 15%
where the time goes in v6:
time: 167 us
  starting transfers between devices  47.3 us (28%)
  blocking collectives  44.7 us (27%)
  Pallas kernels  34.3 us (21%)
  waiting for transfers between devices  33.2 us (20%)
  local copies, waits for them, and re-layouts  6.15 us (4%)
    all_to_all x1, blocking collectives, body(): mine = lax.all_to_all(spread, CHIPS, 0, 0)  44.7 us
    ppermute x20, starting transfers between devices, send(): return lax.ppermute(x, ALL, perm)  34.8 us
    pallas_call x20, Pallas kernels, call(): pl.pallas_call(kernel, out_shape=tuple(outs), in_specs=specs, out_specs=(...  34.3 us
    all_to_all x1, waiting for transfers between devices, body(): pieces = lax.all_to_all(total, CHIPS, 0, 0)  18.9 us
    ppermute x20, waiting for transfers between devices, send(): return lax.ppermute(x, ALL, perm)  14.3 us
    all_to_all x1, starting transfers between devices, body(): pieces = lax.all_to_all(total, CHIPS, 0, 0)  12.5 us
    unnamed x22, local copies, waits for them, and re-layouts  5.57 us
  transfers between devices with their start and end apart: 21, of which 9 were waited for; matrix products, arithmetic and copies ran while one was open for 0% of the time, Pallas kernels for 15%

profile of v6, /device:TPU:1, one launch (start us, length us, event | category | flops | bytes accessed | tf_op | source)
XLA Modules:
  0.0 166.7 jit_solution(15425376911457744561)
XLA Ops:
  0.6 0.8 copy-done.4
  1.4 0.7 copy-done.6
  2.1 1.5 collective-permute-start
  3.6 0.8 collective-permute-done.got_ref
  4.4 0.8 spread.1
  5.2 44.7 %all_to_all.10.mine_ref = bf16[64,152,128]{2,1,0:T(8,128)(2,1)S(1)} all-to-all(bf16[64,152,128]{2,1,0:T(8,128)(2,1)S(1)} %spread.1), channel_id=1, replica_groups=mesh['y'=4,'x'=4,'z'=4,'core'=2] {'y','x','z'}, dimensions={0} | all-to-all | bytes 4980736 | tf_op jit(solution)/shard_map/all_to_all | solution.py:373
  49.9 1.9 %collective-permute-start.1 = (bf16[64,152,128]{2,1,0:T(8,128)(2,1)S(1)}, bf16[64,152,128]{2,1,0:T(8,128)(2,1)S(1)}, u32[]{:S(2)}, u32[]{:S(2)}) collective-permute-start(bf16[64,152,128]{2,1,0:T(8,128)(2,1)S(1)} %all_to_all.10.mine_ref), channel_id=1, source_target_pairs={{0,1},{1,0},{2,3},{3,2},{4,5},{5,4},{6,7},{7,6},{8,9},{9,8},{10,11... | collective-permute-start | bytes 7471112 | tf_op jit(solution)/shard_map/ppermute | solution.py:337
  51.9 0.9 flip.1.ft_ref
  52.8 3.4 %collective-permute-done.1.other_ref = bf16[64,152,128]{2,1,0:T(8,128)(2,1)S(1)} collective-permute-done((bf16[64,152,128]{2,1,0:T(8,128)(2,1)S(1)}, bf16[64,152,128]{2,1,0:T(8,128)(2,1)S(1)}, u32[]{:S(2)}, u32[]{:S(2)}) %collective-permute-start.1) | collective-permute-done | bytes 2490400 | tf_op jit(solution)/shard_map/ppermute | solution.py:337
  56.2 2.6 %rows_out.1 = (bf16[16,48,256]{2,1,0:T(8,128)(2,1)S(1)}, bf16[16,48,256]{2,1,0:T(8,128)(2,1)S(1)}, bf16[32,16,256]{2,1,0:T(8,128)(2,1)S(1)}, bf16[16,16,256]{2,1,0:T(8,128)(2,1)S(1)}, bf16[16,16,256]{2,1,0:T(8,128)(2,1)S(1)}) custom-call(s32[1]{0:T(128)} %bitcast.core_ref, bf16[32,48,1024]{2,1,0:T(8,128)(2,1)S(1)} %copy-done, ...), custom_call_target="tpu_custom_call" | custom-call | flops 1700000000 | bytes 9000000 | tf_op jit(solution)/shard_map/rows_out/pallas_call | solution.py:344
  58.9 0.4 collective-permute-start.2
  59.3 1.3 sides_out.1
  60.8 2.2 %collective-permute-start.3 = (bf16[16,48,256]{2,1,0:T(8,128)(2,1)S(1)}, bf16[16,48,256]{2,1,0:T(8,128)(2,1)S(1)}, u32[]{:S(2)}, u32[]{:S(2)}) collective-permute-start(bf16[16,48,256]{2,1,0:T(8,128)(2,1)S(1)} %get-tuple-element.87), channel_id=1, source_target_pairs={{0,8},{1,9},{2,10},{3,11},{4,12},{5,13},{6,14},{7,15},{8,16},{9,17... | collective-permute-start | bytes 1179656 | tf_op jit(solution)/shard_map/ppermute | solution.py:337
  63.0 1.3 collective-permute-start.4
  64.3 5.0 %collective-permute-start.7 = (bf16[16,16,256]{2,1,0:T(8,128)(2,1)S(1)}, bf16[16,16,256]{2,1,0:T(8,128)(2,1)S(1)}, u32[]{:S(2)}, u32[]{:S(2)}) collective-permute-start(bf16[16,16,256]{2,1,0:T(8,128)(2,1)S(1)} %get-tuple-element.91), channel_id=1, source_target_pairs={{1,10},{2,9},{3,12},{4,11},{5,14},{6,13},{9,18},{10,17},{11,20},{1... | collective-permute-start | bytes 393224 | tf_op jit(solution)/shard_map/ppermute | solution.py:337
  69.5 2.3 %collective-permute-start.6 = (bf16[32,16,256]{2,1,0:T(8,128)(2,1)S(1)}, bf16[32,16,256]{2,1,0:T(8,128)(2,1)S(1)}, u32[]{:S(2)}, u32[]{:S(2)}) collective-permute-start(bf16[32,16,256]{2,1,0:T(8,128)(2,1)S(1)} %get-tuple-element.90), channel_id=1, source_target_pairs={{1,2},{2,1},{3,4},{4,3},{5,6},{6,5},{9,10},{10,9},{11,12},{12,11},... | collective-permute-start | bytes 786440 | tf_op jit(solution)/shard_map/ppermute | solution.py:337
  71.8 1.5 collective-permute-done.7.cn_ref
  73.3 1.3 collective-permute-start.8
  74.7 4.3 %own.1 = (f32[32,48,256]{2,1,0:T(8,128)S(1)}, f32[32,48,256]{2,1,0:T(8,128)S(1)}) custom-call(s32[1]{0:T(128)} %bitcast.core_ref, bf16[32,48,1024]{2,1,0:T(8,128)(2,1)S(1)} %copy-done, bf16[64,152,128]{2,1,0:T(8,128)(2,1)S(1)} %all_to_all.10.mine_ref, bf16[64,152,128]{2,1,0:T(8,128)(2,1)S(1)} %collective-permute-done.1.other_ref, ...), custom_call_target="tpu_custom_call" | custom-call | flops 100000000 | bytes 12000000 | tf_op jit(solution)/shard_map/own/pallas_call | solution.py:344
  78.9 3.0 %collective-permute-done.8.cs_ref = bf16[16,16,256]{2,1,0:T(8,128)(2,1)S(1)} collective-permute-done((bf16[16,16,256]{2,1,0:T(8,128)(2,1)S(1)}, bf16[16,16,256]{2,1,0:T(8,128)(2,1)S(1)}, u32[]{:S(2)}, u32[]{:S(2)}) %collective-permute-start.8) | collective-permute-done | bytes 131104 | tf_op jit(solution)/shard_map/ppermute | solution.py:337
  81.9 1.1 point.1
  83.1 1.3 collective-permute-start.12
  84.4 5.7 %collective-permute-start.11 = (bf16[16,48,256]{2,1,0:T(8,128)(2,1)S(1)}, bf16[16,48,256]{2,1,0:T(8,128)(2,1)S(1)}, u32[]{:S(2)}, u32[]{:S(2)}) collective-permute-start(bf16[16,48,256]{2,1,0:T(8,128)(2,1)S(1)} %get-tuple-element.96.gl_ref.low_ref), channel_id=1, source_target_pairs={{0,8},{1,9},{2,10},{3,11},{4,12},{5,13},{6,14},{7,15},{8,16},{9,17... | collective-permute-start | bytes 1179656 | tf_op jit(solution)/shard_map/ppermute | solution.py:337
  90.1 2.2 %collective-permute-start.10 = (bf16[32,16,256]{2,1,0:T(8,128)(2,1)S(1)}, bf16[32,16,256]{2,1,0:T(8,128)(2,1)S(1)}, u32[]{:S(2)}, u32[]{:S(2)}) collective-permute-start(bf16[32,16,256]{2,1,0:T(8,128)(2,1)S(1)} %get-tuple-element.98), channel_id=1, source_target_pairs={{1,2},{2,1},{3,4},{4,3},{5,6},{6,5},{9,10},{10,9},{11,12},{12,11},... | collective-permute-start | bytes 786440 | tf_op jit(solution)/shard_map/ppermute | solution.py:337
  92.3 4.5 %collective-permute-start.13 = (bf16[16,16,256]{2,1,0:T(8,128)(2,1)S(1)}, bf16[16,16,256]{2,1,0:T(8,128)(2,1)S(1)}, u32[]{:S(2)}, u32[]{:S(2)}) collective-permute-start(bf16[16,16,256]{2,1,0:T(8,128)(2,1)S(1)} %get-tuple-element.103), channel_id=1, source_target_pairs={{1,10},{2,9},{3,12},{4,11},{5,14},{6,13},{9,18},{10,17},{11,20},{1... | collective-permute-start | bytes 393224 | tf_op jit(solution)/shard_map/ppermute | solution.py:337
  96.8 1.5 collective-permute-start.14
  98.3 2.7 %wgrad1.1 = (bf16[32,80,256]{2,1,0:T(8,128)(2,1)S(1)}, bf16[3072,128]{1,0:T(8,128)(2,1)S(1)}, bf16[3072,128]{1,0:T(8,128)(2,1)S(1)}) custom-call(s32[1]{0:T(128)} %bitcast.core_ref, bf16[1024,1536]{1,0:T(8,128)(2,1)S(1)} %flip.1.ft_ref, bf16[16,48,256]{2,1,0:T(8,128)(2,1)S(1)} %get-tuple-element.95.gt_ref.top_ref, ...), custom_call_target="tpu_custom_call" | custom-call | flops 100000000 | bytes 6000000 | tf_op jit(solution)/shard_map/wgrad1/pallas_call | solution.py:344
  101.1 1.5 proj.1
  102.5 2.8 %collective-permute-done.14.c_ref = bf16[16,16,256]{2,1,0:T(8,128)(2,1)S(1)} collective-permute-done((bf16[16,16,256]{2,1,0:T(8,128)(2,1)S(1)}, bf16[16,16,256]{2,1,0:T(8,128)(2,1)S(1)}, u32[]{:S(2)}, u32[]{:S(2)}) %collective-permute-start.14) | collective-permute-done | bytes 131104 | tf_op jit(solution)/shard_map/ppermute | solution.py:337
  105.4 0.5 collective-permute-start.17
  105.9 1.0 collective-permute-done.15.edge_ref
  107.0 2.6 %wgrad0.1 = (bf16[16,80,256]{2,1,0:T(8,128)(2,1)S(1)}, bf16[3072,128]{1,0:T(8,128)(2,1)S(1)}, bf16[3584,128]{1,0:T(8,128)(2,1)S(1)}) custom-call(s32[1]{0:T(128)} %bitcast.core_ref, bf16[1024,1536]{1,0:T(8,128)(2,1)S(1)} %flip.1.ft_ref, bf16[32,80,256]{2,1,0:T(8,128)(2,1)S(1)} %get-tuple-element.102.g_ref.mid_ref, ...), custom_call_target="tpu_custom_call" | custom-call | flops 2400000000 | bytes 6000000 | tf_op jit(solution)/shard_map/wgrad0/pallas_call | solution.py:344
  109.8 2.7 %wgrad2.1 = (bf16[16,80,256]{2,1,0:T(8,128)(2,1)S(1)}, bf16[3072,128]{1,0:T(8,128)(2,1)S(1)}, bf16[3072,128]{1,0:T(8,128)(2,1)S(1)}) custom-call(s32[1]{0:T(128)} %bitcast.core_ref, bf16[1024,1536]{1,0:T(8,128)(2,1)S(1)} %flip.1.ft_ref, bf16[32,80,256]{2,1,0:T(8,128)(2,1)S(1)} %get-tuple-element.102.g_ref.mid_ref, ...), custom_call_target="tpu_custom_call" | custom-call | flops 2400000000 | bytes 6000000 | tf_op jit(solution)/shard_map/wgrad2/pallas_call | solution.py:344
  112.5 0.5 collective-permute-start.18
  113.2 0.2 add0.1.t0_ref
  113.5 1.4 collective-permute-done.18.r2_ref
  114.9 1.6 gather.1
  116.5 12.5 %all-to-all-start.1 = ((bf16[64,152,128]{2,1,0:T(8,128)(2,1)}), bf16[64,152,128]{2,1,0:T(8,128)(2,1)}, u32[]{:S(2)}, u32[]{:S(2)}) async-start(bf16[64,152,128]{2,1,0:T(8,128)(2,1)} %gather.1), calls=%async_computation.1 | async-start | bytes 4980736 | tf_op jit(solution)/shard_map/all_to_all | solution.py:492
  129.1 1.7 %copy-done.2 = bf16[64,152,128]{2,1,0:T(8,128)(2,1)S(1)} copy-done((bf16[64,152,128]{2,1,0:T(8,128)(2,1)S(1)}, bf16[64,152,128]{2,1,0:T(8,128)(2,1)}, u32[]{:S(2)}) %copy-start.2) | copy-done | bytes 2490392
  130.8 1.3 copy-done.8
  132.1 1.1 copy-done.10
  133.2 9.2 %fgrad.1 = bf16[32,48,1024]{2,1,0:T(8,128)(2,1)} custom-call(bf16[16,80,256]{2,1,0:T(8,128)(2,1)S(1)} %copy-done.10, bf16[32,80,256]{2,1,0:T(8,128)(2,1)S(1)} %copy-done.8, bf16[16,80,256]{2,1,0:T(8,128)(2,1)S(1)} %get-tuple-element.115.low_ref, bf16[64,152,128]{2,1,0:T(8,128)(2,1)S(1)} %all_to_all.10.mine_ref, bf16[64,152,128]{2,1,0:T(8,128)(2,1)S(1)} %copy-done.2), custom_call_target="tpu_custom_call" | custom-call | flops 7200000000 | bytes 12000000 | tf_op jit(solution)/shard_map/fgrad/pallas_call | solution.py:344
  142.3 18.9 %all-to-all-done.1.far_ref = bf16[64,152,128]{2,1,0:T(8,128)(2,1)} async-done(((bf16[64,152,128]{2,1,0:T(8,128)(2,1)}), bf16[64,152,128]{2,1,0:T(8,128)(2,1)}, u32[]{:S(2)}, u32[]{:S(2)}) %all-to-all-start.1) | async-done | bytes 2490400 | tf_op jit(solution)/shard_map/all_to_all | solution.py:492
  161.2 1.8 %sum.1 = (f32[80,128]{1,0:T(8,128)S(1)}, f32[80,128]{1,0:T(8,128)S(1)}, f32[1,128]{1,0:T(1,128)S(1)}) custom-call(s32[1]{0:T(128)} %bitcast.core_ref, bf16[64,152,128]{2,1,0:T(8,128)(2,1)} %all-to-all-done.1.far_ref), custom_call_target="tpu_custom_call" | custom-call | flops 1000000 | bytes 3000000 | tf_op jit(solution)/shard_map/sum/pallas_call | solution.py:344
  163.0 2.2 %collective-permute-start.19 = (f32[80,128]{1,0:T(8,128)S(1)}, f32[80,128]{1,0:T(8,128)S(1)}, u32[]{:S(2)}, u32[]{:S(2)}) collective-permute-start(f32[80,128]{1,0:T(8,128)S(1)} %get-tuple-element.123), channel_id=1, source_target_pairs={{0,1},{1,0},{2,3},{3,2},{4,5},{5,4},{6,7},{7,6},{8,9},{9,8},{10,11... | collective-permute-start | bytes 122888 | tf_op jit(solution)/shard_map/ppermute | solution.py:337
  165.2 0.6 dynamic-slice_bitcast_fusion
  165.8 0.3 collective-permute-done.19.got_ref
  166.1 0.6 join.1
  (38 shorter events, 1.0 us)
Async XLA Ops:
  0.6 0.8 copy-start.4
  1.4 0.7 copy-start.6
  2.1 2.3 %collective-permute-start = (bf16[80,128]{1,0:T(8,128)(2,1)S(1)}, bf16[80,128]{1,0:T(8,128)(2,1)S(1)}, u32[]{:S(2)}, u32[]{:S(2)}) collective-permute-start(bf16[80,128]{1,0:T(8,128)(2,1)S(1)} %get-tuple-element.67), channel_id=1, source_target_pairs={{0,1},{1,0},{2,3},{3,2},{4,5},{5,4},{6,7},{7,6},{8,9},{9,8},{10,11... | collective-permute-start | bytes 61448 | tf_op jit(solution)/shard_map/ppermute | solution.py:337
  5.2 46.7 %copy-start = (bf16[32,48,1024]{2,1,0:T(8,128)(2,1)S(1)}, bf16[32,48,1024]{2,1,0:T(8,128)(2,1)}, u32[]{:S(2)}) copy-start(bf16[32,48,1024]{2,1,0:T(8,128)(2,1)} %f_ref.3) | copy-start | bytes 9437188
  49.9 6.3 %collective-permute-start.1 = (bf16[64,152,128]{2,1,0:T(8,128)(2,1)S(1)}, bf16[64,152,128]{2,1,0:T(8,128)(2,1)S(1)}, u32[]{:S(2)}, u32[]{:S(2)}) collective-permute-start(bf16[64,152,128]{2,1,0:T(8,128)(2,1)S(1)} %all_to_all.10.mine_ref), channel_id=1, source_target_pairs={{0,1},{1,0},{2,3},{3,2},{4,5},{5,4},{6,7},{7,6},{8,9},{9,8},{10,11... | collective-permute-start | bytes 7471112 | tf_op jit(solution)/shard_map/ppermute | solution.py:337
  56.2 18.4 %copy-start.1 = (bf16[64,152,128]{2,1,0:T(8,128)(2,1)}, bf16[64,152,128]{2,1,0:T(8,128)(2,1)S(1)}, u32[]{:S(2)}) copy-start(bf16[64,152,128]{2,1,0:T(8,128)(2,1)S(1)} %collective-permute-done.1.other_ref) | copy-start | bytes 7471108
  58.9 15.8 %copy-start.3 = (bf16[32,48,256]{2,1,0:T(8,128)(2,1)S(1)}, bf16[32,48,256]{2,1,0:T(8,128)(2,1)}, u32[]{:S(2)}) copy-start(bf16[32,48,256]{2,1,0:T(8,128)(2,1)} %cot_ref.3) | copy-start | bytes 2359300
  58.9 15.8 %copy-start.5 = (f32[256]{0:T(256)S(1)}, f32[256]{0:T(256)}, u32[]{:S(2)}) copy-start(f32[256]{0:T(256)} %param.7) | copy-start | bytes 3076
  58.9 1.8 %collective-permute-start.2 = (bf16[32,16,256]{2,1,0:T(8,128)(2,1)S(1)}, bf16[32,16,256]{2,1,0:T(8,128)(2,1)S(1)}, u32[]{:S(2)}, u32[]{:S(2)}) collective-permute-start(bf16[32,16,256]{2,1,0:T(8,128)(2,1)S(1)} %get-tuple-element.80), channel_id=1, source_target_pairs={{0,1},{1,0},{2,3},{3,2},{4,5},{5,4},{6,7},{7,6},{8,9},{9,8},{10,11... | collective-permute-start | bytes 786440 | tf_op jit(solution)/shard_map/ppermute | solution.py:337
  60.8 21.1 %collective-permute-start.3 = (bf16[16,48,256]{2,1,0:T(8,128)(2,1)S(1)}, bf16[16,48,256]{2,1,0:T(8,128)(2,1)S(1)}, u32[]{:S(2)}, u32[]{:S(2)}) collective-permute-start(bf16[16,48,256]{2,1,0:T(8,128)(2,1)S(1)} %get-tuple-element.87), channel_id=1, source_target_pairs={{0,8},{1,9},{2,10},{3,11},{4,12},{5,13},{6,14},{7,15},{8,16},{9,17... | collective-permute-start | bytes 1179656 | tf_op jit(solution)/shard_map/ppermute | solution.py:337
  63.0 18.9 %collective-permute-start.4 = (bf16[16,48,256]{2,1,0:T(8,128)(2,1)S(1)}, bf16[16,48,256]{2,1,0:T(8,128)(2,1)S(1)}, u32[]{:S(2)}, u32[]{:S(2)}) collective-permute-start(bf16[16,48,256]{2,1,0:T(8,128)(2,1)S(1)} %get-tuple-element.88), channel_id=1, source_target_pairs={{8,0},{9,1},{10,2},{11,3},{12,4},{13,5},{14,6},{15,7},{16,8},{17,9... | collective-permute-start | bytes 1179656 | tf_op jit(solution)/shard_map/ppermute | solution.py:337
  64.3 9.0 %collective-permute-start.7 = (bf16[16,16,256]{2,1,0:T(8,128)(2,1)S(1)}, bf16[16,16,256]{2,1,0:T(8,128)(2,1)S(1)}, u32[]{:S(2)}, u32[]{:S(2)}) collective-permute-start(bf16[16,16,256]{2,1,0:T(8,128)(2,1)S(1)} %get-tuple-element.91), channel_id=1, source_target_pairs={{1,10},{2,9},{3,12},{4,11},{5,14},{6,13},{9,18},{10,17},{11,20},{1... | collective-permute-start | bytes 393224 | tf_op jit(solution)/shard_map/ppermute | solution.py:337
  69.4 12.5 %collective-permute-start.5 = (bf16[32,16,256]{2,1,0:T(8,128)(2,1)S(1)}, bf16[32,16,256]{2,1,0:T(8,128)(2,1)S(1)}, u32[]{:S(2)}, u32[]{:S(2)}) collective-permute-start(bf16[32,16,256]{2,1,0:T(8,128)(2,1)S(1)} %get-tuple-element.89), channel_id=1, source_target_pairs={{0,1},{1,0},{2,3},{3,2},{4,5},{5,4},{6,7},{7,6},{8,9},{9,8},{10,11... | collective-permute-start | bytes 786440 | tf_op jit(solution)/shard_map/ppermute | solution.py:337
  69.5 12.4 %collective-permute-start.6 = (bf16[32,16,256]{2,1,0:T(8,128)(2,1)S(1)}, bf16[32,16,256]{2,1,0:T(8,128)(2,1)S(1)}, u32[]{:S(2)}, u32[]{:S(2)}) collective-permute-start(bf16[32,16,256]{2,1,0:T(8,128)(2,1)S(1)} %get-tuple-element.90), channel_id=1, source_target_pairs={{1,2},{2,1},{3,4},{4,3},{5,6},{6,5},{9,10},{10,9},{11,12},{12,11},... | collective-permute-start | bytes 786440 | tf_op jit(solution)/shard_map/ppermute | solution.py:337
  73.3 8.6 %collective-permute-start.8 = (bf16[16,16,256]{2,1,0:T(8,128)(2,1)S(1)}, bf16[16,16,256]{2,1,0:T(8,128)(2,1)S(1)}, u32[]{:S(2)}, u32[]{:S(2)}) collective-permute-start(bf16[16,16,256]{2,1,0:T(8,128)(2,1)S(1)} %get-tuple-element.92), channel_id=1, source_target_pairs={{9,2},{10,1},{11,4},{12,3},{13,6},{14,5},{17,10},{18,9},{19,12},{2... | collective-permute-start | bytes 393224 | tf_op jit(solution)/shard_map/ppermute | solution.py:337
  83.0 13.8 %collective-permute-start.9 = (bf16[32,16,256]{2,1,0:T(8,128)(2,1)S(1)}, bf16[32,16,256]{2,1,0:T(8,128)(2,1)S(1)}, u32[]{:S(2)}, u32[]{:S(2)}) collective-permute-start(bf16[32,16,256]{2,1,0:T(8,128)(2,1)S(1)} %get-tuple-element.97), channel_id=1, source_target_pairs={{0,1},{1,0},{2,3},{3,2},{4,5},{5,4},{6,7},{7,6},{8,9},{9,8},{10,11... | collective-permute-start | bytes 786440 | tf_op jit(solution)/shard_map/ppermute | solution.py:337
  83.1 22.2 %collective-permute-start.12 = (bf16[16,48,256]{2,1,0:T(8,128)(2,1)S(1)}, bf16[16,48,256]{2,1,0:T(8,128)(2,1)S(1)}, u32[]{:S(2)}, u32[]{:S(2)}) collective-permute-start(bf16[16,48,256]{2,1,0:T(8,128)(2,1)S(1)} %get-tuple-element.95.gt_ref.top_ref), channel_id=1, source_target_pairs={{8,0},{9,1},{10,2},{11,3},{12,4},{13,5},{14,6},{15,7},{16,8},{17,9... | collective-permute-start | bytes 1179656 | tf_op jit(solution)/shard_map/ppermute | solution.py:337
  84.4 20.9 %collective-permute-start.11 = (bf16[16,48,256]{2,1,0:T(8,128)(2,1)S(1)}, bf16[16,48,256]{2,1,0:T(8,128)(2,1)S(1)}, u32[]{:S(2)}, u32[]{:S(2)}) collective-permute-start(bf16[16,48,256]{2,1,0:T(8,128)(2,1)S(1)} %get-tuple-element.96.gl_ref.low_ref), channel_id=1, source_target_pairs={{0,8},{1,9},{2,10},{3,11},{4,12},{5,13},{6,14},{7,15},{8,16},{9,17... | collective-permute-start | bytes 1179656 | tf_op jit(solution)/shard_map/ppermute | solution.py:337
  90.1 8.2 %collective-permute-start.10 = (bf16[32,16,256]{2,1,0:T(8,128)(2,1)S(1)}, bf16[32,16,256]{2,1,0:T(8,128)(2,1)S(1)}, u32[]{:S(2)}, u32[]{:S(2)}) collective-permute-start(bf16[32,16,256]{2,1,0:T(8,128)(2,1)S(1)} %get-tuple-element.98), channel_id=1, source_target_pairs={{1,2},{2,1},{3,4},{4,3},{5,6},{6,5},{9,10},{10,9},{11,12},{12,11},... | collective-permute-start | bytes 786440 | tf_op jit(solution)/shard_map/ppermute | solution.py:337
  92.3 10.3 %collective-permute-start.13 = (bf16[16,16,256]{2,1,0:T(8,128)(2,1)S(1)}, bf16[16,16,256]{2,1,0:T(8,128)(2,1)S(1)}, u32[]{:S(2)}, u32[]{:S(2)}) collective-permute-start(bf16[16,16,256]{2,1,0:T(8,128)(2,1)S(1)} %get-tuple-element.103), channel_id=1, source_target_pairs={{1,10},{2,9},{3,12},{4,11},{5,14},{6,13},{9,18},{10,17},{11,20},{1... | collective-permute-start | bytes 393224 | tf_op jit(solution)/shard_map/ppermute | solution.py:337
  96.8 8.5 %collective-permute-start.14 = (bf16[16,16,256]{2,1,0:T(8,128)(2,1)S(1)}, bf16[16,16,256]{2,1,0:T(8,128)(2,1)S(1)}, u32[]{:S(2)}, u32[]{:S(2)}) collective-permute-start(bf16[16,16,256]{2,1,0:T(8,128)(2,1)S(1)} %get-tuple-element.104), channel_id=1, source_target_pairs={{9,2},{10,1},{11,4},{12,3},{13,6},{14,5},{17,10},{18,9},{19,12},{2... | collective-permute-start | bytes 393224 | tf_op jit(solution)/shard_map/ppermute | solution.py:337
  101.0 8.8 %copy-start.7 = (bf16[32,80,256]{2,1,0:T(8,128)(2,1)}, bf16[32,80,256]{2,1,0:T(8,128)(2,1)S(1)}, u32[]{:S(2)}) copy-start(bf16[32,80,256]{2,1,0:T(8,128)(2,1)S(1)} %get-tuple-element.102.g_ref.mid_ref) | copy-start | bytes 3932164
  105.4 1.6 collective-permute-start.15
  105.4 7.5 %collective-permute-start.17 = (bf16[3072,128]{1,0:T(8,128)(2,1)S(1)}, bf16[3072,128]{1,0:T(8,128)(2,1)S(1)}, u32[]{:S(2)}, u32[]{:S(2)}) collective-permute-start(bf16[3072,128]{1,0:T(8,128)(2,1)S(1)} %get-tuple-element.119), channel_id=1, source_target_pairs={{0,1},{1,0},{2,3},{3,2},{4,5},{5,4},{6,7},{7,6},{8,9},{9,8},{10,11... | collective-permute-start | bytes 2359304 | tf_op jit(solution)/shard_map/ppermute | solution.py:337
  109.6 3.6 %collective-permute-start.16 = (bf16[3584,128]{1,0:T(8,128)(2,1)S(1)}, bf16[3584,128]{1,0:T(8,128)(2,1)S(1)}, u32[]{:S(2)}, u32[]{:S(2)}) collective-permute-start(bf16[3584,128]{1,0:T(8,128)(2,1)S(1)} %get-tuple-element.117), channel_id=1, source_target_pairs={{0,1},{1,0},{2,3},{3,2},{4,5},{5,4},{6,7},{7,6},{8,9},{9,8},{10,11... | collective-permute-start | bytes 2752520 | tf_op jit(solution)/shard_map/ppermute | solution.py:337
  112.5 2.4 %copy-start.9 = (bf16[16,80,256]{2,1,0:T(8,128)(2,1)}, bf16[16,80,256]{2,1,0:T(8,128)(2,1)S(1)}, u32[]{:S(2)}) copy-start(bf16[16,80,256]{2,1,0:T(8,128)(2,1)S(1)} %get-tuple-element.112.top_ref) | copy-start | bytes 1966084
  112.5 2.4 %collective-permute-start.18 = (bf16[3072,128]{1,0:T(8,128)(2,1)S(1)}, bf16[3072,128]{1,0:T(8,128)(2,1)S(1)}, u32[]{:S(2)}, u32[]{:S(2)}) collective-permute-start(bf16[3072,128]{1,0:T(8,128)(2,1)S(1)} %get-tuple-element.121), channel_id=1, source_target_pairs={{0,1},{1,0},{2,3},{3,2},{4,5},{5,4},{6,7},{7,6},{8,9},{9,8},{10,11... | collective-permute-start | bytes 2359304 | tf_op jit(solution)/shard_map/ppermute | solution.py:337
  116.5 44.7 %all-to-all-start.1 = ((bf16[64,152,128]{2,1,0:T(8,128)(2,1)}), bf16[64,152,128]{2,1,0:T(8,128)(2,1)}, u32[]{:S(2)}, u32[]{:S(2)}) async-start(bf16[64,152,128]{2,1,0:T(8,128)(2,1)} %gather.1), calls=%async_computation.1 | async-start | bytes 4980736 | tf_op jit(solution)/shard_map/all_to_all | solution.py:492
  129.1 1.7 %copy-start.2 = (bf16[64,152,128]{2,1,0:T(8,128)(2,1)S(1)}, bf16[64,152,128]{2,1,0:T(8,128)(2,1)}, u32[]{:S(2)}) copy-start(bf16[64,152,128]{2,1,0:T(8,128)(2,1)} %copy-done.1) | copy-start | bytes 7471108
  130.8 1.3 copy-start.8
  132.1 1.1 copy-start.10
  163.0 3.1 %collective-permute-start.19 = (f32[80,128]{1,0:T(8,128)S(1)}, f32[80,128]{1,0:T(8,128)S(1)}, u32[]{:S(2)}, u32[]{:S(2)}) collective-permute-start(f32[80,128]{1,0:T(8,128)S(1)} %get-tuple-element.123), channel_id=1, source_target_pairs={{0,1},{1,0},{2,3},{3,2},{4,5},{5,4},{6,7},{7,6},{8,9},{9,8},{10,11... | collective-permute-start | bytes 122888 | tf_op jit(solution)/shard_map/ppermute | solution.py:337
